TPU v7x, 32 devices: a whole 2x2x4 slice. The times are simulated.
32 devices in a mesh: rec: 2 (over x), row: 4 (over y, core), col: 4 (over z).
Axes of the slice: x: 2, y: 2, z: 4, core: 2. Of those that a mesh axis runs over, the one named last changes fastest.
Arguments:
- local_derivs: bfloat16 [64, 256, 128], P(('rec', 'row', 'col')), may hold values from -6 to 6
- global_derivs: bfloat16 [64, 256, 384], P(('rec', 'row', 'col')), may hold values from -64 to 64
- weights: float32 [64, 256], P(('rec', 'row', 'col')), may hold values from 0.25 to 4
- first_block: int32 [64], P(('rec', 'row', 'col')), may hold values from 0 to 6
- bundle_count: int32 [32], P(('rec', 'row', 'col')), may hold values from 1 to 2
- trailing_block: float32 [2048, 2048], P(('rec', 'row'), 'col'), may hold values from -6 to 6
Outputs:
- updated: float32 [2048, 2048], P(('rec', 'row'), 'col')
All inputs are finite; a program needn't handle non-finite values.
Results may differ from a plain program's by a relative error of at most 0.0094.
Values may be sent and summed in bfloat16 or wider, within the bound.
No kernel may reach another device: no remote copies, remote signals or barrier semaphores. Data moves between devices by JAX's collectives and lax.ppermute only.
A program may use at most 64 MiB of HBM per device.

v0:
```python
import jax
import jax.numpy as jnp
from jax import lax
from jax.sharding import PartitionSpec as P

PBLK = 8


HIGH = lax.Precision.HIGHEST


def shifted(shard, axis, by):
    length = lax.axis_size(axis)
    pairs = [(i, i + by) for i in range(length) if 0 <= i + by < length]
    return lax.ppermute(shard, axis, pairs)


def invert_lower(factor):
    eye = jnp.eye(factor.shape[-1], dtype=factor.dtype)
    eye = jnp.broadcast_to(eye, factor.shape)
    return lax.linalg.triangular_solve(factor, eye, left_side=True, lower=True)


def bundle_terms(local_derivs, global_derivs, weights, first_block, live, panel_blocks):
    block = global_derivs.shape[2] // 3
    root = jnp.sqrt(weights)[:, :, None]
    scaled_local = (root * local_derivs.astype(jnp.float32)).astype(jnp.bfloat16)
    scaled_global = (root * global_derivs.astype(jnp.float32)).astype(jnp.bfloat16)
    local_gram = jnp.einsum(
        "nrl,nrm->nlm", scaled_local, scaled_local, preferred_element_type=jnp.float32
    )
    cross_gram = jnp.einsum(
        "nrg,nrl->ngl", scaled_global, scaled_local, preferred_element_type=jnp.float32
    )
    panel_gram = jnp.einsum(
        "nra,nrg->nag",
        scaled_global[:, :, : 2 * block],
        scaled_global,
        preferred_element_type=jnp.float32,
    )
    local_inverse = invert_lower(jnp.linalg.cholesky(local_gram))
    whitened = jnp.einsum("nlm,ngm->nlg", local_inverse, cross_gram, precision=HIGH)
    reduced = panel_gram - jnp.einsum(
        "nla,nlg->nag", whitened[:, :, : 2 * block], whitened, precision=HIGH
    )
    reduced = reduced * live[:, None, None]
    marks = jnp.arange(panel_blocks, dtype=jnp.int32)
    first_hot = (first_block[:, None] == marks[None, :]).astype(jnp.float32)
    second_hot = (first_block[:, None] + 1 == marks[None, :]).astype(jnp.float32)
    diag_part = jnp.einsum("nk,nab->kab", first_hot, reduced[:, :block, :block], precision=HIGH)
    diag_part = diag_part + jnp.einsum(
        "nk,nab->kab", second_hot, reduced[:, block : 2 * block, block : 2 * block], precision=HIGH
    )
    sub_part = jnp.einsum(
        "nk,nab->kab", second_hot, reduced[:, block : 2 * block, :block], precision=HIGH
    )
    panel_part = jnp.einsum(
        "nk,nab->kab", first_hot, reduced[:, :block, 2 * block :], precision=HIGH
    )
    panel_part = panel_part + jnp.einsum(
        "nk,nab->kab", second_hot, reduced[:, block : 2 * block, 2 * block :], precision=HIGH
    )
    return (
        jnp.stack([diag_part, sub_part], axis=1),
        panel_part.reshape(panel_blocks * block, block),
    )


def step_block(diag, sub, panel_rows, inv_prev, sol_prev):
    low = jnp.dot(sub, inv_prev.T, precision=HIGH)
    inverse = invert_lower(jnp.linalg.cholesky(diag - jnp.dot(low, low.T, precision=HIGH)))
    solved = jnp.dot(inverse, panel_rows - jnp.dot(low, sol_prev, precision=HIGH), precision=HIGH)
    return (inverse, solved)


def run_blocks(blocks, panel, inv_prev, sol_prev):
    block = blocks.shape[2]
    pieces = []
    for index in range(blocks.shape[0]):
        rows = panel[index * block : (index + 1) * block]
        inv_prev, sol_prev = step_block(
            blocks[index, 0], blocks[index, 1], rows, inv_prev, sol_prev
        )
        pieces.append(sol_prev)
    return (inv_prev, sol_prev, jnp.concatenate(pieces, axis=0))


def body(local_derivs, global_derivs, weights, first_block, bundle_count, trailing_block):
    block = global_derivs.shape[2] // 3
    slots = local_derivs.shape[0]
    live = (jnp.arange(slots, dtype=jnp.int32) < bundle_count[0]).astype(jnp.float32)
    stacked, panel_part = bundle_terms(
        local_derivs, global_derivs, weights, first_block, live, PBLK
    )
    n_rec = lax.axis_size("rec")
    n_row = lax.axis_size("row")
    rec_index = lax.axis_index("rec")
    identity = jnp.eye(block, dtype=jnp.float32)
    empty = jnp.zeros((block, block), jnp.float32)
    blocks_mine, panel_mine = (
        lax.psum_scatter(stacked, "rec", scatter_dimension=0, tiled=True),
        lax.psum_scatter(panel_part, "rec", scatter_dimension=0, tiled=True),
    )
    blocks_mine = lax.psum(blocks_mine, ("row", "col"))

    def one_round(turn, carry):
        inv_last, sol_last, _ = run_blocks(blocks_mine, panel_mine, carry[0], carry[1])
        inv_in, sol_in = shifted((inv_last, sol_last), "rec", 1)
        inv_in = jnp.where(rec_index == 0, identity, inv_in)
        return (inv_in, sol_in)

    inv_prev, sol_prev = lax.fori_loop(0, n_rec - 1, one_round, (identity, empty))
    _, _, solved = run_blocks(blocks_mine, panel_mine, inv_prev, sol_prev)
    solved_low = solved.astype(jnp.bfloat16)
    tile_rows = trailing_block.shape[0]
    tile_cols = trailing_block.shape[1]
    whole = lax.all_gather(solved_low, ("row", "col"), axis=1, tiled=True)
    span = whole.shape[0]
    grid = whole.reshape(span, n_rec, n_row, tile_rows)
    row_part = lax.dynamic_slice_in_dim(grid, lax.axis_index("row"), 1, 2).reshape(
        span, n_rec, tile_rows
    )
    col_part = lax.dynamic_slice_in_dim(whole, lax.axis_index("col") * tile_cols, tile_cols, 1)
    copies = jnp.broadcast_to(col_part[:, None, :], (span, n_rec, tile_cols))
    payload = jnp.concatenate([row_part, copies], axis=2)
    mixed = lax.all_to_all(payload, "rec", split_axis=1, concat_axis=0, tiled=True).reshape(
        span * n_rec, tile_rows + tile_cols
    )
    left = mixed[:, :tile_rows]
    right = mixed[:, tile_rows:]
    update = lax.dot_general(
        left, right, (((0,), (0,)), ((), ())), preferred_element_type=jnp.float32
    )
    return trailing_block - update


def solution(mesh):
    return jax.shard_map(
        body,
        mesh=mesh,
        in_specs=(
            P(("rec", "row", "col"), None, None),
            P(("rec", "row", "col"), None, None),
            P(("rec", "row", "col"), None),
            P(("rec", "row", "col")),
            P(("rec", "row", "col")),
            P(("rec", "row"), "col"),
        ),
        out_specs=P(("rec", "row"), "col"),
        check_vma=False,
    )
```

profile of v0, /device:TPU:0, one launch (start us, length us, event | category | flops | bytes accessed | tf_op | source)
XLA Modules:
  0.0 462.6 jit_solution(11671530559094511789)
XLA Ops:
  6.6 0.7 sqrt.3
  7.3 1.2 copy.67
  8.5 1.4 fusion.35
  9.8 1.3 fusion.34
  12.0 23.5 %custom-call.12 = f32[2,128,128]{2,1,0:T(8,128)S(1)} custom-call(f32[2,128,128]{2,1,0:T(8,128)S(1)} %fusion.24), custom_call_target="Cholesky" | custom-call | tf_op jit(solution)/shard_map/jit(cholesky)/cholesky | solution.py:41
  35.7 19.7 %custom-call.13 = f32[2,1,128,128]{2,3,1,0:T(8,128)S(1)} custom-call(f32[2,1,128,128]{3,2,1,0:T(8,128)S(1)} %select_bitcast_fusion), custom_call_target="InvertDiagBlocksLowerTriangular" | custom-call | tf_op jit(solution)/shard_map/triangular_solve | solution.py:21
  55.7 0.4 fusion.22
  56.1 0.6 fusion.95
  56.7 0.9 fusion
  57.7 0.5 fusion.32
  58.4 0.5 fusion.28
  59.2 0.5 fusion.30
  60.0 1.1 pad_maximum_fusion.1
  61.2 23.1 %reduce-scatter.3.cloned.1.call-done = f32[4,2,128,128]{2,3,1,0:T(8,128)} async-done(((f32[8,2,128,128]{2,3,1,0:T(8,128)}), f32[4,2,128,128]{2,3,1,0:T(8,128)}) %reduce-scatter.3.cloned.1.call-update) | async-done | bytes 524304 | tf_op jit(solution)/shard_map/reduce_scatter | solution.py:101
  84.3 0.5 fusion.26
  84.9 0.5 convolution_add_fusion
  85.4 0.9 copy.91
  86.7 91.5 %all-reduce.2.cloned.1.call-done = f32[4,2,128,128]{2,3,1,0:T(8,128)} async-done(((f32[4,2,128,128]{2,3,1,0:T(8,128)}), f32[4,2,128,128]{2,3,1,0:T(8,128)}) %all-reduce.2.cloned.1.call-update) | async-done | bytes 524304 | tf_op jit(solution)/shard_map/psum | solution.py:104
  178.2 1.2 fusion.65
  179.3 1.1 convolution_subtract_fusion.17
  180.6 11.7 %cholesky.192 = f32[128,128]{1,0:T(8,128)S(1)} custom-call(f32[128,128]{1,0:T(8,128)S(1)} %fusion.60), custom_call_target="Cholesky" | custom-call | tf_op jit(solution)/shard_map/while/body/eval_jaxpr/jit(cholesky)/cholesky | solution.py:71
  192.3 0.7 compare_reduce_fusion.7
  193.0 0.6 fusion.36
  193.7 9.8 %custom-call.21 = f32[1,128,128]{1,2,0:T(8,128)S(1)} custom-call(f32[1,128,128]{2,1,0:T(8,128)S(1)} %fusion.36), custom_call_target="InvertDiagBlocksLowerTriangular" | custom-call | tf_op jit(solution)/shard_map/while/body/eval_jaxpr/triangular_solve/custom-call.2 | solution.py:21
  203.8 1.1 convolution_subtract_fusion.12
  205.1 1.1 fusion.77
  206.7 11.7 %cholesky.203 = f32[128,128]{1,0:T(8,128)S(1)} custom-call(f32[128,128]{1,0:T(8,128)S(1)} %fusion.58), custom_call_target="Cholesky" | custom-call | tf_op jit(solution)/shard_map/while/body/eval_jaxpr/jit(cholesky)/cholesky | solution.py:71
  218.4 0.6 compare_reduce_fusion.6
  219.0 0.7 fusion.37
  219.7 9.9 %custom-call.22 = f32[1,128,128]{1,2,0:T(8,128)S(1)} custom-call(f32[1,128,128]{2,1,0:T(8,128)S(1)} %fusion.37), custom_call_target="InvertDiagBlocksLowerTriangular" | custom-call | tf_op jit(solution)/shard_map/while/body/eval_jaxpr/triangular_solve/custom-call.2 | solution.py:21
  230.0 1.0 convolution_subtract_fusion.11
  231.9 11.7 %cholesky.214 = f32[128,128]{1,0:T(8,128)S(1)} custom-call(f32[128,128]{1,0:T(8,128)S(1)} %fusion.56), custom_call_target="Cholesky" | custom-call | tf_op jit(solution)/shard_map/while/body/eval_jaxpr/jit(cholesky)/cholesky | solution.py:71
  243.6 0.6 compare_reduce_fusion.5
  244.3 0.7 fusion.38
  245.0 9.8 %custom-call.23 = f32[1,128,128]{1,2,0:T(8,128)S(1)} custom-call(f32[1,128,128]{2,1,0:T(8,128)S(1)} %fusion.38), custom_call_target="InvertDiagBlocksLowerTriangular" | custom-call | tf_op jit(solution)/shard_map/while/body/eval_jaxpr/triangular_solve/custom-call.2 | solution.py:21
  256.2 12.1 %cholesky.225 = f32[128,128]{1,0:T(8,128)S(1)} custom-call(f32[128,128]{1,0:T(8,128)S(1)} %fusion.54), custom_call_target="Cholesky" | custom-call | tf_op jit(solution)/shard_map/while/body/eval_jaxpr/jit(cholesky)/cholesky | solution.py:71
  268.3 0.6 compare_reduce_fusion.4
  268.9 0.7 fusion.39
  269.6 9.8 %custom-call.24 = f32[1,128,128]{1,2,0:T(8,128)S(1)} custom-call(f32[1,128,128]{2,1,0:T(8,128)S(1)} %fusion.39), custom_call_target="InvertDiagBlocksLowerTriangular" | custom-call | tf_op jit(solution)/shard_map/while/body/eval_jaxpr/triangular_solve/custom-call.2 | solution.py:21
  279.7 3.4 collective-permute-start
  283.5 1.3 collective-permute-start.1
  285.7 11.7 %cholesky.236 = f32[128,128]{1,0:T(8,128)S(1)} custom-call(f32[128,128]{1,0:T(8,128)S(1)} %fusion.52), custom_call_target="Cholesky" | custom-call | tf_op jit(solution)/shard_map/jit(cholesky)/cholesky | solution.py:71
  297.5 0.6 compare_reduce_fusion.3
  298.1 0.7 fusion.40
  298.8 9.8 %custom-call.25 = f32[1,128,128]{1,2,0:T(8,128)S(1)} custom-call(f32[1,128,128]{2,1,0:T(8,128)S(1)} %fusion.40), custom_call_target="InvertDiagBlocksLowerTriangular" | custom-call | tf_op jit(solution)/shard_map/triangular_solve/custom-call.2 | solution.py:21
  310.0 11.7 %cholesky.247 = f32[128,128]{1,0:T(8,128)S(1)} custom-call(f32[128,128]{1,0:T(8,128)S(1)} %fusion.50), custom_call_target="Cholesky" | custom-call | tf_op jit(solution)/shard_map/jit(cholesky)/cholesky | solution.py:71
  321.8 0.6 compare_reduce_fusion.2
  322.4 0.7 fusion.41
  323.1 9.9 %custom-call.26 = f32[1,128,128]{1,2,0:T(8,128)S(1)} custom-call(f32[1,128,128]{2,1,0:T(8,128)S(1)} %fusion.41), custom_call_target="InvertDiagBlocksLowerTriangular" | custom-call | tf_op jit(solution)/shard_map/triangular_solve/custom-call.2 | solution.py:21
  334.4 11.7 %cholesky.258 = f32[128,128]{1,0:T(8,128)S(1)} custom-call(f32[128,128]{1,0:T(8,128)S(1)} %fusion.48), custom_call_target="Cholesky" | custom-call | tf_op jit(solution)/shard_map/jit(cholesky)/cholesky | solution.py:71
  346.2 0.6 compare_reduce_fusion.1
  346.8 0.7 fusion.42
  347.5 9.8 %custom-call.27 = f32[1,128,128]{1,2,0:T(8,128)S(1)} custom-call(f32[1,128,128]{2,1,0:T(8,128)S(1)} %fusion.42), custom_call_target="InvertDiagBlocksLowerTriangular" | custom-call | tf_op jit(solution)/shard_map/triangular_solve/custom-call.2 | solution.py:21
  358.7 11.9 %cholesky.269 = f32[128,128]{1,0:T(8,128)S(1)} custom-call(f32[128,128]{1,0:T(8,128)S(1)} %fusion.46), custom_call_target="Cholesky" | custom-call | tf_op jit(solution)/shard_map/jit(cholesky)/cholesky | solution.py:71
  370.6 0.6 compare_reduce_fusion
  371.2 0.7 fusion.43
  371.9 9.8 %custom-call.28 = f32[1,128,128]{1,2,0:T(8,128)S(1)} custom-call(f32[1,128,128]{2,1,0:T(8,128)S(1)} %fusion.43), custom_call_target="InvertDiagBlocksLowerTriangular" | custom-call | tf_op jit(solution)/shard_map/triangular_solve/custom-call.2 | solution.py:21
  382.4 0.7 pad_maximum_fusion.2
  383.1 43.1 %all-gather.2.cloned.1.call-done = bf16[512,2048]{1,0:T(8,128)(2,1)} async-done(((bf16[512,128]{1,0:T(8,128)(2,1)}), bf16[512,2048]{1,0:T(8,128)(2,1)}) %all-gather.2.cloned.1.call-update) | async-done | bytes 2097168 | tf_op jit(solution)/shard_map/all_gather | solution.py:117
  426.3 3.3 reshape.45
  429.6 1.1 constant_dynamic-slice_fusion.1
  430.8 1.1 constant_dynamic-slice_fusion
  432.1 22.5 %all_to_all.15 = bf16[512,2,768]{2,0,1:T(8,128)(2,1)S(1)} all-to-all(bf16[512,2,768]{2,0,1:T(8,128)(2,1)S(1)} %pad_maximum_fusion), channel_id=1, replica_groups=mesh['rec'=2,'row'=4,'col'=4] {'rec'}, dimensions={1} | all-to-all | bytes 3145728 | tf_op jit(solution)/shard_map/all_to_all | solution.py:126
  454.6 1.3 convolution_subtract_fusion.1
  (98 shorter events, 12.5 us)
Async XLA Ops:
  6.5 5.3 %copy-start.2 = (s32[2]{0:T(128)S(1)}, s32[2]{0:T(128)}, u32[]{:S(2)}) copy-start(s32[2]{0:T(128)} %param.12) | copy-start | bytes 28
  6.5 77.7 %reduce-scatter.3.cloned.1.call-start = ((), (), s32[]{:S(2)}) async-start(), calls=%async_computation.3 | async-start | bytes 1572864 | tf_op jit(solution)/shard_map/reduce_scatter | solution.py:101
  61.1 117.1 %all-reduce.2.cloned.1.call-start = ((), (), s32[]{:S(2)}) async-start(), calls=%async_computation.4 | async-start | bytes 1048576 | tf_op jit(solution)/shard_map/psum | solution.py:104
  84.3 119.5 %reduce-scatter.5.cloned.1.call-start = ((), (), s32[]{:S(2)}) async-start(), calls=%async_computation.5 | async-start | bytes 786432 | tf_op jit(solution)/shard_map/reduce_scatter | solution.py:102
  86.3 339.9 %all-gather.2.cloned.1.call-start = ((), (), s32[]{:S(2)}) async-start(), calls=%async_computation.6 | async-start | bytes 2228224 | tf_op jit(solution)/shard_map/all_gather | solution.py:117
  178.2 28.1 %copy-start = (f32[4,2,128,128]{2,3,1,0:T(8,128)S(1)}, f32[4,2,128,128]{2,3,1,0:T(8,128)}, u32[]{:S(2)}) copy-start(f32[4,2,128,128]{2,3,1,0:T(8,128)} %all-reduce.2.cloned.1.call-done) | copy-start | bytes 1572868
  203.8 51.3 %copy-start.1 = (f32[512,128]{1,0:T(8,128)S(1)}, f32[512,128]{1,0:T(8,128)}, u32[]{:S(2)}) copy-start(f32[512,128]{1,0:T(8,128)} %reduce-scatter.5.cloned.1.call-done) | copy-start | bytes 786436
  279.7 5.3 %collective-permute-start = (f32[128,128]{1,0:T(8,128)S(1)}, f32[128,128]{1,0:T(8,128)S(1)}, u32[]{:S(2)}, u32[]{:S(2)}) collective-permute-start(f32[128,128]{1,0:T(8,128)S(1)} %fusion.14), channel_id=1, source_target_pairs={{0,16},{1,17},{2,18},{3,19},{4,20},{5,21},{6,22},{7,23},{8,24},{9,... | collective-permute-start | bytes 196616 | tf_op jit(solution)/shard_map/while/body/eval_jaxpr/ppermute | solution.py:15
  283.5 25.4 %collective-permute-start.1 = (f32[128,128]{1,0:T(8,128)S(1)}, f32[128,128]{1,0:T(8,128)S(1)}, u32[]{:S(2)}, u32[]{:S(2)}) collective-permute-start(f32[128,128]{1,0:T(8,128)S(1)} %fusion.99), channel_id=1, source_target_pairs={{0,16},{1,17},{2,18},{3,19},{4,20},{5,21},{6,22},{7,23},{8,24},{9,... | collective-permute-start | bytes 196616 | tf_op jit(solution)/shard_map/while/body/eval_jaxpr/ppermute | solution.py:15
  432.1 22.6 %copy-start.3 = (f32[256,512]{1,0:T(8,128)S(1)}, f32[256,512]{1,0:T(8,128)}, u32[]{:S(2)}) copy-start(f32[256,512]{1,0:T(8,128)} %param.14) | copy-start | bytes 1572868
Sparse Core Ops, SparseCore 0:
  61.2 22.9 reduce-scatter.2
  88.1 90.0 all-reduce.1
  180.5 15.1 reduce-scatter.4
  383.3 42.9 all-gather.1
where the time goes:
time: 472 us; the launch traced here: 463 us
  other arithmetic  229 us (49%)
  waiting for transfers between devices  158 us (33%)
  matrix products  22.9 us (5%)
  blocking collectives  22.5 us (5%)
  between operations  14.8 us (3%)
  local copies, waits for them, and re-layouts  9.97 us (2%)
  starting transfers between devices  5.13 us (1%)
    another operation x19, other arithmetic, invert_lower(): return lax.linalg.triangular_solve(factor, eye, left_side=True, lower=True)  104 us
    another operation x25, other arithmetic, step_block(): jnp.linalg.cholesky(diag - jnp.dot(low, low.T, precision=HIGH))  99.7 us
    psum x1, waiting for transfers between devices, body(): blocks_mine = lax.psum(blocks_mine, ('row', 'col'))  91.5 us
    all_gather x1, waiting for transfers between devices, body(): whole = lax.all_gather(solved_low, ('row', 'col'), axis=1, tiled=True)  43.1 us
    another operation x3, other arithmetic, bundle_terms(): local_inverse = invert_lower(jnp.linalg.cholesky(local_gram))  23.6 us
    reduce_scatter x1, waiting for transfers between devices, body(): lax.psum_scatter(stacked, 'rec', scatter_dimension=0, tiled=True)  23.1 us
    all_to_all x1, blocking collectives, body(): lax.all_to_all(payload, 'rec', split_axis=1, concat_axis=0, tiled=True)  22.5 us
  transfers between devices with their start and end apart: 6, of which 4 were waited for; matrix products, arithmetic and copies ran while one was open for 11% of the time, Pallas kernels for 0%

commit v1 on v0

v1 whole, which is shorter than its diff:
```python
import functools

import jax
import jax.numpy as jnp
from jax import lax
from jax.experimental import pallas as pl
from jax.experimental.pallas import tpu as pltpu
from jax.sharding import PartitionSpec as P

PBLK = 8
AXES = ("rec", "row", "col")
F32 = jnp.float32
BF16 = jnp.bfloat16
SUB = 8
VMEM_BYTES = 40 * 1024 * 1024

ROWS_BY_ROWS = (((0,), (0,)), ((), ()))
COLS_BY_COLS = (((1,), (1,)), ((), ()))
PLAIN = (((1,), (0,)), ((), ()))


def split(x):
    if x.dtype == BF16:
        return x, None
    high = x.astype(BF16)
    return high, (x - high.astype(F32)).astype(BF16)


def dot3(a, b, dims):
    a_high, a_low = split(a)
    b_high, b_low = split(b)
    mul = functools.partial(lax.dot_general, dimension_numbers=dims, preferred_element_type=F32)
    out = mul(a_high, b_high)
    if b_low is not None:
        out = out + mul(a_high, b_low)
    if a_low is not None:
        out = out + mul(a_low, b_high)
    return out


def lane_copy(x, at, size):
    return jnp.broadcast_to(x[:, at : at + 1], (SUB, size))


def row_copy(x, at, size):
    return jnp.broadcast_to(x[at : at + 1, :], (SUB, size))


def factor_step(rows, step, lane, sub):
    size = lane.shape[1]
    first = step * SUB
    inside = (lane >= first) & (lane < first + SUB)
    pivot_rows = [row_copy(rows[step], i, size) for i in range(SUB)]
    entry = {
        (i, j): lane_copy(pivot_rows[i], first + j, size) for i in range(SUB) for j in range(i, SUB)
    }
    below = range(step + 1, len(rows))
    cols = {r: [lane_copy(rows[r], first + j, size) for j in range(SUB)] for r in below}
    left = [
        jnp.where(inside, jnp.where(lane == first + i, 1.0, 0.0), pivot_rows[i]) for i in range(SUB)
    ]
    recip = [None] * SUB
    mult = {}
    for k in range(SUB):
        recip[k] = 1.0 / entry[(k, k)]
        for i in range(k + 1, SUB):
            mult[(i, k)] = entry[(k, i)] * recip[k]
        for i in range(k + 1, SUB):
            for j in range(i, SUB):
                entry[(i, j)] = entry[(i, j)] - mult[(i, k)] * entry[(k, j)]
            left[i] = left[i] - mult[(i, k)] * left[k]
    solved = [left[i] * recip[i] for i in range(SUB)]
    done = left[0] * lax.sqrt(recip[0])
    for i in range(1, SUB):
        done = jnp.where(sub == i, left[i] * lax.sqrt(recip[i]), done)
    for k in range(SUB - 1, 0, -1):
        for i in range(k):
            solved[i] = solved[i] - mult[(k, i)] * solved[k]
    for r in below:
        part = [cols[r][j] * solved[j] for j in range(SUB)]
        while len(part) > 1:
            part = [part[i] + part[i + 1] for i in range(0, len(part), 2)]
        rows[r] = jnp.where(inside, 0.0, rows[r]) - part[0]
    rows[step] = jnp.where(lane < first + SUB, done, 0.0)


def inverse_factors(mats):
    size = mats[0].shape[0]
    lane = lax.broadcasted_iota(jnp.int32, (SUB, size), 1)
    sub = lax.broadcasted_iota(jnp.int32, (SUB, size), 0)
    state = [[m[r : r + SUB, :] for r in range(0, size, SUB)] for m in mats]
    for step in range(size // SUB):
        for rows in state:
            factor_step(rows, step, lane, sub)
    return [jnp.concatenate(rows, axis=0) for rows in state]


def local_kernel(
    me, pan, first_ref, count_ref, local_ref, global_ref, weight_ref,
    keep_ref, send_ref, pkeep_ref, psend_ref, tri, panel,
):
    slots = local_ref.shape[0]
    block = local_ref.shape[2]
    tri[...] = jnp.zeros_like(tri)
    panel[...] = jnp.zeros_like(panel)
    root = jnp.sqrt(weight_ref[...])
    root = jnp.transpose(jnp.concatenate([root] * (SUB // slots), axis=0))
    grams, crosses, panels = [], [], []
    for b in range(slots):
        col = root[:, b : b + 1]
        loc = (col * local_ref[b].astype(F32)).astype(BF16)
        glo = (col * global_ref[b].astype(F32)).astype(BF16)
        dot = functools.partial(
            lax.dot_general, dimension_numbers=ROWS_BY_ROWS, preferred_element_type=F32
        )
        grams.append(dot(loc, loc))
        crosses.append(dot(loc, glo))
        panels.append(dot(glo[:, : 2 * block], glo))
    inverses = inverse_factors(grams)
    for b in range(slots):
        white = dot3(inverses[b], crosses[b], PLAIN)
        reduced = panels[b] - dot3(white[:, : 2 * block], white, ROWS_BY_ROWS)
        live = jnp.where(count_ref[0] > b, 1.0, 0.0)
        reduced = reduced * live
        k = first_ref[b]
        one = lax.bitwise_xor(k, me)
        two = lax.bitwise_xor(k + 1, me)
        tri[one, 0] += reduced[:block, :block]
        tri[two, 0] += reduced[block:, block : 2 * block]
        tri[two, 1] += reduced[block:, :block]
        panel[lax.bitwise_xor(k, pan)] += reduced[:block, 2 * block :]
        panel[lax.bitwise_xor(k + 1, pan)] += reduced[block:, 2 * block :]
    half = PBLK // 2
    for j in range(half):
        keep_ref[j] = tri[2 * j]
        send_ref[j] = tri[2 * j + 1]
    pkeep_ref[...] = panel[:half]
    psend_ref[...] = panel[half:].astype(BF16)


def add_kernel(a_ref, b_ref, *out_refs):
    for j, ref in enumerate(out_refs):
        ref[...] = a_ref[j] + b_ref[j]


def levels_of(count):
    left = list(range(count))
    levels = []
    while left:
        gone = left[0::2] if len(left) > 1 else left
        level = []
        for k in gone:
            at = left.index(k)
            before = left[at - 1] if at > 0 else None
            after = left[at + 1] if at + 1 < len(left) else None
            level.append((k, before, after))
        levels.append(level)
        left = [k for k in left if k not in gone]
    return levels


def couplings_of(count):
    return [
        (k, n, side)
        for level in levels_of(count)
        for k, before, after in level
        for n, side in ((before, "before"), (after, "after"))
        if n is not None
    ]


def chain_kernel(me, *refs):
    pieces = refs[:PBLK]
    inv_ref, low_ref, tri = refs[PBLK:]
    for j in range(PBLK):
        tri[lax.bitwise_xor(me, j)] = pieces[j][...]
    diag = {k: tri[k, 0] for k in range(PBLK)}
    off = {(k, k - 1): tri[k, 1] for k in range(1, PBLK)}
    slot = {key[:2]: i for i, key in enumerate(couplings_of(PBLK))}
    for level in levels_of(PBLK):
        inverses = inverse_factors([diag[k] for k, _, _ in level])
        for (k, before, after), inv in zip(level, inverses):
            inv_ref[k] = inv
            if before is not None:
                low_b = dot3(inv, off[(k, before)], PLAIN)
                low_ref[slot[(k, before)]] = low_b
                diag[before] = diag[before] - dot3(low_b, low_b, ROWS_BY_ROWS)
            if after is not None:
                low_a = dot3(off[(after, k)], inv, COLS_BY_COLS)
                low_ref[slot[(k, after)]] = low_a
                diag[after] = diag[after] - dot3(low_a, low_a, COLS_BY_COLS)
            if before is not None and after is not None:
                off[(after, before)] = -dot3(low_a, low_b, PLAIN)


def final_kernel(col_me, n_rec, inv_ref, low_ref, pc_ref, *refs):
    n_col = len(refs) - 4
    rows_refs = refs[:n_col]
    trail_ref, out_ref, panel, solved = refs[n_col:]
    height, block = rows_refs[0].shape
    tile_rows = trail_ref.shape[0]
    n_row = pc_ref.shape[0] // n_rec
    for r in range(n_rec):
        for i in range(n_row):
            at = tile_rows + i * block
            panel[r * height : (r + 1) * height, at : at + block] = pc_ref[r * n_row + i]
    for m in range(n_col):
        q = lax.bitwise_xor(col_me, m)
        down = pl.multiple_of(lax.rem(q, n_rec) * height, height)
        over = pl.multiple_of(lax.div(q, n_rec) * block, block)
        panel[pl.ds(down, height), pl.ds(over, block)] = rows_refs[m][...]
    slot = {key[:2]: i for i, key in enumerate(couplings_of(PBLK))}
    value = {k: panel[k * block : (k + 1) * block, :] for k in range(PBLK)}
    for level in levels_of(PBLK):
        for k, before, after in level:
            sol = dot3(inv_ref[k], value[k], PLAIN)
            solved[k * block : (k + 1) * block, :] = sol.astype(BF16)
            if before is not None:
                low_b = low_ref[slot[(k, before)]]
                value[before] = value[before].astype(F32) - dot3(low_b, sol, ROWS_BY_ROWS)
            if after is not None:
                low_a = low_ref[slot[(k, after)]]
                value[after] = value[after].astype(F32) - dot3(low_a, sol, PLAIN)
    update = lax.dot_general(
        solved[:, :tile_rows], solved[:, tile_rows:], ROWS_BY_ROWS, preferred_element_type=F32
    )
    out_ref[...] = trail_ref[...] - update


VMEM = pl.BlockSpec(memory_space=pltpu.VMEM)
SMEM = pl.BlockSpec(memory_space=pltpu.SMEM)
PARAMS = pltpu.CompilerParams(vmem_limit_bytes=VMEM_BYTES)


def call(kernel, out_shape, ins, scratch=(), scalars=0):
    return pl.pallas_call(
        kernel,
        out_shape=out_shape,
        in_specs=[SMEM] * scalars + [VMEM] * (len(ins) - scalars),
        out_specs=jax.tree.map(lambda _: VMEM, out_shape),
        scratch_shapes=scratch,
        compiler_params=PARAMS,
    )(*ins)


def flipped(x, mask, count):
    return lax.ppermute(x, AXES, [(i, i ^ mask) for i in range(count)])


def body(local_derivs, global_derivs, weights, first_block, bundle_count, trailing_block):
    n_rec, n_row, n_col = (lax.axis_size(a) for a in AXES)
    count = n_rec * n_row * n_col
    rec, row, col = (lax.axis_index(a) for a in AXES)
    block = local_derivs.shape[2]
    half = PBLK // 2
    low_rec = PBLK // n_row
    me = row + n_row * lax.rem(rec, low_rec)
    pan = rec * half if n_rec == 2 else jnp.int32(0)
    ids = jnp.stack([me, pan, col]).astype(jnp.int32)
    shape = jax.ShapeDtypeStruct

    def local_body(ids_ref, *refs):
        local_kernel(ids_ref[0], ids_ref[1], *refs)

    keep, send, pkeep, psend = call(
        local_body,
        [
            shape((half, 2, block, block), F32),
            shape((half, 2, block, block), F32),
            shape((half, block, block), F32),
            shape((half, block, block), BF16),
        ],
        [ids, first_block, bundle_count, local_derivs, global_derivs, weights],
        [pltpu.VMEM((PBLK, 2, block, block), F32), pltpu.VMEM((PBLK, block, block), F32)],
        scalars=3,
    )
    got = flipped(send, n_col, count)
    if n_rec == 2:
        pgot = flipped(psend, n_row * n_col, count)
        height = half * block
        pmine = (pkeep + pgot.astype(F32)).astype(BF16).reshape(height, block)
    else:
        whole = jnp.concatenate([pkeep, psend.astype(F32)], axis=0).reshape(PBLK * block, block)
        pmine = lax.psum_scatter(whole, "rec", scatter_dimension=0, tiled=True).astype(BF16)
        height = pmine.shape[0]
    pieces = call(add_kernel, [shape((2, block, block), F32)] * half, [keep, got])
    total = pieces[0]
    for j in range(1, half):
        total = total + flipped(pieces[j], 2 * j * n_col, count)
    for bit in range(1, n_rec // low_rec):
        if bit & (bit - 1) == 0:
            total = total + flipped(total, bit * low_rec * n_row * n_col, count)
    if n_col <= 4:
        total = sum((flipped(total, m, count) for m in range(1, n_col)), total)
    else:
        total = lax.psum(total, "col")
    evens = [total] + [flipped(total, 2 * j * n_col, count) for j in range(1, half)]
    odds = [flipped(x, n_col, count) for x in evens]
    tri = [x for pair in zip(evens, odds) for x in pair]

    owner = lambda r, c: (r * n_row + c // n_col) * n_col + c % n_col
    device = lambda r, i, j: (r * n_row + i) * n_col + j
    grid = [(r, i, j) for r in range(n_rec) for i in range(n_row) for j in range(n_col)]
    to_cols = [(owner(r, n_row * j + i), device(r, i, j)) for r, i, j in grid]
    per = n_col // n_rec
    to_rows = [
        (owner(j % n_rec, (r * n_row + i) * per + j // n_rec), device(r, i, j)) for r, i, j in grid
    ]
    pcols = lax.all_gather(lax.ppermute(pmine, AXES, to_cols), ("rec", "row"), axis=0)
    prows = lax.ppermute(pmine, AXES, to_rows)
    if n_col <= 4:
        prows = [prows] + [flipped(prows, m, count) for m in range(1, n_col)]
        col_key = col
    else:
        every = lax.all_gather(prows, "col", axis=0)
        prows = [every[m] for m in range(n_col)]
        col_key = jnp.int32(0)

    inverses, lows = call(
        lambda ids_ref, *refs: chain_kernel(ids_ref[0], *refs),
        [
            shape((PBLK, block, block), F32),
            shape((len(couplings_of(PBLK)), block, block), F32),
        ],
        [ids, *tri],
        [pltpu.VMEM((PBLK, 2, block, block), F32)],
        scalars=1,
    )
    wide = trailing_block.shape[0] + trailing_block.shape[1]
    key = jnp.reshape(col_key, (1,)).astype(jnp.int32)
    return call(
        lambda key_ref, *refs: final_kernel(key_ref[0], n_rec, *refs),
        shape(trailing_block.shape, F32),
        [key, inverses, lows, pcols, *prows, trailing_block],
        [pltpu.VMEM((PBLK * block, wide), BF16), pltpu.VMEM((PBLK * block, wide), BF16)],
        scalars=1,
    )


def solution(mesh):
    return jax.shard_map(
        body,
        mesh=mesh,
        in_specs=(
            P(("rec", "row", "col"), None, None),
            P(("rec", "row", "col"), None, None),
            P(("rec", "row", "col"), None),
            P(("rec", "row", "col")),
            P(("rec", "row", "col")),
            P(("rec", "row"), "col"),
        ),
        out_specs=P(("rec", "row"), "col"),
        check_vma=False,
    )
```

time: 472 us -> 124 us (0.26); the launches traced: 463 us -> 124 us
  other arithmetic: 229 us -> 0.18 us
  waiting for transfers between devices: 158 us -> 21.7 us
  Pallas kernels: 0 us -> 42.4 us
  starting transfers between devices: 5.13 us -> 41.3 us
  matrix products: 22.9 us -> 0 us
  blocking collectives: 22.5 us -> 0 us
  local copies, waits for them, and re-layouts: 9.97 us -> 4.37 us
    another operation x49 -> x1, other arithmetic: 228 us -> 0.08 us  [body(): ids = jnp.stack([me, pan, col]).astype(jnp.int32)]
    psum x1 -> x0, waiting for transfers between devices: 91.5 us -> none  [body(): blocks_mine = lax.psum(blocks_mine, ('row', 'col'))]
    all_gather x1, waiting for transfers between devices: 43.1 us -> 0.02 us  [body(): lax.all_gather(lax.ppermute(pmine, AXES, to_cols), ('rec', 'row'), axis=0)]
    pallas_call x0 -> x4, Pallas kernels: none -> 42.4 us  [call(): pl.pallas_call(kernel, out_shape=out_shape, in_specs=[SMEM] * scalars + [...]
    ppermute x2 -> x20, starting transfers between devices: 4.66 us -> 41.3 us  [the longest x18 39.8 us: flipped(): return lax.ppermute(x, AXES, [(i, i ^ mask) for i in range(count)])]
    reduce_scatter x2 -> x0, waiting for transfers between devices: 23.1 us -> none  [the longest x1 23.1 us: body(): lax.psum_scatter(stacked, 'rec', scatter_dimension=0, tiled=True)]
    all_to_all x1 -> x0, blocking collectives: 22.5 us -> none  [body(): lax.all_to_all(payload, 'rec', split_axis=1, concat_axis=0, tiled=True)]
    ppermute x2 -> x20, waiting for transfers between devices: 0.24 us -> 21.7 us  [the longest x18 21.7 us: flipped(): return lax.ppermute(x, AXES, [(i, i ^ mask) for i in range(count)])]
  transfers between devices with their start and end apart: 6 -> 21, of which waited for: 4 -> 8; matrix products, arithmetic and copies ran while one was open for 11% -> 0% of each run, Pallas kernels for 0% -> 23%
where the time goes in v1:
time: 124 us
  Pallas kernels  42.4 us (34%)
  starting transfers between devices  41.3 us (33%)
  waiting for transfers between devices  21.7 us (18%)
  between operations  14.2 us (11%)
  local copies, waits for them, and re-layouts  4.37 us (4%)
    pallas_call x4, Pallas kernels, call(): pl.pallas_call(kernel, out_shape=out_shape, in_specs=[SMEM] * scalars + [...  42.4 us
    ppermute x18, starting transfers between devices, flipped(): return lax.ppermute(x, AXES, [(i, i ^ mask) for i in range(count)])  39.8 us
    ppermute x18, waiting for transfers between devices, flipped(): return lax.ppermute(x, AXES, [(i, i ^ mask) for i in range(count)])  21.7 us
    unnamed x14, local copies, waits for them, and re-layouts  4.37 us
  transfers between devices with their start and end apart: 21, of which 8 were waited for; matrix products, arithmetic and copies ran while one was open for 0% of the time, Pallas kernels for 23%

profile of v1, /device:TPU:0, one launch (start us, length us, event | category | flops | bytes accessed | tf_op | source)
XLA Modules:
  0.0 124.2 jit_solution(4630878753367786848)
XLA Ops:
  6.5 0.0 all-gather.3.cloned.1.call-start
  7.2 0.0 copy-start.4
  7.2 0.0 copy-start.5
  7.2 0.1 pad_add_fusion.ids_ref
  7.3 0.6 copy-done.4
  7.9 0.0 copy-done.5
  7.9 0.0 copy-start.2
  7.9 1.0 copy-done.2
  8.9 0.0 copy-start.3
  8.9 0.9 copy-done.3
  9.8 8.9 %shard_map.64 = (f32[4,2,128,128]{3,2,1,0:T(8,128)S(1)}, f32[4,2,128,128]{3,2,1,0:T(8,128)S(1)}, f32[4,128,128]{2,1,0:T(8,128)S(1)}, bf16[4,128,128]{2,1,0:T(8,128)(2,1)S(1)}) custom-call(s32[3]{0:T(128)S(1)} %pad_add_fusion.ids_ref, s32[2]{0:T(128)S(1)} %copy-done.5, s32[1]{0:T(128)S(6)} %copy.7.refs_1_, bf16[2,256,128]{2,1,0:T(8,128)(2,1)S(1)} %copy-done.3, ...), custom_call_target="tpu_custom_call" | custom-call | tf_op jit(solution)/shard_map/pallas_call | solution.py:236
  18.7 3.0 %collective-permute-start.14 = (bf16[4,128,128]{2,1,0:T(8,128)(2,1)S(1)}, bf16[4,128,128]{2,1,0:T(8,128)(2,1)S(1)}, u32[]{:S(2)}, u32[]{:S(2)}) collective-permute-start(bf16[4,128,128]{2,1,0:T(8,128)(2,1)S(1)} %get-tuple-element.24), channel_id=1, source_target_pairs={{0,16},{1,17},{2,18},{3,19},{4,20},{5,21},{6,22},{7,23},{8,24},{9,... | collective-permute-start | bytes 393224 | tf_op jit(solution)/shard_map/ppermute | solution.py:247
  21.7 3.5 %collective-permute-done.14 = bf16[4,128,128]{2,1,0:T(8,128)(2,1)S(1)} collective-permute-done((bf16[4,128,128]{2,1,0:T(8,128)(2,1)S(1)}, bf16[4,128,128]{2,1,0:T(8,128)(2,1)S(1)}, u32[]{:S(2)}, u32[]{:S(2)}) %collective-permute-start.14) | collective-permute-done | bytes 131104 | tf_op jit(solution)/shard_map/ppermute | solution.py:247
  25.3 0.7 collective-permute-start.15
  25.9 0.0 collective-permute-done.15
  26.0 0.0 copy-start.6
  26.0 0.6 copy-done.6
  26.6 0.0 all-gather.3.cloned.1.call-update
  26.6 5.9 %collective-permute-start = (f32[4,2,128,128]{3,2,1,0:T(8,128)S(1)}, f32[4,2,128,128]{3,2,1,0:T(8,128)S(1)}, u32[]{:S(2)}, u32[]{:S(2)}) collective-permute-start(f32[4,2,128,128]{3,2,1,0:T(8,128)S(1)} %get-tuple-element.16), channel_id=1, source_target_pairs={{0,4},{1,5},{2,6},{3,7},{4,0},{5,1},{6,2},{7,3},{8,12},{9,13},{10,... | collective-permute-start | bytes 1572872 | tf_op jit(solution)/shard_map/ppermute | solution.py:247
  32.5 1.5 %collective-permute-done.b_ref = f32[4,2,128,128]{3,2,1,0:T(8,128)S(1)} collective-permute-done((f32[4,2,128,128]{3,2,1,0:T(8,128)S(1)}, f32[4,2,128,128]{3,2,1,0:T(8,128)S(1)}, u32[]{:S(2)}, u32[]{:S(2)}) %collective-permute-start) | collective-permute-done | bytes 524320 | tf_op jit(solution)/shard_map/ppermute | solution.py:247
  34.0 0.1 shard_map.65
  34.1 7.6 %collective-permute-start.1 = (f32[2,128,128]{2,1,0:T(8,128)S(1)}, f32[2,128,128]{2,1,0:T(8,128)S(1)}, u32[]{:S(2)}, u32[]{:S(2)}) collective-permute-start(f32[2,128,128]{2,1,0:T(8,128)S(1)} %get-tuple-element.18), channel_id=1, source_target_pairs={{0,8},{1,9},{2,10},{3,11},{4,12},{5,13},{6,14},{7,15},{8,0},{9,1},... | collective-permute-start | bytes 393224 | tf_op jit(solution)/shard_map/ppermute | solution.py:247
  41.7 1.5 %collective-permute-start.2 = (f32[2,128,128]{2,1,0:T(8,128)S(1)}, f32[2,128,128]{2,1,0:T(8,128)S(1)}, u32[]{:S(2)}, u32[]{:S(2)}) collective-permute-start(f32[2,128,128]{2,1,0:T(8,128)S(1)} %get-tuple-element.19), channel_id=1, source_target_pairs={{0,16},{1,17},{2,18},{3,19},{4,20},{5,21},{6,22},{7,23},{8,24},{9,... | collective-permute-start | bytes 393224 | tf_op jit(solution)/shard_map/ppermute | solution.py:247
  43.2 0.0 collective-permute-start.3
  43.2 2.3 %collective-permute-done.1 = f32[2,128,128]{2,1,0:T(8,128)S(1)} collective-permute-done((f32[2,128,128]{2,1,0:T(8,128)S(1)}, f32[2,128,128]{2,1,0:T(8,128)S(1)}, u32[]{:S(2)}, u32[]{:S(2)}) %collective-permute-start.1) | collective-permute-done | bytes 131104 | tf_op jit(solution)/shard_map/ppermute | solution.py:247
  45.5 3.9 %collective-permute-done.2 = f32[2,128,128]{2,1,0:T(8,128)S(1)} collective-permute-done((f32[2,128,128]{2,1,0:T(8,128)S(1)}, f32[2,128,128]{2,1,0:T(8,128)S(1)}, u32[]{:S(2)}, u32[]{:S(2)}) %collective-permute-start.2) | collective-permute-done | bytes 131104 | tf_op jit(solution)/shard_map/ppermute | solution.py:247
  49.4 1.6 %collective-permute-done.3 = f32[2,128,128]{2,1,0:T(8,128)S(1)} collective-permute-done((f32[2,128,128]{2,1,0:T(8,128)S(1)}, f32[2,128,128]{2,1,0:T(8,128)S(1)}, u32[]{:S(2)}, u32[]{:S(2)}) %collective-permute-start.3) | collective-permute-done | bytes 131104 | tf_op jit(solution)/shard_map/ppermute | solution.py:247
  51.0 0.6 collective-permute-start.4
  51.6 1.7 %collective-permute-start.5 = (f32[2,128,128]{2,1,0:T(8,128)S(1)}, f32[2,128,128]{2,1,0:T(8,128)S(1)}, u32[]{:S(2)}, u32[]{:S(2)}) collective-permute-start(f32[2,128,128]{2,1,0:T(8,128)S(1)} %add_add_fusion.1), channel_id=1, source_target_pairs={{0,2},{1,3},{2,0},{3,1},{4,6},{5,7},{6,4},{7,5},{8,10},{9,11},{10,... | collective-permute-start | bytes 393224 | tf_op jit(solution)/shard_map/ppermute | solution.py:247
  53.3 2.2 %collective-permute-start.6 = (f32[2,128,128]{2,1,0:T(8,128)S(1)}, f32[2,128,128]{2,1,0:T(8,128)S(1)}, u32[]{:S(2)}, u32[]{:S(2)}) collective-permute-start(f32[2,128,128]{2,1,0:T(8,128)S(1)} %add_add_fusion.1), channel_id=1, source_target_pairs={{0,3},{1,2},{2,1},{3,0},{4,7},{5,6},{6,5},{7,4},{8,11},{9,10},{10,... | collective-permute-start | bytes 393224 | tf_op jit(solution)/shard_map/ppermute | solution.py:247
  55.4 1.5 %collective-permute-done.4 = f32[2,128,128]{2,1,0:T(8,128)S(1)} collective-permute-done((f32[2,128,128]{2,1,0:T(8,128)S(1)}, f32[2,128,128]{2,1,0:T(8,128)S(1)}, u32[]{:S(2)}, u32[]{:S(2)}) %collective-permute-start.4) | collective-permute-done | bytes 131104 | tf_op jit(solution)/shard_map/ppermute | solution.py:247
  56.9 6.5 %collective-permute-done.5 = f32[2,128,128]{2,1,0:T(8,128)S(1)} collective-permute-done((f32[2,128,128]{2,1,0:T(8,128)S(1)}, f32[2,128,128]{2,1,0:T(8,128)S(1)}, u32[]{:S(2)}, u32[]{:S(2)}) %collective-permute-start.5) | collective-permute-done | bytes 131104 | tf_op jit(solution)/shard_map/ppermute | solution.py:247
  63.4 0.0 collective-permute-done.6
  63.4 0.0 copy-start.1
  63.4 2.0 %collective-permute-start.10 = (f32[2,128,128]{2,1,0:T(8,128)S(1)}, f32[2,128,128]{2,1,0:T(8,128)S(1)}, u32[]{:S(2)}, u32[]{:S(2)}) collective-permute-start(f32[2,128,128]{2,1,0:T(8,128)S(1)} %add_add_fusion.refs_0_), channel_id=1, source_target_pairs={{0,16},{1,17},{2,18},{3,19},{4,20},{5,21},{6,22},{7,23},{8,24},{9,... | collective-permute-start | bytes 393224 | tf_op jit(solution)/shard_map/ppermute | solution.py:247
  65.4 0.8 collective-permute-start.16
  66.3 4.3 %collective-permute-start.12 = (f32[2,128,128]{2,1,0:T(8,128)S(1)}, f32[2,128,128]{2,1,0:T(8,128)S(1)}, u32[]{:S(2)}, u32[]{:S(2)}) collective-permute-start(f32[2,128,128]{2,1,0:T(8,128)S(1)} %add_add_fusion.refs_0_), channel_id=1, source_target_pairs={{0,24},{1,25},{2,26},{3,27},{4,28},{5,29},{6,30},{7,31},{8,16},{9,... | collective-permute-start | bytes 393224 | tf_op jit(solution)/shard_map/ppermute | solution.py:247
  70.5 1.9 %collective-permute-start.8 = (f32[2,128,128]{2,1,0:T(8,128)S(1)}, f32[2,128,128]{2,1,0:T(8,128)S(1)}, u32[]{:S(2)}, u32[]{:S(2)}) collective-permute-start(f32[2,128,128]{2,1,0:T(8,128)S(1)} %add_add_fusion.refs_0_), channel_id=1, source_target_pairs={{0,8},{1,9},{2,10},{3,11},{4,12},{5,13},{6,14},{7,15},{8,0},{9,1},... | collective-permute-start | bytes 393224 | tf_op jit(solution)/shard_map/ppermute | solution.py:247
  72.5 0.5 collective-permute-start.7
  73.0 0.0 collective-permute-done.10.refs_4_
  73.0 0.0 collective-permute-start.11
  73.0 0.0 collective-permute-done.16.refs_3_
  73.0 3.7 %collective-permute-start.17 = (bf16[512,128]{1,0:T(8,128)(2,1)S(1)}, bf16[512,128]{1,0:T(8,128)(2,1)S(1)}, u32[]{:S(2)}, u32[]{:S(2)}) collective-permute-start(bf16[512,128]{1,0:T(8,128)(2,1)S(1)} %collective-permute-done.16.refs_3_), channel_id=1, source_target_pairs={{0,1},{1,0},{2,3},{3,2},{4,5},{5,4},{6,7},{7,6},{8,9},{9,8},{10,11... | collective-permute-start | bytes 393224 | tf_op jit(solution)/shard_map/ppermute | solution.py:247
  76.7 0.0 collective-permute-done.12.refs_6_
  76.7 0.0 collective-permute-start.13
  76.7 1.0 collective-permute-done.8.refs_2_
  77.7 0.1 collective-permute-start.9
  77.8 0.0 collective-permute-done.7.refs_1_
  77.8 1.3 %collective-permute-start.18 = (bf16[512,128]{1,0:T(8,128)(2,1)S(1)}, bf16[512,128]{1,0:T(8,128)(2,1)S(1)}, u32[]{:S(2)}, u32[]{:S(2)}) collective-permute-start(bf16[512,128]{1,0:T(8,128)(2,1)S(1)} %collective-permute-done.16.refs_3_), channel_id=1, source_target_pairs={{0,2},{1,3},{2,0},{3,1},{4,6},{5,7},{6,4},{7,5},{8,10},{9,11},{10,... | collective-permute-start | bytes 393224 | tf_op jit(solution)/shard_map/ppermute | solution.py:247
  79.1 0.0 collective-permute-done.11.refs_5_
  79.1 3.5 %collective-permute-start.19 = (bf16[512,128]{1,0:T(8,128)(2,1)S(1)}, bf16[512,128]{1,0:T(8,128)(2,1)S(1)}, u32[]{:S(2)}, u32[]{:S(2)}) collective-permute-start(bf16[512,128]{1,0:T(8,128)(2,1)S(1)} %collective-permute-done.16.refs_3_), channel_id=1, source_target_pairs={{0,3},{1,2},{2,1},{3,0},{4,7},{5,6},{6,5},{7,4},{8,11},{9,10},{10,... | collective-permute-start | bytes 393224 | tf_op jit(solution)/shard_map/ppermute | solution.py:247
  82.6 0.0 collective-permute-done.13.refs_7_
  82.6 0.0 collective-permute-done.9.refs_3_
  82.6 28.1 %shard_map.66 = (f32[8,128,128]{2,1,0:T(8,128)S(1)}, f32[11,128,128]{2,1,0:T(8,128)S(1)}) custom-call(s32[3]{0:T(128)S(1)} %pad_add_fusion.ids_ref, f32[2,128,128]{2,1,0:T(8,128)S(1)} %add_add_fusion.refs_0_, f32[2,128,128]{2,1,0:T(8,128)S(1)} %collective-permute-done.7.refs_1_, f32[2,128,128]{2,1,0:T(8,128)S(1)} %collective-permute-done.8.refs_2_, ...), custom_call_target="tpu_custom_call" | custom-call | tf_op jit(solution)/shard_map/pallas_call | solution.py:236
  110.7 0.0 collective-permute-done.17.refs_4_
  110.7 0.0 collective-permute-done.18.refs_5_
  110.7 0.0 collective-permute-done.19.refs_6_
  110.7 0.0 all-gather.3.cloned.1.call-done
  110.8 0.0 copy-done.1
  110.8 0.0 copy-start
  110.8 1.2 copy-done
  112.0 5.4 %shard_map.67 = f32[256,512]{1,0:T(8,128)} custom-call(s32[1]{0:T(128)} %bitcast.key_ref, f32[8,128,128]{2,1,0:T(8,128)S(1)} %get-tuple-element.21.refs_0_, f32[11,128,128]{2,1,0:T(8,128)S(1)} %get-tuple-element.22.refs_1_, bf16[8,512,128]{2,1,0:T(8,128)(2,1)S(1)} %bitcast.5, bf16[512,128]{1,0:T(8,128)(2,1)S(1)} %collective-permute-done.16.refs_3_, ...), custom_call_target="tpu_custom_call" | custom-call | tf_op jit(solution)/shard_map/pallas_call | solution.py:236
  (3 shorter events, 0.1 us)
Async XLA Ops:
  6.5 104.2 %all-gather.3.cloned.1.call-start = ((), (), s32[]{:S(2)}) async-start(), calls=%async_computation | async-start | bytes 1179648 | tf_op jit(solution)/shard_map/all_gather | solution.py:309
  7.2 0.7 copy-start.4
  7.2 0.7 copy-start.5
  7.9 1.0 copy-start.2
  8.9 0.9 copy-start.3
  18.7 6.5 %collective-permute-start.14 = (bf16[4,128,128]{2,1,0:T(8,128)(2,1)S(1)}, bf16[4,128,128]{2,1,0:T(8,128)(2,1)S(1)}, u32[]{:S(2)}, u32[]{:S(2)}) collective-permute-start(bf16[4,128,128]{2,1,0:T(8,128)(2,1)S(1)} %get-tuple-element.24), channel_id=1, source_target_pairs={{0,16},{1,17},{2,18},{3,19},{4,20},{5,21},{6,22},{7,23},{8,24},{9,... | collective-permute-start | bytes 393224 | tf_op jit(solution)/shard_map/ppermute | solution.py:247
  25.3 0.7 collective-permute-start.15
  26.0 0.7 copy-start.6
  26.6 7.4 %collective-permute-start = (f32[4,2,128,128]{3,2,1,0:T(8,128)S(1)}, f32[4,2,128,128]{3,2,1,0:T(8,128)S(1)}, u32[]{:S(2)}, u32[]{:S(2)}) collective-permute-start(f32[4,2,128,128]{3,2,1,0:T(8,128)S(1)} %get-tuple-element.16), channel_id=1, source_target_pairs={{0,4},{1,5},{2,6},{3,7},{4,0},{5,1},{6,2},{7,3},{8,12},{9,13},{10,... | collective-permute-start | bytes 1572872 | tf_op jit(solution)/shard_map/ppermute | solution.py:247
  34.1 11.4 %collective-permute-start.1 = (f32[2,128,128]{2,1,0:T(8,128)S(1)}, f32[2,128,128]{2,1,0:T(8,128)S(1)}, u32[]{:S(2)}, u32[]{:S(2)}) collective-permute-start(f32[2,128,128]{2,1,0:T(8,128)S(1)} %get-tuple-element.18), channel_id=1, source_target_pairs={{0,8},{1,9},{2,10},{3,11},{4,12},{5,13},{6,14},{7,15},{8,0},{9,1},... | collective-permute-start | bytes 393224 | tf_op jit(solution)/shard_map/ppermute | solution.py:247
  41.7 7.7 %collective-permute-start.2 = (f32[2,128,128]{2,1,0:T(8,128)S(1)}, f32[2,128,128]{2,1,0:T(8,128)S(1)}, u32[]{:S(2)}, u32[]{:S(2)}) collective-permute-start(f32[2,128,128]{2,1,0:T(8,128)S(1)} %get-tuple-element.19), channel_id=1, source_target_pairs={{0,16},{1,17},{2,18},{3,19},{4,20},{5,21},{6,22},{7,23},{8,24},{9,... | collective-permute-start | bytes 393224 | tf_op jit(solution)/shard_map/ppermute | solution.py:247
  43.2 7.8 %collective-permute-start.3 = (f32[2,128,128]{2,1,0:T(8,128)S(1)}, f32[2,128,128]{2,1,0:T(8,128)S(1)}, u32[]{:S(2)}, u32[]{:S(2)}) collective-permute-start(f32[2,128,128]{2,1,0:T(8,128)S(1)} %get-tuple-element.20), channel_id=1, source_target_pairs={{0,24},{1,25},{2,26},{3,27},{4,28},{5,29},{6,30},{7,31},{8,16},{9,... | collective-permute-start | bytes 393224 | tf_op jit(solution)/shard_map/ppermute | solution.py:247
  51.0 5.9 %collective-permute-start.4 = (f32[2,128,128]{2,1,0:T(8,128)S(1)}, f32[2,128,128]{2,1,0:T(8,128)S(1)}, u32[]{:S(2)}, u32[]{:S(2)}) collective-permute-start(f32[2,128,128]{2,1,0:T(8,128)S(1)} %add_add_fusion.1), channel_id=1, source_target_pairs={{0,1},{1,0},{2,3},{3,2},{4,5},{5,4},{6,7},{7,6},{8,9},{9,8},{10,11... | collective-permute-start | bytes 393224 | tf_op jit(solution)/shard_map/ppermute | solution.py:247
  51.6 11.8 %collective-permute-start.5 = (f32[2,128,128]{2,1,0:T(8,128)S(1)}, f32[2,128,128]{2,1,0:T(8,128)S(1)}, u32[]{:S(2)}, u32[]{:S(2)}) collective-permute-start(f32[2,128,128]{2,1,0:T(8,128)S(1)} %add_add_fusion.1), channel_id=1, source_target_pairs={{0,2},{1,3},{2,0},{3,1},{4,6},{5,7},{6,4},{7,5},{8,10},{9,11},{10,... | collective-permute-start | bytes 393224 | tf_op jit(solution)/shard_map/ppermute | solution.py:247
  53.3 10.1 %collective-permute-start.6 = (f32[2,128,128]{2,1,0:T(8,128)S(1)}, f32[2,128,128]{2,1,0:T(8,128)S(1)}, u32[]{:S(2)}, u32[]{:S(2)}) collective-permute-start(f32[2,128,128]{2,1,0:T(8,128)S(1)} %add_add_fusion.1), channel_id=1, source_target_pairs={{0,3},{1,2},{2,1},{3,0},{4,7},{5,6},{6,5},{7,4},{8,11},{9,10},{10,... | collective-permute-start | bytes 393224 | tf_op jit(solution)/shard_map/ppermute | solution.py:247
  63.4 47.3 %copy-start.1 = (f32[256,512]{1,0:T(8,128)S(1)}, f32[256,512]{1,0:T(8,128)}, u32[]{:S(2)}) copy-start(f32[256,512]{1,0:T(8,128)} %refs_7_.1) | copy-start | bytes 1572868
  63.4 9.5 %collective-permute-start.10 = (f32[2,128,128]{2,1,0:T(8,128)S(1)}, f32[2,128,128]{2,1,0:T(8,128)S(1)}, u32[]{:S(2)}, u32[]{:S(2)}) collective-permute-start(f32[2,128,128]{2,1,0:T(8,128)S(1)} %add_add_fusion.refs_0_), channel_id=1, source_target_pairs={{0,16},{1,17},{2,18},{3,19},{4,20},{5,21},{6,22},{7,23},{8,24},{9,... | collective-permute-start | bytes 393224 | tf_op jit(solution)/shard_map/ppermute | solution.py:247
  65.4 7.6 %collective-permute-start.16 = (bf16[512,128]{1,0:T(8,128)(2,1)S(1)}, bf16[512,128]{1,0:T(8,128)(2,1)S(1)}, u32[]{:S(2)}, u32[]{:S(2)}) collective-permute-start(bf16[512,128]{1,0:T(8,128)(2,1)S(1)} %bitcast.7), channel_id=1, source_target_pairs={{0,0},{16,1},{1,2},{17,3},{2,4},{18,5},{3,6},{19,7},{4,8},{20,9},{... | collective-permute-start | bytes 393224 | tf_op jit(solution)/shard_map/ppermute | solution.py:310
  66.3 10.4 %collective-permute-start.12 = (f32[2,128,128]{2,1,0:T(8,128)S(1)}, f32[2,128,128]{2,1,0:T(8,128)S(1)}, u32[]{:S(2)}, u32[]{:S(2)}) collective-permute-start(f32[2,128,128]{2,1,0:T(8,128)S(1)} %add_add_fusion.refs_0_), channel_id=1, source_target_pairs={{0,24},{1,25},{2,26},{3,27},{4,28},{5,29},{6,30},{7,31},{8,16},{9,... | collective-permute-start | bytes 393224 | tf_op jit(solution)/shard_map/ppermute | solution.py:247
  70.5 7.2 %collective-permute-start.8 = (f32[2,128,128]{2,1,0:T(8,128)S(1)}, f32[2,128,128]{2,1,0:T(8,128)S(1)}, u32[]{:S(2)}, u32[]{:S(2)}) collective-permute-start(f32[2,128,128]{2,1,0:T(8,128)S(1)} %add_add_fusion.refs_0_), channel_id=1, source_target_pairs={{0,8},{1,9},{2,10},{3,11},{4,12},{5,13},{6,14},{7,15},{8,0},{9,1},... | collective-permute-start | bytes 393224 | tf_op jit(solution)/shard_map/ppermute | solution.py:247
  72.5 5.3 %collective-permute-start.7 = (f32[2,128,128]{2,1,0:T(8,128)S(1)}, f32[2,128,128]{2,1,0:T(8,128)S(1)}, u32[]{:S(2)}, u32[]{:S(2)}) collective-permute-start(f32[2,128,128]{2,1,0:T(8,128)S(1)} %add_add_fusion.refs_0_), channel_id=1, source_target_pairs={{0,4},{1,5},{2,6},{3,7},{4,0},{5,1},{6,2},{7,3},{8,12},{9,13},{10,... | collective-permute-start | bytes 393224 | tf_op jit(solution)/shard_map/ppermute | solution.py:247
  73.0 6.2 %collective-permute-start.11 = (f32[2,128,128]{2,1,0:T(8,128)S(1)}, f32[2,128,128]{2,1,0:T(8,128)S(1)}, u32[]{:S(2)}, u32[]{:S(2)}) collective-permute-start(f32[2,128,128]{2,1,0:T(8,128)S(1)} %collective-permute-done.10.refs_4_), channel_id=1, source_target_pairs={{0,4},{1,5},{2,6},{3,7},{4,0},{5,1},{6,2},{7,3},{8,12},{9,13},{10,... | collective-permute-start | bytes 393224 | tf_op jit(solution)/shard_map/ppermute | solution.py:247
  73.0 37.7 %collective-permute-start.17 = (bf16[512,128]{1,0:T(8,128)(2,1)S(1)}, bf16[512,128]{1,0:T(8,128)(2,1)S(1)}, u32[]{:S(2)}, u32[]{:S(2)}) collective-permute-start(bf16[512,128]{1,0:T(8,128)(2,1)S(1)} %collective-permute-done.16.refs_3_), channel_id=1, source_target_pairs={{0,1},{1,0},{2,3},{3,2},{4,5},{5,4},{6,7},{7,6},{8,9},{9,8},{10,11... | collective-permute-start | bytes 393224 | tf_op jit(solution)/shard_map/ppermute | solution.py:247
  76.7 5.9 %collective-permute-start.13 = (f32[2,128,128]{2,1,0:T(8,128)S(1)}, f32[2,128,128]{2,1,0:T(8,128)S(1)}, u32[]{:S(2)}, u32[]{:S(2)}) collective-permute-start(f32[2,128,128]{2,1,0:T(8,128)S(1)} %collective-permute-done.12.refs_6_), channel_id=1, source_target_pairs={{0,4},{1,5},{2,6},{3,7},{4,0},{5,1},{6,2},{7,3},{8,12},{9,13},{10,... | collective-permute-start | bytes 393224 | tf_op jit(solution)/shard_map/ppermute | solution.py:247
  77.7 4.9 %collective-permute-start.9 = (f32[2,128,128]{2,1,0:T(8,128)S(1)}, f32[2,128,128]{2,1,0:T(8,128)S(1)}, u32[]{:S(2)}, u32[]{:S(2)}) collective-permute-start(f32[2,128,128]{2,1,0:T(8,128)S(1)} %collective-permute-done.8.refs_2_), channel_id=1, source_target_pairs={{0,4},{1,5},{2,6},{3,7},{4,0},{5,1},{6,2},{7,3},{8,12},{9,13},{10,... | collective-permute-start | bytes 393224 | tf_op jit(solution)/shard_map/ppermute | solution.py:247
  77.8 32.9 %collective-permute-start.18 = (bf16[512,128]{1,0:T(8,128)(2,1)S(1)}, bf16[512,128]{1,0:T(8,128)(2,1)S(1)}, u32[]{:S(2)}, u32[]{:S(2)}) collective-permute-start(bf16[512,128]{1,0:T(8,128)(2,1)S(1)} %collective-permute-done.16.refs_3_), channel_id=1, source_target_pairs={{0,2},{1,3},{2,0},{3,1},{4,6},{5,7},{6,4},{7,5},{8,10},{9,11},{10,... | collective-permute-start | bytes 393224 | tf_op jit(solution)/shard_map/ppermute | solution.py:247
  79.1 31.6 %collective-permute-start.19 = (bf16[512,128]{1,0:T(8,128)(2,1)S(1)}, bf16[512,128]{1,0:T(8,128)(2,1)S(1)}, u32[]{:S(2)}, u32[]{:S(2)}) collective-permute-start(bf16[512,128]{1,0:T(8,128)(2,1)S(1)} %collective-permute-done.16.refs_3_), channel_id=1, source_target_pairs={{0,3},{1,2},{2,1},{3,0},{4,7},{5,6},{6,5},{7,4},{8,11},{9,10},{10,... | collective-permute-start | bytes 393224 | tf_op jit(solution)/shard_map/ppermute | solution.py:247
  110.8 1.2 copy-start
Sparse Core Ops, SparseCore 0:
  26.8 34.3 all-gather.2

commit v2 on v1

--- a/solution.py
+++ b/solution.py
@@ -12,6 +12,7 @@
 F32 = jnp.float32
 BF16 = jnp.bfloat16
 SUB = 8
+TAIL = 16
 VMEM_BYTES = 40 * 1024 * 1024
 
 ROWS_BY_ROWS = (((0,), (0,)), ((), ()))
@@ -96,25 +97,35 @@
 
 
 def local_kernel(
-    me, pan, first_ref, count_ref, local_ref, global_ref, weight_ref,
-    keep_ref, send_ref, pkeep_ref, psend_ref, tri, panel,
+    me, first_ref, count_ref, local_hbm, global_hbm, weight_hbm,
+    keep_ref, send_ref, piece_ref, tri, local_ref, global_ref, weight_ref, sems,
 ):
+    copies = [
+        pltpu.make_async_copy(src, dst, sems.at[i])
+        for i, (src, dst) in enumerate(
+            [(weight_hbm, weight_ref), (local_hbm, local_ref), (global_hbm, global_ref)]
+        )
+    ]
+    for copy in copies:
+        copy.start()
     slots = local_ref.shape[0]
     block = local_ref.shape[2]
     tri[...] = jnp.zeros_like(tri)
-    panel[...] = jnp.zeros_like(panel)
+    dot = functools.partial(
+        lax.dot_general, dimension_numbers=ROWS_BY_ROWS, preferred_element_type=F32
+    )
+    copies[0].wait()
     root = jnp.sqrt(weight_ref[...])
     root = jnp.transpose(jnp.concatenate([root] * (SUB // slots), axis=0))
-    grams, crosses, panels = [], [], []
+    copies[1].wait()
+    cols = [root[:, b : b + 1] for b in range(slots)]
+    locs = [(cols[b] * local_ref[b].astype(F32)).astype(BF16) for b in range(slots)]
+    grams = [dot(loc, loc) for loc in locs]
+    copies[2].wait()
+    crosses, panels = [], []
     for b in range(slots):
-        col = root[:, b : b + 1]
-        loc = (col * local_ref[b].astype(F32)).astype(BF16)
-        glo = (col * global_ref[b].astype(F32)).astype(BF16)
-        dot = functools.partial(
-            lax.dot_general, dimension_numbers=ROWS_BY_ROWS, preferred_element_type=F32
-        )
-        grams.append(dot(loc, loc))
-        crosses.append(dot(loc, glo))
+        glo = (cols[b] * global_ref[b].astype(F32)).astype(BF16)
+        crosses.append(dot(locs[b], glo))
         panels.append(dot(glo[:, : 2 * block], glo))
     inverses = inverse_factors(grams)
     for b in range(slots):
@@ -128,14 +139,13 @@
         tri[one, 0] += reduced[:block, :block]
         tri[two, 0] += reduced[block:, block : 2 * block]
         tri[two, 1] += reduced[block:, :block]
-        panel[lax.bitwise_xor(k, pan)] += reduced[:block, 2 * block :]
-        panel[lax.bitwise_xor(k + 1, pan)] += reduced[block:, 2 * block :]
+        piece_ref[b, : 2 * block, :] = reduced[:, 2 * block :].astype(BF16)
+        tail = jnp.broadcast_to(k.astype(F32), (TAIL, block))
+        piece_ref[b, 2 * block :, :] = tail.astype(BF16)
     half = PBLK // 2
     for j in range(half):
         keep_ref[j] = tri[2 * j]
         send_ref[j] = tri[2 * j + 1]
-    pkeep_ref[...] = panel[:half]
-    psend_ref[...] = panel[half:].astype(BF16)
 
 
 def add_kernel(a_ref, b_ref, *out_refs):
@@ -193,22 +203,22 @@
                 off[(after, before)] = -dot3(low_a, low_b, PLAIN)
 
 
-def final_kernel(col_me, n_rec, inv_ref, low_ref, pc_ref, *refs):
-    n_col = len(refs) - 4
-    rows_refs = refs[:n_col]
-    trail_ref, out_ref, panel, solved = refs[n_col:]
-    height, block = rows_refs[0].shape
+def final_kernel(cols_me, rows_me, n_row, per, n_cols, inv_ref, low_ref, *refs):
+    terms, (trail_ref, out_ref, panel, solved) = refs[:-4], refs[-4:]
+    slots, height, block = terms[0].shape
+    height = height - TAIL
     tile_rows = trail_ref.shape[0]
-    n_row = pc_ref.shape[0] // n_rec
-    for r in range(n_rec):
-        for i in range(n_row):
-            at = tile_rows + i * block
-            panel[r * height : (r + 1) * height, at : at + block] = pc_ref[r * n_row + i]
-    for m in range(n_col):
-        q = lax.bitwise_xor(col_me, m)
-        down = pl.multiple_of(lax.rem(q, n_rec) * height, height)
-        over = pl.multiple_of(lax.div(q, n_rec) * block, block)
-        panel[pl.ds(down, height), pl.ds(over, block)] = rows_refs[m][...]
+    panel[...] = jnp.zeros_like(panel)
+    for n, term in enumerate(terms):
+        if n < n_cols:
+            over = tile_rows + lax.rem(lax.bitwise_xor(cols_me, n), n_row) * block
+        else:
+            over = lax.rem(lax.bitwise_xor(rows_me, n - n_cols), per) * block
+        over = pl.multiple_of(over, block)
+        for b in range(slots):
+            k = jnp.max(term[b, height:, :].astype(F32)).astype(jnp.int32)
+            down = pl.multiple_of(k * block, block)
+            panel[pl.ds(down, height), pl.ds(over, block)] += term[b, :height, :].astype(F32)
     slot = {key[:2]: i for i, key in enumerate(couplings_of(PBLK))}
     value = {k: panel[k * block : (k + 1) * block, :] for k in range(PBLK)}
     for level in levels_of(PBLK):
@@ -217,10 +227,10 @@
             solved[k * block : (k + 1) * block, :] = sol.astype(BF16)
             if before is not None:
                 low_b = low_ref[slot[(k, before)]]
-                value[before] = value[before].astype(F32) - dot3(low_b, sol, ROWS_BY_ROWS)
+                value[before] = value[before] - dot3(low_b, sol, ROWS_BY_ROWS)
             if after is not None:
                 low_a = low_ref[slot[(k, after)]]
-                value[after] = value[after].astype(F32) - dot3(low_a, sol, PLAIN)
+                value[after] = value[after] - dot3(low_a, sol, PLAIN)
     update = lax.dot_general(
         solved[:, :tile_rows], solved[:, tile_rows:], ROWS_BY_ROWS, preferred_element_type=F32
     )
@@ -229,18 +239,23 @@
 
 VMEM = pl.BlockSpec(memory_space=pltpu.VMEM)
 SMEM = pl.BlockSpec(memory_space=pltpu.SMEM)
+HBM = pl.BlockSpec(memory_space=pltpu.HBM)
 PARAMS = pltpu.CompilerParams(vmem_limit_bytes=VMEM_BYTES)
 
 
-def call(kernel, out_shape, ins, scratch=(), scalars=0):
+def call(kernel, out_shape, ins, scratch=(), scalars=0, hbm=()):
     return pl.pallas_call(
         kernel,
         out_shape=out_shape,
-        in_specs=[SMEM] * scalars + [VMEM] * (len(ins) - scalars),
+        in_specs=[SMEM if i < scalars else HBM if i in hbm else VMEM for i in range(len(ins))],
         out_specs=jax.tree.map(lambda _: VMEM, out_shape),
         scratch_shapes=scratch,
         compiler_params=PARAMS,
     )(*ins)
+
+
+def after(x, *others):
+    return lax.optimization_barrier((x, others))[0]
 
 
 def flipped(x, mask, count):
@@ -255,66 +270,66 @@
     half = PBLK // 2
     low_rec = PBLK // n_row
     me = row + n_row * lax.rem(rec, low_rec)
-    pan = rec * half if n_rec == 2 else jnp.int32(0)
-    ids = jnp.stack([me, pan, col]).astype(jnp.int32)
+    ids = jnp.reshape(me, (1,)).astype(jnp.int32)
     shape = jax.ShapeDtypeStruct
-
-    def local_body(ids_ref, *refs):
-        local_kernel(ids_ref[0], ids_ref[1], *refs)
-
-    keep, send, pkeep, psend = call(
-        local_body,
+    slots, height = local_derivs.shape[0], 2 * block + TAIL
+    keep, send, piece = call(
+        lambda ids_ref, *refs: local_kernel(ids_ref[0], *refs),
         [
             shape((half, 2, block, block), F32),
             shape((half, 2, block, block), F32),
-            shape((half, block, block), F32),
-            shape((half, block, block), BF16),
+            shape((slots, height, block), BF16),
         ],
         [ids, first_block, bundle_count, local_derivs, global_derivs, weights],
-        [pltpu.VMEM((PBLK, 2, block, block), F32), pltpu.VMEM((PBLK, block, block), F32)],
+        [
+            pltpu.VMEM((PBLK, 2, block, block), F32),
+            pltpu.VMEM(local_derivs.shape, BF16),
+            pltpu.VMEM(global_derivs.shape, BF16),
+            pltpu.VMEM(weights.shape, F32),
+            pltpu.SemaphoreType.DMA((3,)),
+        ],
         scalars=3,
-    )
-    got = flipped(send, n_col, count)
-    if n_rec == 2:
-        pgot = flipped(psend, n_row * n_col, count)
-        height = half * block
-        pmine = (pkeep + pgot.astype(F32)).astype(BF16).reshape(height, block)
-    else:
-        whole = jnp.concatenate([pkeep, psend.astype(F32)], axis=0).reshape(PBLK * block, block)
-        pmine = lax.psum_scatter(whole, "rec", scatter_dimension=0, tiled=True).astype(BF16)
-        height = pmine.shape[0]
-    pieces = call(add_kernel, [shape((2, block, block), F32)] * half, [keep, got])
-    total = pieces[0]
-    for j in range(1, half):
-        total = total + flipped(pieces[j], 2 * j * n_col, count)
-    for bit in range(1, n_rec // low_rec):
-        if bit & (bit - 1) == 0:
-            total = total + flipped(total, bit * low_rec * n_row * n_col, count)
-    if n_col <= 4:
-        total = sum((flipped(total, m, count) for m in range(1, n_col)), total)
-    else:
-        total = lax.psum(total, "col")
-    evens = [total] + [flipped(total, 2 * j * n_col, count) for j in range(1, half)]
-    odds = [flipped(x, n_col, count) for x in evens]
-    tri = [x for pair in zip(evens, odds) for x in pair]
-
+        hbm=(3, 4, 5),
+    )
+    per = n_col // n_rec
     owner = lambda r, c: (r * n_row + c // n_col) * n_col + c % n_col
     device = lambda r, i, j: (r * n_row + i) * n_col + j
     grid = [(r, i, j) for r in range(n_rec) for i in range(n_row) for j in range(n_col)]
     to_cols = [(owner(r, n_row * j + i), device(r, i, j)) for r, i, j in grid]
-    per = n_col // n_rec
     to_rows = [
-        (owner(j % n_rec, (r * n_row + i) * per + j // n_rec), device(r, i, j)) for r, i, j in grid
+        (owner((j // per) ^ r ^ (i % 2), (r * n_row + i) * per + j % per), device(r, i, j))
+        for r, i, j in grid
     ]
-    pcols = lax.all_gather(lax.ppermute(pmine, AXES, to_cols), ("rec", "row"), axis=0)
-    prows = lax.ppermute(pmine, AXES, to_rows)
-    if n_col <= 4:
+    direct = n_col <= 4 and n_rec == low_rec
+    got = flipped(send, n_col, count)
+    piece = after(piece, got)
+    pcols = lax.ppermute(piece, AXES, to_cols)
+    prows = lax.ppermute(piece, AXES, to_rows)
+    pieces = call(add_kernel, [shape((2, block, block), F32)] * half, [keep, got])
+    total = sum([flipped(pieces[j], 2 * j * n_col, count) for j in range(1, half)], pieces[0])
+    for bit in range(1, n_rec // low_rec):
+        if bit & (bit - 1) == 0:
+            total = total + flipped(total, bit * low_rec * n_row * n_col, count)
+    if direct:
+        parts = [flipped(total, m, count) for m in range(1, n_col)]
+        pcols = after(pcols, parts[0])
+        pcols = [pcols] + [flipped(pcols, 2 * j * n_col, count) for j in range(1, half)]
+        total = sum(parts, total)
+    else:
+        total = lax.psum(total, "col")
+    evens = [total] + [flipped(total, 2 * j * n_col, count) for j in range(1, half)]
+    if direct:
+        prows = after(prows, evens[1])
         prows = [prows] + [flipped(prows, m, count) for m in range(1, n_col)]
-        col_key = col
+        others = [flipped(x, n_col, count) for x in pcols]
+        pcols = [x for pair in zip(pcols, others) for x in pair]
+        cols_me, rows_me = me, col
     else:
-        every = lax.all_gather(prows, "col", axis=0)
-        prows = [every[m] for m in range(n_col)]
-        col_key = jnp.int32(0)
+        pcols = list(lax.all_gather(pcols, ("rec", "row"), axis=0))
+        prows = list(lax.all_gather(prows, "col", axis=0))
+        cols_me = rows_me = jnp.int32(0)
+    odds = [flipped(x, n_col, count) for x in evens]
+    tri = [x for pair in zip(evens, odds) for x in pair]
 
     inverses, lows = call(
         lambda ids_ref, *refs: chain_kernel(ids_ref[0], *refs),
@@ -327,12 +342,16 @@
         scalars=1,
     )
     wide = trailing_block.shape[0] + trailing_block.shape[1]
-    key = jnp.reshape(col_key, (1,)).astype(jnp.int32)
+    key = jnp.stack([cols_me, rows_me]).astype(jnp.int32)
+
+    def final_body(key_ref, *refs):
+        final_kernel(key_ref[0], key_ref[1], n_row, per, len(pcols), *refs)
+
     return call(
-        lambda key_ref, *refs: final_kernel(key_ref[0], n_rec, *refs),
+        final_body,
         shape(trailing_block.shape, F32),
-        [key, inverses, lows, pcols, *prows, trailing_block],
-        [pltpu.VMEM((PBLK * block, wide), BF16), pltpu.VMEM((PBLK * block, wide), BF16)],
+        [key, inverses, lows, *pcols, *prows, trailing_block],
+        [pltpu.VMEM((PBLK * block, wide), F32), pltpu.VMEM((PBLK * block, wide), BF16)],
         scalars=1,
     )
 

time: 124 us -> 102 us (0.82)
  between operations: 14.2 us -> 0.79 us
  starting transfers between devices: 41.3 us -> 28.6 us
  waiting for transfers between devices: 21.7 us -> 25.6 us
  local copies, waits for them, and re-layouts: 4.37 us -> 2.57 us
  Pallas kernels: 42.4 us -> 43.9 us
    ppermute x18 -> x24, starting transfers between devices: 39.8 us -> 27.1 us  [flipped(): return lax.ppermute(x, AXES, [(i, i ^ mask) for i in range(count)])]
    ppermute x18 -> x24, waiting for transfers between devices: 21.7 us -> 25.5 us  [flipped(): return lax.ppermute(x, AXES, [(i, i ^ mask) for i in range(count)])]
    unnamed x14 -> x10, local copies, waits for them, and re-layouts: 4.37 us -> 2.57 us
    pallas_call x4, Pallas kernels: 42.4 us -> 43.9 us  [call(): pl.pallas_call(kernel, out_shape=out_shape, in_specs=[SMEM if i < scalars...]
  transfers between devices with their start and end apart: 21 -> 26, of which waited for: 8 -> 8; matrix products, arithmetic and copies ran while one was open for 0% -> 0% of each run, Pallas kernels for 23% -> 27%
where the time goes in v2:
time: 102 us
  Pallas kernels  43.9 us (43%)
  starting transfers between devices  28.6 us (28%)
  waiting for transfers between devices  25.6 us (25%)
  local copies, waits for them, and re-layouts  2.57 us (3%)
    pallas_call x4, Pallas kernels, call(): pl.pallas_call(kernel, out_shape=out_shape, in_specs=[SMEM if i < scalars...  43.9 us
    ppermute x24, starting transfers between devices, flipped(): return lax.ppermute(x, AXES, [(i, i ^ mask) for i in range(count)])  27.1 us
    ppermute x24, waiting for transfers between devices, flipped(): return lax.ppermute(x, AXES, [(i, i ^ mask) for i in range(count)])  25.5 us
    unnamed x10, local copies, waits for them, and re-layouts  2.57 us
  transfers between devices with their start and end apart: 26, of which 8 were waited for; matrix products, arithmetic and copies ran while one was open for 0% of the time, Pallas kernels for 27%

profile of v2, /device:TPU:0, one launch (start us, length us, event | category | flops | bytes accessed | tf_op | source)
XLA Modules:
  0.0 101.5 jit_solution(5374440413343653109)
XLA Ops:
  0.7 0.0 copy-start.3
  0.7 0.0 copy-start.4
  0.7 0.7 copy-done.3
  1.3 0.0 copy-done.4
  1.3 1.0 copy-done.1
  2.3 0.9 copy-done.2
  3.2 9.4 %shard_map.64 = (f32[4,2,128,128]{3,2,1,0:T(8,128)S(1)}, f32[4,2,128,128]{3,2,1,0:T(8,128)S(1)}, bf16[2,272,128]{2,1,0:T(8,128)(2,1)S(1)}) custom-call(s32[1]{0:T(128)} %bitcast.ids_ref, s32[2]{0:T(128)S(1)} %copy-done.4, s32[1]{0:T(128)S(6)} %copy.7.refs_1_, bf16[2,256,128]{2,1,0:T(8,128)(2,1)S(1)} %copy-done.2, bf16[2,256,384]{2,1,0:T(8,128)(2,1)S(1)} %copy-done.1, ...), custom_call_target="tpu_custom_call" | custom-call | tf_op jit(solution)/shard_map/pallas_call | solution.py:247
  12.6 0.5 collective-permute-start
  13.1 1.5 %collective-permute-done.b_ref = f32[4,2,128,128]{3,2,1,0:T(8,128)S(1)} collective-permute-done((f32[4,2,128,128]{3,2,1,0:T(8,128)S(1)}, f32[4,2,128,128]{3,2,1,0:T(8,128)S(1)}, u32[]{:S(2)}, u32[]{:S(2)}) %collective-permute-start) | collective-permute-done | bytes 524320 | tf_op jit(solution)/shard_map/ppermute | solution.py:262
  14.7 0.1 shard_map.65
  14.7 3.9 %collective-permute-start.3 = (f32[2,128,128]{2,1,0:T(8,128)S(1)}, f32[2,128,128]{2,1,0:T(8,128)S(1)}, u32[]{:S(2)}, u32[]{:S(2)}) collective-permute-start(f32[2,128,128]{2,1,0:T(8,128)S(1)} %get-tuple-element.22), channel_id=1, source_target_pairs={{0,24},{1,25},{2,26},{3,27},{4,28},{5,29},{6,30},{7,31},{8,16},{9,... | collective-permute-start | bytes 393224 | tf_op jit(solution)/shard_map/ppermute | solution.py:262
  18.6 0.5 collective-permute-start.2
  19.2 0.1 collective-permute-start.1
  19.3 3.6 %collective-permute-done.3 = f32[2,128,128]{2,1,0:T(8,128)S(1)} collective-permute-done((f32[2,128,128]{2,1,0:T(8,128)S(1)}, f32[2,128,128]{2,1,0:T(8,128)S(1)}, u32[]{:S(2)}, u32[]{:S(2)}) %collective-permute-start.3) | collective-permute-done | bytes 131104 | tf_op jit(solution)/shard_map/ppermute | solution.py:262
  22.9 2.6 %collective-permute-done.2 = f32[2,128,128]{2,1,0:T(8,128)S(1)} collective-permute-done((f32[2,128,128]{2,1,0:T(8,128)S(1)}, f32[2,128,128]{2,1,0:T(8,128)S(1)}, u32[]{:S(2)}, u32[]{:S(2)}) %collective-permute-start.2) | collective-permute-done | bytes 131104 | tf_op jit(solution)/shard_map/ppermute | solution.py:262
  25.5 0.0 collective-permute-done.1
  25.5 3.7 %collective-permute-start.6 = (f32[2,128,128]{2,1,0:T(8,128)S(1)}, f32[2,128,128]{2,1,0:T(8,128)S(1)}, u32[]{:S(2)}, u32[]{:S(2)}) collective-permute-start(f32[2,128,128]{2,1,0:T(8,128)S(1)} %add_add_fusion.1), channel_id=1, source_target_pairs={{0,3},{1,2},{2,1},{3,0},{4,7},{5,6},{6,5},{7,4},{8,11},{9,10},{10,... | collective-permute-start | bytes 393224 | tf_op jit(solution)/shard_map/ppermute | solution.py:262
  29.2 0.0 collective-permute-start.5
  29.2 0.8 collective-permute-start.4
  30.0 0.7 collective-permute-start.14
  30.7 0.8 collective-permute-start.22
  31.5 2.4 %collective-permute-done.6 = f32[2,128,128]{2,1,0:T(8,128)S(1)} collective-permute-done((f32[2,128,128]{2,1,0:T(8,128)S(1)}, f32[2,128,128]{2,1,0:T(8,128)S(1)}, u32[]{:S(2)}, u32[]{:S(2)}) %collective-permute-start.6) | collective-permute-done | bytes 131104 | tf_op jit(solution)/shard_map/ppermute | solution.py:262
  33.9 10.1 %collective-permute-done.5 = f32[2,128,128]{2,1,0:T(8,128)S(1)} collective-permute-done((f32[2,128,128]{2,1,0:T(8,128)S(1)}, f32[2,128,128]{2,1,0:T(8,128)S(1)}, u32[]{:S(2)}, u32[]{:S(2)}) %collective-permute-start.5) | collective-permute-done | bytes 131104 | tf_op jit(solution)/shard_map/ppermute | solution.py:262
  44.0 0.0 collective-permute-done.4
  44.0 0.1 collective-permute-start.7
  44.1 1.3 %collective-permute-start.8 = (f32[2,128,128]{2,1,0:T(8,128)S(1)}, f32[2,128,128]{2,1,0:T(8,128)S(1)}, u32[]{:S(2)}, u32[]{:S(2)}) collective-permute-start(f32[2,128,128]{2,1,0:T(8,128)S(1)} %add_add_fusion.refs_0_), channel_id=1, source_target_pairs={{0,8},{1,9},{2,10},{3,11},{4,12},{5,13},{6,14},{7,15},{8,0},{9,1},... | collective-permute-start | bytes 393224 | tf_op jit(solution)/shard_map/ppermute | solution.py:262
  45.3 3.4 %collective-permute-start.10 = (f32[2,128,128]{2,1,0:T(8,128)S(1)}, f32[2,128,128]{2,1,0:T(8,128)S(1)}, u32[]{:S(2)}, u32[]{:S(2)}) collective-permute-start(f32[2,128,128]{2,1,0:T(8,128)S(1)} %add_add_fusion.refs_0_), channel_id=1, source_target_pairs={{0,16},{1,17},{2,18},{3,19},{4,20},{5,21},{6,22},{7,23},{8,24},{9,... | collective-permute-start | bytes 393224 | tf_op jit(solution)/shard_map/ppermute | solution.py:262
  48.7 0.0 collective-permute-done.14.refs_2_
  48.7 0.1 collective-permute-start.15
  48.8 0.0 collective-permute-done.22.refs_10_
  48.8 1.9 %collective-permute-start.16 = (bf16[2,272,128]{2,1,0:T(8,128)(2,1)S(1)}, bf16[2,272,128]{2,1,0:T(8,128)(2,1)S(1)}, u32[]{:S(2)}, u32[]{:S(2)}) collective-permute-start(bf16[2,272,128]{2,1,0:T(8,128)(2,1)S(1)} %collective-permute-done.14.refs_2_), channel_id=1, source_target_pairs={{0,8},{1,9},{2,10},{3,11},{4,12},{5,13},{6,14},{7,15},{8,0},{9,1},... | collective-permute-start | bytes 417800 | tf_op jit(solution)/shard_map/ppermute | solution.py:262
  50.7 0.0 collective-permute-done.7.refs_1_
  50.7 2.2 %collective-permute-start.18 = (bf16[2,272,128]{2,1,0:T(8,128)(2,1)S(1)}, bf16[2,272,128]{2,1,0:T(8,128)(2,1)S(1)}, u32[]{:S(2)}, u32[]{:S(2)}) collective-permute-start(bf16[2,272,128]{2,1,0:T(8,128)(2,1)S(1)} %collective-permute-done.14.refs_2_), channel_id=1, source_target_pairs={{0,16},{1,17},{2,18},{3,19},{4,20},{5,21},{6,22},{7,23},{8,24},{9,... | collective-permute-start | bytes 417800 | tf_op jit(solution)/shard_map/ppermute | solution.py:262
  52.9 0.0 collective-permute-done.8.refs_2_
  52.9 1.8 %collective-permute-start.12 = (f32[2,128,128]{2,1,0:T(8,128)S(1)}, f32[2,128,128]{2,1,0:T(8,128)S(1)}, u32[]{:S(2)}, u32[]{:S(2)}) collective-permute-start(f32[2,128,128]{2,1,0:T(8,128)S(1)} %add_add_fusion.refs_0_), channel_id=1, source_target_pairs={{0,24},{1,25},{2,26},{3,27},{4,28},{5,29},{6,30},{7,31},{8,16},{9,... | collective-permute-start | bytes 393224 | tf_op jit(solution)/shard_map/ppermute | solution.py:262
  54.7 0.5 collective-permute-done.10.refs_4_
  55.2 0.7 collective-permute-start.20
  55.8 4.3 %collective-permute-done.12.refs_6_ = f32[2,128,128]{2,1,0:T(8,128)S(1)} collective-permute-done((f32[2,128,128]{2,1,0:T(8,128)S(1)}, f32[2,128,128]{2,1,0:T(8,128)S(1)}, u32[]{:S(2)}, u32[]{:S(2)}) %collective-permute-start.12) | collective-permute-done | bytes 131104 | tf_op jit(solution)/shard_map/ppermute | solution.py:262
  60.1 1.9 %collective-permute-start.23 = (bf16[2,272,128]{2,1,0:T(8,128)(2,1)S(1)}, bf16[2,272,128]{2,1,0:T(8,128)(2,1)S(1)}, u32[]{:S(2)}, u32[]{:S(2)}) collective-permute-start(bf16[2,272,128]{2,1,0:T(8,128)(2,1)S(1)} %collective-permute-done.22.refs_10_), channel_id=1, source_target_pairs={{0,1},{1,0},{2,3},{3,2},{4,5},{5,4},{6,7},{7,6},{8,9},{9,8},{10,11... | collective-permute-start | bytes 417800 | tf_op jit(solution)/shard_map/ppermute | solution.py:262
  62.1 0.0 collective-permute-done.15.refs_3_
  62.1 0.0 collective-permute-start.9
  62.1 0.0 collective-permute-done.16.refs_4_
  62.1 0.5 collective-permute-start.11
  62.6 0.0 collective-permute-done.18.refs_6_
  62.6 0.1 collective-permute-start.13
  62.7 0.5 collective-permute-done.20.refs_8_
  63.1 2.8 %collective-permute-start.24 = (bf16[2,272,128]{2,1,0:T(8,128)(2,1)S(1)}, bf16[2,272,128]{2,1,0:T(8,128)(2,1)S(1)}, u32[]{:S(2)}, u32[]{:S(2)}) collective-permute-start(bf16[2,272,128]{2,1,0:T(8,128)(2,1)S(1)} %collective-permute-done.22.refs_10_), channel_id=1, source_target_pairs={{0,2},{1,3},{2,0},{3,1},{4,6},{5,7},{6,4},{7,5},{8,10},{9,11},{10,... | collective-permute-start | bytes 417800 | tf_op jit(solution)/shard_map/ppermute | solution.py:262
  66.0 0.0 collective-permute-done.9.refs_3_
  66.0 0.4 collective-permute-start.25
  66.4 0.0 collective-permute-done.11.refs_5_
  66.4 0.0 collective-permute-start.17
  66.4 0.0 collective-permute-done.13.refs_7_
  66.4 0.5 collective-permute-start.19
  66.9 0.0 collective-permute-done.23.refs_11_
  66.9 0.1 collective-permute-start.21
  67.0 0.1 pad_add_fusion.key_ref
  67.0 27.5 %shard_map.66 = (f32[8,128,128]{2,1,0:T(8,128)S(1)}, f32[11,128,128]{2,1,0:T(8,128)S(1)}) custom-call(s32[1]{0:T(128)} %bitcast.ids_ref, f32[2,128,128]{2,1,0:T(8,128)S(1)} %add_add_fusion.refs_0_, f32[2,128,128]{2,1,0:T(8,128)S(1)} %collective-permute-done.7.refs_1_, f32[2,128,128]{2,1,0:T(8,128)S(1)} %collective-permute-done.8.refs_2_, ...), custom_call_target="tpu_custom_call" | custom-call | tf_op jit(solution)/shard_map/pallas_call | solution.py:247
  94.6 0.0 collective-permute-done.24.refs_12_
  94.6 0.0 collective-permute-done.25.refs_13_
  94.6 0.0 collective-permute-done.17.refs_5_
  94.6 0.0 collective-permute-done.19.refs_7_
  94.6 0.0 collective-permute-done.21.refs_9_
  94.6 0.0 copy-done
  94.6 6.9 %shard_map.67 = f32[256,512]{1,0:T(8,128)} custom-call(s32[2]{0:T(128)S(1)} %pad_add_fusion.key_ref, f32[8,128,128]{2,1,0:T(8,128)S(1)} %get-tuple-element.23.refs_0_, f32[11,128,128]{2,1,0:T(8,128)S(1)} %get-tuple-element.24.refs_1_, bf16[2,272,128]{2,1,0:T(8,128)(2,1)S(1)} %collective-permute-done.14.refs_2_, ...), custom_call_target="tpu_custom_call" | custom-call | tf_op jit(solution)/shard_map/pallas_call | solution.py:247
  (5 shorter events, 0.1 us)
Async XLA Ops:
  0.7 0.7 copy-start.3
  0.7 0.7 copy-start.4
  1.3 1.0 copy-start.1
  2.3 0.9 copy-start.2
  12.6 2.1 %collective-permute-start = (f32[4,2,128,128]{3,2,1,0:T(8,128)S(1)}, f32[4,2,128,128]{3,2,1,0:T(8,128)S(1)}, u32[]{:S(2)}, u32[]{:S(2)}) collective-permute-start(f32[4,2,128,128]{3,2,1,0:T(8,128)S(1)} %get-tuple-element.18), channel_id=1, source_target_pairs={{0,4},{1,5},{2,6},{3,7},{4,0},{5,1},{6,2},{7,3},{8,12},{9,13},{10,... | collective-permute-start | bytes 1572872 | tf_op jit(solution)/shard_map/ppermute | solution.py:262
  14.7 8.2 %collective-permute-start.3 = (f32[2,128,128]{2,1,0:T(8,128)S(1)}, f32[2,128,128]{2,1,0:T(8,128)S(1)}, u32[]{:S(2)}, u32[]{:S(2)}) collective-permute-start(f32[2,128,128]{2,1,0:T(8,128)S(1)} %get-tuple-element.22), channel_id=1, source_target_pairs={{0,24},{1,25},{2,26},{3,27},{4,28},{5,29},{6,30},{7,31},{8,16},{9,... | collective-permute-start | bytes 393224 | tf_op jit(solution)/shard_map/ppermute | solution.py:262
  18.6 6.9 %collective-permute-start.2 = (f32[2,128,128]{2,1,0:T(8,128)S(1)}, f32[2,128,128]{2,1,0:T(8,128)S(1)}, u32[]{:S(2)}, u32[]{:S(2)}) collective-permute-start(f32[2,128,128]{2,1,0:T(8,128)S(1)} %get-tuple-element.21), channel_id=1, source_target_pairs={{0,16},{1,17},{2,18},{3,19},{4,20},{5,21},{6,22},{7,23},{8,24},{9,... | collective-permute-start | bytes 393224 | tf_op jit(solution)/shard_map/ppermute | solution.py:262
  19.2 6.3 %collective-permute-start.1 = (f32[2,128,128]{2,1,0:T(8,128)S(1)}, f32[2,128,128]{2,1,0:T(8,128)S(1)}, u32[]{:S(2)}, u32[]{:S(2)}) collective-permute-start(f32[2,128,128]{2,1,0:T(8,128)S(1)} %get-tuple-element.20), channel_id=1, source_target_pairs={{0,8},{1,9},{2,10},{3,11},{4,12},{5,13},{6,14},{7,15},{8,0},{9,1},... | collective-permute-start | bytes 393224 | tf_op jit(solution)/shard_map/ppermute | solution.py:262
  25.5 8.3 %collective-permute-start.6 = (f32[2,128,128]{2,1,0:T(8,128)S(1)}, f32[2,128,128]{2,1,0:T(8,128)S(1)}, u32[]{:S(2)}, u32[]{:S(2)}) collective-permute-start(f32[2,128,128]{2,1,0:T(8,128)S(1)} %add_add_fusion.1), channel_id=1, source_target_pairs={{0,3},{1,2},{2,1},{3,0},{4,7},{5,6},{6,5},{7,4},{8,11},{9,10},{10,... | collective-permute-start | bytes 393224 | tf_op jit(solution)/shard_map/ppermute | solution.py:262
  29.2 14.8 %collective-permute-start.5 = (f32[2,128,128]{2,1,0:T(8,128)S(1)}, f32[2,128,128]{2,1,0:T(8,128)S(1)}, u32[]{:S(2)}, u32[]{:S(2)}) collective-permute-start(f32[2,128,128]{2,1,0:T(8,128)S(1)} %add_add_fusion.1), channel_id=1, source_target_pairs={{0,2},{1,3},{2,0},{3,1},{4,6},{5,7},{6,4},{7,5},{8,10},{9,11},{10,... | collective-permute-start | bytes 393224 | tf_op jit(solution)/shard_map/ppermute | solution.py:262
  29.2 14.8 %collective-permute-start.4 = (f32[2,128,128]{2,1,0:T(8,128)S(1)}, f32[2,128,128]{2,1,0:T(8,128)S(1)}, u32[]{:S(2)}, u32[]{:S(2)}) collective-permute-start(f32[2,128,128]{2,1,0:T(8,128)S(1)} %add_add_fusion.1), channel_id=1, source_target_pairs={{0,1},{1,0},{2,3},{3,2},{4,5},{5,4},{6,7},{7,6},{8,9},{9,8},{10,11... | collective-permute-start | bytes 393224 | tf_op jit(solution)/shard_map/ppermute | solution.py:262
  30.0 18.7 %collective-permute-start.14 = (bf16[2,272,128]{2,1,0:T(8,128)(2,1)S(1)}, bf16[2,272,128]{2,1,0:T(8,128)(2,1)S(1)}, u32[]{:S(2)}, u32[]{:S(2)}) collective-permute-start(bf16[2,272,128]{2,1,0:T(8,128)(2,1)S(1)} %get-tuple-element.26), channel_id=1, source_target_pairs={{0,0},{4,1},{8,2},{12,3},{1,4},{5,5},{9,6},{13,7},{2,8},{6,9},{10,... | collective-permute-start | bytes 417800 | tf_op jit(solution)/shard_map/ppermute | solution.py:306
  30.7 18.1 %collective-permute-start.22 = (bf16[2,272,128]{2,1,0:T(8,128)(2,1)S(1)}, bf16[2,272,128]{2,1,0:T(8,128)(2,1)S(1)}, u32[]{:S(2)}, u32[]{:S(2)}) collective-permute-start(bf16[2,272,128]{2,1,0:T(8,128)(2,1)S(1)} %get-tuple-element.26), channel_id=1, source_target_pairs={{0,0},{1,1},{16,2},{17,3},{18,4},{19,5},{2,6},{3,7},{4,8},{5,9},{2... | collective-permute-start | bytes 417800 | tf_op jit(solution)/shard_map/ppermute | solution.py:307
  44.0 6.7 %collective-permute-start.7 = (f32[2,128,128]{2,1,0:T(8,128)S(1)}, f32[2,128,128]{2,1,0:T(8,128)S(1)}, u32[]{:S(2)}, u32[]{:S(2)}) collective-permute-start(f32[2,128,128]{2,1,0:T(8,128)S(1)} %add_add_fusion.refs_0_), channel_id=1, source_target_pairs={{0,4},{1,5},{2,6},{3,7},{4,0},{5,1},{6,2},{7,3},{8,12},{9,13},{10,... | collective-permute-start | bytes 393224 | tf_op jit(solution)/shard_map/ppermute | solution.py:262
  44.1 8.8 %collective-permute-start.8 = (f32[2,128,128]{2,1,0:T(8,128)S(1)}, f32[2,128,128]{2,1,0:T(8,128)S(1)}, u32[]{:S(2)}, u32[]{:S(2)}) collective-permute-start(f32[2,128,128]{2,1,0:T(8,128)S(1)} %add_add_fusion.refs_0_), channel_id=1, source_target_pairs={{0,8},{1,9},{2,10},{3,11},{4,12},{5,13},{6,14},{7,15},{8,0},{9,1},... | collective-permute-start | bytes 393224 | tf_op jit(solution)/shard_map/ppermute | solution.py:262
  45.3 9.8 %collective-permute-start.10 = (f32[2,128,128]{2,1,0:T(8,128)S(1)}, f32[2,128,128]{2,1,0:T(8,128)S(1)}, u32[]{:S(2)}, u32[]{:S(2)}) collective-permute-start(f32[2,128,128]{2,1,0:T(8,128)S(1)} %add_add_fusion.refs_0_), channel_id=1, source_target_pairs={{0,16},{1,17},{2,18},{3,19},{4,20},{5,21},{6,22},{7,23},{8,24},{9,... | collective-permute-start | bytes 393224 | tf_op jit(solution)/shard_map/ppermute | solution.py:262
  48.7 13.4 %collective-permute-start.15 = (bf16[2,272,128]{2,1,0:T(8,128)(2,1)S(1)}, bf16[2,272,128]{2,1,0:T(8,128)(2,1)S(1)}, u32[]{:S(2)}, u32[]{:S(2)}) collective-permute-start(bf16[2,272,128]{2,1,0:T(8,128)(2,1)S(1)} %collective-permute-done.14.refs_2_), channel_id=1, source_target_pairs={{0,4},{1,5},{2,6},{3,7},{4,0},{5,1},{6,2},{7,3},{8,12},{9,13},{10,... | collective-permute-start | bytes 417800 | tf_op jit(solution)/shard_map/ppermute | solution.py:262
  48.8 13.3 %collective-permute-start.16 = (bf16[2,272,128]{2,1,0:T(8,128)(2,1)S(1)}, bf16[2,272,128]{2,1,0:T(8,128)(2,1)S(1)}, u32[]{:S(2)}, u32[]{:S(2)}) collective-permute-start(bf16[2,272,128]{2,1,0:T(8,128)(2,1)S(1)} %collective-permute-done.14.refs_2_), channel_id=1, source_target_pairs={{0,8},{1,9},{2,10},{3,11},{4,12},{5,13},{6,14},{7,15},{8,0},{9,1},... | collective-permute-start | bytes 417800 | tf_op jit(solution)/shard_map/ppermute | solution.py:262
  50.7 11.9 %collective-permute-start.18 = (bf16[2,272,128]{2,1,0:T(8,128)(2,1)S(1)}, bf16[2,272,128]{2,1,0:T(8,128)(2,1)S(1)}, u32[]{:S(2)}, u32[]{:S(2)}) collective-permute-start(bf16[2,272,128]{2,1,0:T(8,128)(2,1)S(1)} %collective-permute-done.14.refs_2_), channel_id=1, source_target_pairs={{0,16},{1,17},{2,18},{3,19},{4,20},{5,21},{6,22},{7,23},{8,24},{9,... | collective-permute-start | bytes 417800 | tf_op jit(solution)/shard_map/ppermute | solution.py:262
  52.9 7.2 %collective-permute-start.12 = (f32[2,128,128]{2,1,0:T(8,128)S(1)}, f32[2,128,128]{2,1,0:T(8,128)S(1)}, u32[]{:S(2)}, u32[]{:S(2)}) collective-permute-start(f32[2,128,128]{2,1,0:T(8,128)S(1)} %add_add_fusion.refs_0_), channel_id=1, source_target_pairs={{0,24},{1,25},{2,26},{3,27},{4,28},{5,29},{6,30},{7,31},{8,16},{9,... | collective-permute-start | bytes 393224 | tf_op jit(solution)/shard_map/ppermute | solution.py:262
  55.2 8.0 %collective-permute-start.20 = (bf16[2,272,128]{2,1,0:T(8,128)(2,1)S(1)}, bf16[2,272,128]{2,1,0:T(8,128)(2,1)S(1)}, u32[]{:S(2)}, u32[]{:S(2)}) collective-permute-start(bf16[2,272,128]{2,1,0:T(8,128)(2,1)S(1)} %collective-permute-done.14.refs_2_), channel_id=1, source_target_pairs={{0,24},{1,25},{2,26},{3,27},{4,28},{5,29},{6,30},{7,31},{8,16},{9,... | collective-permute-start | bytes 417800 | tf_op jit(solution)/shard_map/ppermute | solution.py:262
  60.1 6.8 %collective-permute-start.23 = (bf16[2,272,128]{2,1,0:T(8,128)(2,1)S(1)}, bf16[2,272,128]{2,1,0:T(8,128)(2,1)S(1)}, u32[]{:S(2)}, u32[]{:S(2)}) collective-permute-start(bf16[2,272,128]{2,1,0:T(8,128)(2,1)S(1)} %collective-permute-done.22.refs_10_), channel_id=1, source_target_pairs={{0,1},{1,0},{2,3},{3,2},{4,5},{5,4},{6,7},{7,6},{8,9},{9,8},{10,11... | collective-permute-start | bytes 417800 | tf_op jit(solution)/shard_map/ppermute | solution.py:262
  62.1 3.9 %collective-permute-start.9 = (f32[2,128,128]{2,1,0:T(8,128)S(1)}, f32[2,128,128]{2,1,0:T(8,128)S(1)}, u32[]{:S(2)}, u32[]{:S(2)}) collective-permute-start(f32[2,128,128]{2,1,0:T(8,128)S(1)} %collective-permute-done.8.refs_2_), channel_id=1, source_target_pairs={{0,4},{1,5},{2,6},{3,7},{4,0},{5,1},{6,2},{7,3},{8,12},{9,13},{10,... | collective-permute-start | bytes 393224 | tf_op jit(solution)/shard_map/ppermute | solution.py:262
  62.1 4.3 %collective-permute-start.11 = (f32[2,128,128]{2,1,0:T(8,128)S(1)}, f32[2,128,128]{2,1,0:T(8,128)S(1)}, u32[]{:S(2)}, u32[]{:S(2)}) collective-permute-start(f32[2,128,128]{2,1,0:T(8,128)S(1)} %collective-permute-done.10.refs_4_), channel_id=1, source_target_pairs={{0,4},{1,5},{2,6},{3,7},{4,0},{5,1},{6,2},{7,3},{8,12},{9,13},{10,... | collective-permute-start | bytes 393224 | tf_op jit(solution)/shard_map/ppermute | solution.py:262
  62.6 3.8 %collective-permute-start.13 = (f32[2,128,128]{2,1,0:T(8,128)S(1)}, f32[2,128,128]{2,1,0:T(8,128)S(1)}, u32[]{:S(2)}, u32[]{:S(2)}) collective-permute-start(f32[2,128,128]{2,1,0:T(8,128)S(1)} %collective-permute-done.12.refs_6_), channel_id=1, source_target_pairs={{0,4},{1,5},{2,6},{3,7},{4,0},{5,1},{6,2},{7,3},{8,12},{9,13},{10,... | collective-permute-start | bytes 393224 | tf_op jit(solution)/shard_map/ppermute | solution.py:262
  63.1 31.4 %collective-permute-start.24 = (bf16[2,272,128]{2,1,0:T(8,128)(2,1)S(1)}, bf16[2,272,128]{2,1,0:T(8,128)(2,1)S(1)}, u32[]{:S(2)}, u32[]{:S(2)}) collective-permute-start(bf16[2,272,128]{2,1,0:T(8,128)(2,1)S(1)} %collective-permute-done.22.refs_10_), channel_id=1, source_target_pairs={{0,2},{1,3},{2,0},{3,1},{4,6},{5,7},{6,4},{7,5},{8,10},{9,11},{10,... | collective-permute-start | bytes 417800 | tf_op jit(solution)/shard_map/ppermute | solution.py:262
  66.0 28.6 %collective-permute-start.25 = (bf16[2,272,128]{2,1,0:T(8,128)(2,1)S(1)}, bf16[2,272,128]{2,1,0:T(8,128)(2,1)S(1)}, u32[]{:S(2)}, u32[]{:S(2)}) collective-permute-start(bf16[2,272,128]{2,1,0:T(8,128)(2,1)S(1)} %collective-permute-done.22.refs_10_), channel_id=1, source_target_pairs={{0,3},{1,2},{2,1},{3,0},{4,7},{5,6},{6,5},{7,4},{8,11},{9,10},{10,... | collective-permute-start | bytes 417800 | tf_op jit(solution)/shard_map/ppermute | solution.py:262
  66.4 28.2 %collective-permute-start.17 = (bf16[2,272,128]{2,1,0:T(8,128)(2,1)S(1)}, bf16[2,272,128]{2,1,0:T(8,128)(2,1)S(1)}, u32[]{:S(2)}, u32[]{:S(2)}) collective-permute-start(bf16[2,272,128]{2,1,0:T(8,128)(2,1)S(1)} %collective-permute-done.16.refs_4_), channel_id=1, source_target_pairs={{0,4},{1,5},{2,6},{3,7},{4,0},{5,1},{6,2},{7,3},{8,12},{9,13},{10,... | collective-permute-start | bytes 417800 | tf_op jit(solution)/shard_map/ppermute | solution.py:262
  66.4 28.2 %collective-permute-start.19 = (bf16[2,272,128]{2,1,0:T(8,128)(2,1)S(1)}, bf16[2,272,128]{2,1,0:T(8,128)(2,1)S(1)}, u32[]{:S(2)}, u32[]{:S(2)}) collective-permute-start(bf16[2,272,128]{2,1,0:T(8,128)(2,1)S(1)} %collective-permute-done.18.refs_6_), channel_id=1, source_target_pairs={{0,4},{1,5},{2,6},{3,7},{4,0},{5,1},{6,2},{7,3},{8,12},{9,13},{10,... | collective-permute-start | bytes 417800 | tf_op jit(solution)/shard_map/ppermute | solution.py:262
  66.9 27.7 %collective-permute-start.21 = (bf16[2,272,128]{2,1,0:T(8,128)(2,1)S(1)}, bf16[2,272,128]{2,1,0:T(8,128)(2,1)S(1)}, u32[]{:S(2)}, u32[]{:S(2)}) collective-permute-start(bf16[2,272,128]{2,1,0:T(8,128)(2,1)S(1)} %collective-permute-done.20.refs_8_), channel_id=1, source_target_pairs={{0,4},{1,5},{2,6},{3,7},{4,0},{5,1},{6,2},{7,3},{8,12},{9,13},{10,... | collective-permute-start | bytes 417800 | tf_op jit(solution)/shard_map/ppermute | solution.py:262
  67.0 27.6 %copy-start = (f32[256,512]{1,0:T(8,128)S(1)}, f32[256,512]{1,0:T(8,128)}, u32[]{:S(2)}) copy-start(f32[256,512]{1,0:T(8,128)} %refs_14_.1) | copy-start | bytes 1572868

commit v3 on v2

--- a/solution.py
+++ b/solution.py
@@ -13,6 +13,7 @@
 BF16 = jnp.bfloat16
 SUB = 8
 TAIL = 16
+EARLY = 2
 VMEM_BYTES = 40 * 1024 * 1024
 
 ROWS_BY_ROWS = (((0,), (0,)), ((), ()))
@@ -47,7 +48,14 @@
     return jnp.broadcast_to(x[at : at + 1, :], (SUB, size))
 
 
-def factor_step(rows, step, lane, sub):
+def tree_sum(terms):
+    while len(terms) > 1:
+        pairs = [terms[i] + terms[i + 1] for i in range(0, len(terms) - 1, 2)]
+        terms = pairs + terms[len(terms) - len(terms) % 2 :]
+    return terms[0]
+
+
+def factor_step(rows, step, last, lane, sub):
     size = lane.shape[1]
     first = step * SUB
     inside = (lane >= first) & (lane < first + SUB)
@@ -55,45 +63,70 @@
     entry = {
         (i, j): lane_copy(pivot_rows[i], first + j, size) for i in range(SUB) for j in range(i, SUB)
     }
-    below = range(step + 1, len(rows))
+    below = range(step + 1, last)
     cols = {r: [lane_copy(rows[r], first + j, size) for j in range(SUB)] for r in below}
     left = [
         jnp.where(inside, jnp.where(lane == first + i, 1.0, 0.0), pivot_rows[i]) for i in range(SUB)
     ]
     recip = [None] * SUB
-    mult = {}
     for k in range(SUB):
-        recip[k] = 1.0 / entry[(k, k)]
+        if k % 2 == 0:
+            pivot, beside = entry[(k, k)], entry[(k, k + 1)]
+            recip[k] = 1.0 / pivot
+            recip[k + 1] = pivot * (1.0 / (pivot * entry[(k + 1, k + 1)] - beside * beside))
         for i in range(k + 1, SUB):
-            mult[(i, k)] = entry[(k, i)] * recip[k]
-        for i in range(k + 1, SUB):
+            mult = entry[(k, i)] * recip[k]
             for j in range(i, SUB):
-                entry[(i, j)] = entry[(i, j)] - mult[(i, k)] * entry[(k, j)]
-            left[i] = left[i] - mult[(i, k)] * left[k]
+                entry[(i, j)] = entry[(i, j)] - mult * entry[(k, j)]
+            left[i] = left[i] - mult * left[k]
+            for r in below:
+                cols[r][i] = cols[r][i] - mult * cols[r][k]
     solved = [left[i] * recip[i] for i in range(SUB)]
+    for r in below:
+        part = tree_sum([cols[r][j] * solved[j] for j in range(SUB)])
+        rows[r] = jnp.where(inside, 0.0, rows[r]) - part
     done = left[0] * lax.sqrt(recip[0])
     for i in range(1, SUB):
         done = jnp.where(sub == i, left[i] * lax.sqrt(recip[i]), done)
-    for k in range(SUB - 1, 0, -1):
-        for i in range(k):
-            solved[i] = solved[i] - mult[(k, i)] * solved[k]
-    for r in below:
-        part = [cols[r][j] * solved[j] for j in range(SUB)]
-        while len(part) > 1:
-            part = [part[i] + part[i + 1] for i in range(0, len(part), 2)]
-        rows[r] = jnp.where(inside, 0.0, rows[r]) - part[0]
-    rows[step] = jnp.where(lane < first + SUB, done, 0.0)
-
-
-def inverse_factors(mats):
+    rows[step] = done
+
+
+def inverse_factors(mats, work=()):
     size = mats[0].shape[0]
     lane = lax.broadcasted_iota(jnp.int32, (SUB, size), 1)
     sub = lax.broadcasted_iota(jnp.int32, (SUB, size), 0)
     state = [[m[r : r + SUB, :] for r in range(0, size, SUB)] for m in mats]
-    for step in range(size // SUB):
+    steps = size // SUB
+    group = steps // 8 if len(mats) > 2 else steps // 2
+    work = list(work)
+    share = -(-len(work) // steps)
+    for start in range(0, steps, group):
+        stop = start + group
+        for step in range(start, stop):
+            for rows in state:
+                factor_step(rows, step, stop, lane, sub)
+            for item in work[step * share : (step + 1) * share]:
+                item()
         for rows in state:
-            factor_step(rows, step, lane, sub)
-    return [jnp.concatenate(rows, axis=0) for rows in state]
+            for step in range(start, stop):
+                beyond = (lane >= (step + 1) * SUB) & (lane < stop * SUB)
+                rows[step] = jnp.where(beyond, 0.0, rows[step])
+            if stop < steps:
+                high, low = split(jnp.concatenate(rows[start:stop], axis=0))
+                update = lax.dot_general(
+                    jnp.concatenate([high, high, low], axis=0),
+                    jnp.concatenate([high, low, high], axis=0),
+                    ROWS_BY_ROWS,
+                    preferred_element_type=F32,
+                )
+                inside = (lane >= start * SUB) & (lane < stop * SUB)
+                for r in range(stop, steps):
+                    rows[r] = jnp.where(inside, 0.0, rows[r]) - update[r * SUB : (r + 1) * SUB]
+    out = []
+    for rows in state:
+        rows = [jnp.where(lane < (r + 1) * SUB, rows[r], 0.0) for r in range(steps)]
+        out.append(jnp.concatenate(rows, axis=0))
+    return out
 
 
 def local_kernel(
@@ -169,68 +202,107 @@
     return levels
 
 
-def couplings_of(count):
-    return [
-        (k, n, side)
-        for level in levels_of(count)
-        for k, before, after in level
-        for n, side in ((before, "before"), (after, "after"))
-        if n is not None
+def eliminate(level, diag, off, work):
+    inverses = inverse_factors([diag[k] for k, _, _ in level], work)
+    lows = {}
+    for (k, before, after), inv in zip(level, inverses):
+        if before is not None:
+            low_b = dot3(inv, off[(k, before)], PLAIN)
+            lows[(k, before)] = low_b
+            diag[before] = diag[before] - dot3(low_b, low_b, ROWS_BY_ROWS)
+        if after is not None:
+            low_a = dot3(off[(after, k)], inv, COLS_BY_COLS)
+            lows[(k, after)] = low_a
+            diag[after] = diag[after] - dot3(low_a, low_a, COLS_BY_COLS)
+        if before is not None and after is not None:
+            off[(after, before)] = -dot3(low_a, low_b, PLAIN)
+    return {k: inv for (k, _, _), inv in zip(level, inverses)}, lows
+
+
+def early_layout():
+    levels = levels_of(PBLK)
+    early, late = levels[:EARLY], levels[EARLY:]
+    invs = [k for level in early for k, _, _ in level]
+    lows = [
+        (k, n) for level in early for k, before, after in level for n in (before, after) if n is not None
     ]
-
-
-def chain_kernel(me, *refs):
+    left = sorted(k for level in late for k, _, _ in level)
+    return invs, lows, left, list(zip(left[1:], left[:-1]))
+
+
+def factor_kernel(me, *refs):
     pieces = refs[:PBLK]
-    inv_ref, low_ref, tri = refs[PBLK:]
+    inv_ref, low_ref, left_ref, tri = refs[PBLK:]
     for j in range(PBLK):
         tri[lax.bitwise_xor(me, j)] = pieces[j][...]
     diag = {k: tri[k, 0] for k in range(PBLK)}
     off = {(k, k - 1): tri[k, 1] for k in range(1, PBLK)}
-    slot = {key[:2]: i for i, key in enumerate(couplings_of(PBLK))}
-    for level in levels_of(PBLK):
-        inverses = inverse_factors([diag[k] for k, _, _ in level])
-        for (k, before, after), inv in zip(level, inverses):
-            inv_ref[k] = inv
-            if before is not None:
-                low_b = dot3(inv, off[(k, before)], PLAIN)
-                low_ref[slot[(k, before)]] = low_b
-                diag[before] = diag[before] - dot3(low_b, low_b, ROWS_BY_ROWS)
-            if after is not None:
-                low_a = dot3(off[(after, k)], inv, COLS_BY_COLS)
-                low_ref[slot[(k, after)]] = low_a
-                diag[after] = diag[after] - dot3(low_a, low_a, COLS_BY_COLS)
-            if before is not None and after is not None:
-                off[(after, before)] = -dot3(low_a, low_b, PLAIN)
-
-
-def final_kernel(cols_me, rows_me, n_row, per, n_cols, inv_ref, low_ref, *refs):
+    invs, lows, left, links = early_layout()
+    for level in levels_of(PBLK)[:EARLY]:
+        new_invs, new_lows = eliminate(level, diag, off, ())
+        for k, value in new_invs.items():
+            inv_ref[invs.index(k)] = value
+        for key, value in new_lows.items():
+            low_ref[lows.index(key)] = value
+    for i, k in enumerate(left):
+        left_ref[i] = diag[k]
+    for i, key in enumerate(links):
+        left_ref[len(left) + i] = off[key]
+
+
+def panel_kernel(cols_me, rows_me, n_row, per, n_cols, inv_ref, low_ref, left_ref, *refs):
     terms, (trail_ref, out_ref, panel, solved) = refs[:-4], refs[-4:]
     slots, height, block = terms[0].shape
     height = height - TAIL
     tile_rows = trail_ref.shape[0]
-    panel[...] = jnp.zeros_like(panel)
-    for n, term in enumerate(terms):
+
+    def place(n, b):
         if n < n_cols:
             over = tile_rows + lax.rem(lax.bitwise_xor(cols_me, n), n_row) * block
         else:
             over = lax.rem(lax.bitwise_xor(rows_me, n - n_cols), per) * block
         over = pl.multiple_of(over, block)
-        for b in range(slots):
-            k = jnp.max(term[b, height:, :].astype(F32)).astype(jnp.int32)
-            down = pl.multiple_of(k * block, block)
-            panel[pl.ds(down, height), pl.ds(over, block)] += term[b, :height, :].astype(F32)
-    slot = {key[:2]: i for i, key in enumerate(couplings_of(PBLK))}
-    value = {k: panel[k * block : (k + 1) * block, :] for k in range(PBLK)}
-    for level in levels_of(PBLK):
+        term = terms[n]
+        k = jnp.max(term[b, height:, :].astype(F32)).astype(jnp.int32)
+        down = pl.multiple_of(k * block, block)
+        panel[pl.ds(down, height), pl.ds(over, block)] += term[b, :height, :].astype(F32)
+
+    def rows_of(k):
+        return pl.ds(k * block, block)
+
+    def solve(k, inv):
+        value = dot3(inv[...], panel[rows_of(k), :], PLAIN)
+        panel[rows_of(k), :] = value
+        solved[rows_of(k), :] = value.astype(BF16)
+
+    def couple(k, n, low):
+        dims = PLAIN if n > k else ROWS_BY_ROWS
+        panel[rows_of(n), :] -= dot3(low[...], panel[rows_of(k), :], dims)
+
+    def solve_level(level, inverses, lows):
+        items = []
         for k, before, after in level:
-            sol = dot3(inv_ref[k], value[k], PLAIN)
-            solved[k * block : (k + 1) * block, :] = sol.astype(BF16)
-            if before is not None:
-                low_b = low_ref[slot[(k, before)]]
-                value[before] = value[before] - dot3(low_b, sol, ROWS_BY_ROWS)
-            if after is not None:
-                low_a = low_ref[slot[(k, after)]]
-                value[after] = value[after] - dot3(low_a, sol, PLAIN)
+            items.append(functools.partial(solve, k, inverses[k]))
+            for n in (before, after):
+                if n is not None:
+                    items.append(functools.partial(couple, k, n, lows[(k, n)]))
+        return items
+
+    panel[...] = jnp.zeros_like(panel)
+    invs, lows, left, links = early_layout()
+    early_invs = {k: inv_ref.at[i] for i, k in enumerate(invs)}
+    early_lows = {key: low_ref.at[i] for i, key in enumerate(lows)}
+    diag = {k: left_ref[i] for i, k in enumerate(left)}
+    off = {key: left_ref[len(left) + i] for i, key in enumerate(links)}
+    levels = levels_of(PBLK)
+    work = [functools.partial(place, n, b) for n in range(len(terms)) for b in range(slots)]
+    for level in levels[:EARLY]:
+        work += solve_level(level, early_invs, early_lows)
+    for level in levels[EARLY:]:
+        new_invs, new_lows = eliminate(level, diag, off, work)
+        work = solve_level(level, new_invs, new_lows)
+    for item in work:
+        item()
     update = lax.dot_general(
         solved[:, :tile_rows], solved[:, tile_rows:], ROWS_BY_ROWS, preferred_element_type=F32
     )
@@ -311,46 +383,43 @@
         if bit & (bit - 1) == 0:
             total = total + flipped(total, bit * low_rec * n_row * n_col, count)
     if direct:
-        parts = [flipped(total, m, count) for m in range(1, n_col)]
-        pcols = after(pcols, parts[0])
-        pcols = [pcols] + [flipped(pcols, 2 * j * n_col, count) for j in range(1, half)]
-        total = sum(parts, total)
+        total = sum([flipped(total, m, count) for m in range(1, n_col)], total)
     else:
         total = lax.psum(total, "col")
     evens = [total] + [flipped(total, 2 * j * n_col, count) for j in range(1, half)]
+    pcols, prows = after((pcols, prows), evens)
+    odds = [flipped(x, n_col, count) for x in evens]
+    tri = [x for pair in zip(evens, odds) for x in pair]
     if direct:
-        prows = after(prows, evens[1])
+        pcols = [pcols] + [flipped(pcols, 2 * j * n_col, count) for j in range(1, half)]
         prows = [prows] + [flipped(prows, m, count) for m in range(1, n_col)]
-        others = [flipped(x, n_col, count) for x in pcols]
-        pcols = [x for pair in zip(pcols, others) for x in pair]
         cols_me, rows_me = me, col
     else:
         pcols = list(lax.all_gather(pcols, ("rec", "row"), axis=0))
         prows = list(lax.all_gather(prows, "col", axis=0))
         cols_me = rows_me = jnp.int32(0)
-    odds = [flipped(x, n_col, count) for x in evens]
-    tri = [x for pair in zip(evens, odds) for x in pair]
-
-    inverses, lows = call(
-        lambda ids_ref, *refs: chain_kernel(ids_ref[0], *refs),
-        [
-            shape((PBLK, block, block), F32),
-            shape((len(couplings_of(PBLK)), block, block), F32),
-        ],
-        [ids, *tri],
+    wide = trailing_block.shape[0] + trailing_block.shape[1]
+    key = jnp.stack([me, cols_me, rows_me]).astype(jnp.int32)
+    invs, lows, left, links = early_layout()
+    early = call(
+        lambda key_ref, *refs: factor_kernel(key_ref[0], *refs),
+        [shape((n, block, block), F32) for n in (len(invs), len(lows), len(left) + len(links))],
+        [key, *tri],
         [pltpu.VMEM((PBLK, 2, block, block), F32)],
         scalars=1,
     )
-    wide = trailing_block.shape[0] + trailing_block.shape[1]
-    key = jnp.stack([cols_me, rows_me]).astype(jnp.int32)
-
-    def final_body(key_ref, *refs):
-        final_kernel(key_ref[0], key_ref[1], n_row, per, len(pcols), *refs)
+    if direct:
+        pcols = after(pcols, early)
+        others = [flipped(x, n_col, count) for x in pcols]
+        pcols = [x for pair in zip(pcols, others) for x in pair]
+
+    def panel_body(key_ref, *refs):
+        panel_kernel(key_ref[1], key_ref[2], n_row, per, len(pcols), *refs)
 
     return call(
-        final_body,
+        panel_body,
         shape(trailing_block.shape, F32),
-        [key, inverses, lows, *pcols, *prows, trailing_block],
+        [key, *early, *pcols, *prows, trailing_block],
         [pltpu.VMEM((PBLK * block, wide), F32), pltpu.VMEM((PBLK * block, wide), BF16)],
         scalars=1,
     )

time: 102 us -> 93.2 us (0.914)
  Pallas kernels: 43.9 us -> 33.6 us
  starting transfers between devices: 28.6 us -> 32.7 us
  waiting for transfers between devices: 25.6 us -> 23.2 us
    pallas_call x4, Pallas kernels: 43.9 us -> 33.6 us  [call(): pl.pallas_call(kernel, out_shape=out_shape, in_specs=[SMEM if i < scalars...]
    ppermute x24, starting transfers between devices: 27.1 us -> 31.2 us  [flipped(): return lax.ppermute(x, AXES, [(i, i ^ mask) for i in range(count)])]
    ppermute x24, waiting for transfers between devices: 25.5 us -> 23.2 us  [flipped(): return lax.ppermute(x, AXES, [(i, i ^ mask) for i in range(count)])]
  transfers between devices with their start and end apart: 26 -> 26, of which waited for: 8 -> 8; matrix products, arithmetic and copies ran while one was open for 0% -> 0% of each run, Pallas kernels for 27% -> 15%
where the time goes in v3:
time: 93.2 us; the launch traced here: 93 us
  Pallas kernels  33.6 us (36%)
  starting transfers between devices  32.7 us (35%)
  waiting for transfers between devices  23.2 us (25%)
  local copies, waits for them, and re-layouts  2.57 us (3%)
    pallas_call x4, Pallas kernels, call(): pl.pallas_call(kernel, out_shape=out_shape, in_specs=[SMEM if i < scalars...  33.6 us
    ppermute x24, starting transfers between devices, flipped(): return lax.ppermute(x, AXES, [(i, i ^ mask) for i in range(count)])  31.2 us
    ppermute x24, waiting for transfers between devices, flipped(): return lax.ppermute(x, AXES, [(i, i ^ mask) for i in range(count)])  23.2 us
    unnamed x10, local copies, waits for them, and re-layouts  2.57 us
  transfers between devices with their start and end apart: 26, of which 8 were waited for; matrix products, arithmetic and copies ran while one was open for 0% of the time, Pallas kernels for 15%

profile of v3, /device:TPU:0, one launch (start us, length us, event | category | flops | bytes accessed | tf_op | source)
XLA Modules:
  0.0 93.0 jit_solution(5622072684234104617)
XLA Ops:
  0.7 0.0 copy-start.3
  0.7 0.0 copy-start.4
  0.7 0.7 copy-done.3
  1.3 0.0 copy-done.4
  1.3 1.0 %copy-done.1 = bf16[2,256,384]{2,1,0:T(8,128)(2,1)S(1)} copy-done((bf16[2,256,384]{2,1,0:T(8,128)(2,1)S(1)}, bf16[2,256,384]{2,1,0:T(8,128)(2,1)}, u32[]{:S(2)}) %copy-start.1) | copy-done | bytes 393240
  2.3 0.9 copy-done.2
  3.2 7.9 %shard_map.64 = (f32[4,2,128,128]{3,2,1,0:T(8,128)S(1)}, f32[4,2,128,128]{3,2,1,0:T(8,128)S(1)}, bf16[2,272,128]{2,1,0:T(8,128)(2,1)S(1)}) custom-call(s32[1]{0:T(128)} %bitcast.ids_ref, s32[2]{0:T(128)S(1)} %copy-done.4, s32[1]{0:T(128)S(6)} %copy.7.refs_1_, bf16[2,256,128]{2,1,0:T(8,128)(2,1)S(1)} %copy-done.2, bf16[2,256,384]{2,1,0:T(8,128)(2,1)S(1)} %copy-done.1, ...), custom_call_target="tpu_custom_call" | custom-call | tf_op jit(solution)/shard_map/pallas_call | solution.py:319
  11.1 0.5 collective-permute-start
  11.7 1.5 %collective-permute-done.b_ref = f32[4,2,128,128]{3,2,1,0:T(8,128)S(1)} collective-permute-done((f32[4,2,128,128]{3,2,1,0:T(8,128)S(1)}, f32[4,2,128,128]{3,2,1,0:T(8,128)S(1)}, u32[]{:S(2)}, u32[]{:S(2)}) %collective-permute-start) | collective-permute-done | bytes 524320 | tf_op jit(solution)/shard_map/ppermute | solution.py:334
  13.2 0.1 shard_map.65
  13.3 3.0 %collective-permute-start.1 = (f32[2,128,128]{2,1,0:T(8,128)S(1)}, f32[2,128,128]{2,1,0:T(8,128)S(1)}, u32[]{:S(2)}, u32[]{:S(2)}) collective-permute-start(f32[2,128,128]{2,1,0:T(8,128)S(1)} %get-tuple-element.25), channel_id=1, source_target_pairs={{0,8},{1,9},{2,10},{3,11},{4,12},{5,13},{6,14},{7,15},{8,0},{9,1},... | collective-permute-start | bytes 393224 | tf_op jit(solution)/shard_map/ppermute | solution.py:334
  16.2 1.5 %collective-permute-start.2 = (f32[2,128,128]{2,1,0:T(8,128)S(1)}, f32[2,128,128]{2,1,0:T(8,128)S(1)}, u32[]{:S(2)}, u32[]{:S(2)}) collective-permute-start(f32[2,128,128]{2,1,0:T(8,128)S(1)} %get-tuple-element.26), channel_id=1, source_target_pairs={{0,16},{1,17},{2,18},{3,19},{4,20},{5,21},{6,22},{7,23},{8,24},{9,... | collective-permute-start | bytes 393224 | tf_op jit(solution)/shard_map/ppermute | solution.py:334
  17.7 0.1 collective-permute-start.3
  17.8 2.3 %collective-permute-done.1 = f32[2,128,128]{2,1,0:T(8,128)S(1)} collective-permute-done((f32[2,128,128]{2,1,0:T(8,128)S(1)}, f32[2,128,128]{2,1,0:T(8,128)S(1)}, u32[]{:S(2)}, u32[]{:S(2)}) %collective-permute-start.1) | collective-permute-done | bytes 131104 | tf_op jit(solution)/shard_map/ppermute | solution.py:334
  20.0 2.6 %collective-permute-done.2 = f32[2,128,128]{2,1,0:T(8,128)S(1)} collective-permute-done((f32[2,128,128]{2,1,0:T(8,128)S(1)}, f32[2,128,128]{2,1,0:T(8,128)S(1)}, u32[]{:S(2)}, u32[]{:S(2)}) %collective-permute-start.2) | collective-permute-done | bytes 131104 | tf_op jit(solution)/shard_map/ppermute | solution.py:334
  22.6 1.5 %collective-permute-done.3 = f32[2,128,128]{2,1,0:T(8,128)S(1)} collective-permute-done((f32[2,128,128]{2,1,0:T(8,128)S(1)}, f32[2,128,128]{2,1,0:T(8,128)S(1)}, u32[]{:S(2)}, u32[]{:S(2)}) %collective-permute-start.3) | collective-permute-done | bytes 131104 | tf_op jit(solution)/shard_map/ppermute | solution.py:334
  24.1 3.8 %collective-permute-start.6 = (f32[2,128,128]{2,1,0:T(8,128)S(1)}, f32[2,128,128]{2,1,0:T(8,128)S(1)}, u32[]{:S(2)}, u32[]{:S(2)}) collective-permute-start(f32[2,128,128]{2,1,0:T(8,128)S(1)} %add_add_fusion.1), channel_id=1, source_target_pairs={{0,3},{1,2},{2,1},{3,0},{4,7},{5,6},{6,5},{7,4},{8,11},{9,10},{10,... | collective-permute-start | bytes 393224 | tf_op jit(solution)/shard_map/ppermute | solution.py:334
  27.9 0.0 collective-permute-start.5
  27.9 0.6 collective-permute-start.4
  28.6 0.7 collective-permute-start.15
  29.2 3.2 %collective-permute-done.6 = f32[2,128,128]{2,1,0:T(8,128)S(1)} collective-permute-done((f32[2,128,128]{2,1,0:T(8,128)S(1)}, f32[2,128,128]{2,1,0:T(8,128)S(1)}, u32[]{:S(2)}, u32[]{:S(2)}) %collective-permute-start.6) | collective-permute-done | bytes 131104 | tf_op jit(solution)/shard_map/ppermute | solution.py:334
  32.4 6.1 %collective-permute-done.5 = f32[2,128,128]{2,1,0:T(8,128)S(1)} collective-permute-done((f32[2,128,128]{2,1,0:T(8,128)S(1)}, f32[2,128,128]{2,1,0:T(8,128)S(1)}, u32[]{:S(2)}, u32[]{:S(2)}) %collective-permute-start.5) | collective-permute-done | bytes 131104 | tf_op jit(solution)/shard_map/ppermute | solution.py:334
  38.5 0.0 collective-permute-done.4
  38.5 2.2 %collective-permute-start.12 = (f32[2,128,128]{2,1,0:T(8,128)S(1)}, f32[2,128,128]{2,1,0:T(8,128)S(1)}, u32[]{:S(2)}, u32[]{:S(2)}) collective-permute-start(f32[2,128,128]{2,1,0:T(8,128)S(1)} %add_add_fusion.refs_0_), channel_id=1, source_target_pairs={{0,24},{1,25},{2,26},{3,27},{4,28},{5,29},{6,30},{7,31},{8,16},{9,... | collective-permute-start | bytes 393224 | tf_op jit(solution)/shard_map/ppermute | solution.py:334
  40.7 4.5 %collective-permute-start.10 = (f32[2,128,128]{2,1,0:T(8,128)S(1)}, f32[2,128,128]{2,1,0:T(8,128)S(1)}, u32[]{:S(2)}, u32[]{:S(2)}) collective-permute-start(f32[2,128,128]{2,1,0:T(8,128)S(1)} %add_add_fusion.refs_0_), channel_id=1, source_target_pairs={{0,16},{1,17},{2,18},{3,19},{4,20},{5,21},{6,22},{7,23},{8,24},{9,... | collective-permute-start | bytes 393224 | tf_op jit(solution)/shard_map/ppermute | solution.py:334
  45.2 0.0 collective-permute-start.8
  45.2 0.8 collective-permute-start.14
  46.1 0.0 collective-permute-done.15.refs_11_
  46.1 1.6 %collective-permute-start.7 = (f32[2,128,128]{2,1,0:T(8,128)S(1)}, f32[2,128,128]{2,1,0:T(8,128)S(1)}, u32[]{:S(2)}, u32[]{:S(2)}) collective-permute-start(f32[2,128,128]{2,1,0:T(8,128)S(1)} %add_add_fusion.refs_0_), channel_id=1, source_target_pairs={{0,4},{1,5},{2,6},{3,7},{4,0},{5,1},{6,2},{7,3},{8,12},{9,13},{10,... | collective-permute-start | bytes 393224 | tf_op jit(solution)/shard_map/ppermute | solution.py:334
  47.7 0.0 collective-permute-done.12.refs_6_
  47.7 0.1 collective-permute-start.13
  47.7 3.0 %collective-permute-done.10.refs_4_ = f32[2,128,128]{2,1,0:T(8,128)S(1)} collective-permute-done((f32[2,128,128]{2,1,0:T(8,128)S(1)}, f32[2,128,128]{2,1,0:T(8,128)S(1)}, u32[]{:S(2)}, u32[]{:S(2)}) %collective-permute-start.10) | collective-permute-done | bytes 131104 | tf_op jit(solution)/shard_map/ppermute | solution.py:334
  50.7 0.0 collective-permute-start.11
  50.7 0.0 collective-permute-done.8.refs_2_
  50.7 0.5 collective-permute-start.9
  51.2 0.0 collective-permute-done.14.refs_3_
  51.2 5.7 %collective-permute-start.18 = (bf16[2,272,128]{2,1,0:T(8,128)(2,1)S(1)}, bf16[2,272,128]{2,1,0:T(8,128)(2,1)S(1)}, u32[]{:S(2)}, u32[]{:S(2)}) collective-permute-start(bf16[2,272,128]{2,1,0:T(8,128)(2,1)S(1)} %collective-permute-done.14.refs_3_), channel_id=1, source_target_pairs={{0,24},{1,25},{2,26},{3,27},{4,28},{5,29},{6,30},{7,31},{8,16},{9,... | collective-permute-start | bytes 417800 | tf_op jit(solution)/shard_map/ppermute | solution.py:334
  56.9 0.0 collective-permute-done.7.refs_1_
  56.9 1.6 %collective-permute-start.17 = (bf16[2,272,128]{2,1,0:T(8,128)(2,1)S(1)}, bf16[2,272,128]{2,1,0:T(8,128)(2,1)S(1)}, u32[]{:S(2)}, u32[]{:S(2)}) collective-permute-start(bf16[2,272,128]{2,1,0:T(8,128)(2,1)S(1)} %collective-permute-done.14.refs_3_), channel_id=1, source_target_pairs={{0,16},{1,17},{2,18},{3,19},{4,20},{5,21},{6,22},{7,23},{8,24},{9,... | collective-permute-start | bytes 417800 | tf_op jit(solution)/shard_map/ppermute | solution.py:334
  58.5 0.0 collective-permute-done.13.refs_7_
  58.6 0.0 collective-permute-start.16
  58.6 0.0 collective-permute-done.11.refs_5_
  58.6 3.5 %collective-permute-start.25 = (bf16[2,272,128]{2,1,0:T(8,128)(2,1)S(1)}, bf16[2,272,128]{2,1,0:T(8,128)(2,1)S(1)}, u32[]{:S(2)}, u32[]{:S(2)}) collective-permute-start(bf16[2,272,128]{2,1,0:T(8,128)(2,1)S(1)} %collective-permute-done.15.refs_11_), channel_id=1, source_target_pairs={{0,3},{1,2},{2,1},{3,0},{4,7},{5,6},{6,5},{7,4},{8,11},{9,10},{10,... | collective-permute-start | bytes 417800 | tf_op jit(solution)/shard_map/ppermute | solution.py:334
  62.1 0.0 collective-permute-done.9.refs_3_
  62.1 0.0 collective-permute-start.24
  62.1 0.1 pad_add_fusion.key_ref
  62.2 14.0 %shard_map.66 = (f32[6,128,128]{2,1,0:T(8,128)S(1)}, f32[10,128,128]{2,1,0:T(8,128)S(1)}, f32[3,128,128]{2,1,0:T(8,128)S(1)}) custom-call(s32[3]{0:T(128)S(1)} %pad_add_fusion.key_ref, f32[2,128,128]{2,1,0:T(8,128)S(1)} %add_add_fusion.refs_0_, f32[2,128,128]{2,1,0:T(8,128)S(1)} %collective-permute-done.7.refs_1_, ...), custom_call_target="tpu_custom_call" | custom-call | tf_op jit(solution)/shard_map/pallas_call | solution.py:319
  76.1 0.0 collective-permute-done.18.refs_9_
  76.1 1.0 %collective-permute-start.23 = (bf16[2,272,128]{2,1,0:T(8,128)(2,1)S(1)}, bf16[2,272,128]{2,1,0:T(8,128)(2,1)S(1)}, u32[]{:S(2)}, u32[]{:S(2)}) collective-permute-start(bf16[2,272,128]{2,1,0:T(8,128)(2,1)S(1)} %collective-permute-done.15.refs_11_), channel_id=1, source_target_pairs={{0,1},{1,0},{2,3},{3,2},{4,5},{5,4},{6,7},{7,6},{8,9},{9,8},{10,11... | collective-permute-start | bytes 417800 | tf_op jit(solution)/shard_map/ppermute | solution.py:334
  77.1 0.0 collective-permute-done.17.refs_7_
  77.1 0.0 collective-permute-done.16.refs_5_
  77.1 0.0 collective-permute-start.19
  77.1 0.5 collective-permute-start.20
  77.7 0.0 collective-permute-done.25.refs_14_
  77.7 0.1 collective-permute-start.21
  77.7 0.0 collective-permute-done.24.refs_13_
  77.7 0.4 collective-permute-start.22
  78.2 3.1 %collective-permute-done.23.refs_12_ = bf16[2,272,128]{2,1,0:T(8,128)(2,1)S(1)} collective-permute-done((bf16[2,272,128]{2,1,0:T(8,128)(2,1)S(1)}, bf16[2,272,128]{2,1,0:T(8,128)(2,1)S(1)}, u32[]{:S(2)}, u32[]{:S(2)}) %collective-permute-start.23) | collective-permute-done | bytes 139296 | tf_op jit(solution)/shard_map/ppermute | solution.py:334
  81.3 0.0 collective-permute-done.19.refs_4_
  81.3 0.0 collective-permute-done.20.refs_6_
  81.3 0.0 collective-permute-done.21.refs_8_
  81.3 0.0 collective-permute-done.22.refs_10_
  81.3 0.0 copy-done
  81.3 11.7 %shard_map.67 = f32[256,512]{1,0:T(8,128)} custom-call(s32[3]{0:T(128)S(1)} %pad_add_fusion.key_ref, f32[6,128,128]{2,1,0:T(8,128)S(1)} %get-tuple-element.28.refs_0_, f32[10,128,128]{2,1,0:T(8,128)S(1)} %get-tuple-element.29.refs_1_, f32[3,128,128]{2,1,0:T(8,128)S(1)} %get-tuple-element.30.refs_2_, ...), custom_call_target="tpu_custom_call" | custom-call | tf_op jit(solution)/shard_map/pallas_call | solution.py:319
  (5 shorter events, 0.1 us)
Async XLA Ops:
  0.7 0.7 copy-start.3
  0.7 0.7 copy-start.4
  1.3 1.0 %copy-start.1 = (bf16[2,256,384]{2,1,0:T(8,128)(2,1)S(1)}, bf16[2,256,384]{2,1,0:T(8,128)(2,1)}, u32[]{:S(2)}) copy-start(bf16[2,256,384]{2,1,0:T(8,128)(2,1)} %refs_3_.1) | copy-start | bytes 1179652
  2.3 0.9 copy-start.2
  11.1 2.1 %collective-permute-start = (f32[4,2,128,128]{3,2,1,0:T(8,128)S(1)}, f32[4,2,128,128]{3,2,1,0:T(8,128)S(1)}, u32[]{:S(2)}, u32[]{:S(2)}) collective-permute-start(f32[4,2,128,128]{3,2,1,0:T(8,128)S(1)} %get-tuple-element.23), channel_id=1, source_target_pairs={{0,4},{1,5},{2,6},{3,7},{4,0},{5,1},{6,2},{7,3},{8,12},{9,13},{10,... | collective-permute-start | bytes 1572872 | tf_op jit(solution)/shard_map/ppermute | solution.py:334
  13.3 6.8 %collective-permute-start.1 = (f32[2,128,128]{2,1,0:T(8,128)S(1)}, f32[2,128,128]{2,1,0:T(8,128)S(1)}, u32[]{:S(2)}, u32[]{:S(2)}) collective-permute-start(f32[2,128,128]{2,1,0:T(8,128)S(1)} %get-tuple-element.25), channel_id=1, source_target_pairs={{0,8},{1,9},{2,10},{3,11},{4,12},{5,13},{6,14},{7,15},{8,0},{9,1},... | collective-permute-start | bytes 393224 | tf_op jit(solution)/shard_map/ppermute | solution.py:334
  16.2 6.4 %collective-permute-start.2 = (f32[2,128,128]{2,1,0:T(8,128)S(1)}, f32[2,128,128]{2,1,0:T(8,128)S(1)}, u32[]{:S(2)}, u32[]{:S(2)}) collective-permute-start(f32[2,128,128]{2,1,0:T(8,128)S(1)} %get-tuple-element.26), channel_id=1, source_target_pairs={{0,16},{1,17},{2,18},{3,19},{4,20},{5,21},{6,22},{7,23},{8,24},{9,... | collective-permute-start | bytes 393224 | tf_op jit(solution)/shard_map/ppermute | solution.py:334
  17.7 6.4 %collective-permute-start.3 = (f32[2,128,128]{2,1,0:T(8,128)S(1)}, f32[2,128,128]{2,1,0:T(8,128)S(1)}, u32[]{:S(2)}, u32[]{:S(2)}) collective-permute-start(f32[2,128,128]{2,1,0:T(8,128)S(1)} %get-tuple-element.27), channel_id=1, source_target_pairs={{0,24},{1,25},{2,26},{3,27},{4,28},{5,29},{6,30},{7,31},{8,16},{9,... | collective-permute-start | bytes 393224 | tf_op jit(solution)/shard_map/ppermute | solution.py:334
  24.1 8.3 %collective-permute-start.6 = (f32[2,128,128]{2,1,0:T(8,128)S(1)}, f32[2,128,128]{2,1,0:T(8,128)S(1)}, u32[]{:S(2)}, u32[]{:S(2)}) collective-permute-start(f32[2,128,128]{2,1,0:T(8,128)S(1)} %add_add_fusion.1), channel_id=1, source_target_pairs={{0,3},{1,2},{2,1},{3,0},{4,7},{5,6},{6,5},{7,4},{8,11},{9,10},{10,... | collective-permute-start | bytes 393224 | tf_op jit(solution)/shard_map/ppermute | solution.py:334
  27.9 10.6 %collective-permute-start.5 = (f32[2,128,128]{2,1,0:T(8,128)S(1)}, f32[2,128,128]{2,1,0:T(8,128)S(1)}, u32[]{:S(2)}, u32[]{:S(2)}) collective-permute-start(f32[2,128,128]{2,1,0:T(8,128)S(1)} %add_add_fusion.1), channel_id=1, source_target_pairs={{0,2},{1,3},{2,0},{3,1},{4,6},{5,7},{6,4},{7,5},{8,10},{9,11},{10,... | collective-permute-start | bytes 393224 | tf_op jit(solution)/shard_map/ppermute | solution.py:334
  27.9 10.6 %collective-permute-start.4 = (f32[2,128,128]{2,1,0:T(8,128)S(1)}, f32[2,128,128]{2,1,0:T(8,128)S(1)}, u32[]{:S(2)}, u32[]{:S(2)}) collective-permute-start(f32[2,128,128]{2,1,0:T(8,128)S(1)} %add_add_fusion.1), channel_id=1, source_target_pairs={{0,1},{1,0},{2,3},{3,2},{4,5},{5,4},{6,7},{7,6},{8,9},{9,8},{10,11... | collective-permute-start | bytes 393224 | tf_op jit(solution)/shard_map/ppermute | solution.py:334
  28.6 17.5 %collective-permute-start.15 = (bf16[2,272,128]{2,1,0:T(8,128)(2,1)S(1)}, bf16[2,272,128]{2,1,0:T(8,128)(2,1)S(1)}, u32[]{:S(2)}, u32[]{:S(2)}) collective-permute-start(bf16[2,272,128]{2,1,0:T(8,128)(2,1)S(1)} %get-tuple-element.32), channel_id=1, source_target_pairs={{0,0},{1,1},{16,2},{17,3},{18,4},{19,5},{2,6},{3,7},{4,8},{5,9},{2... | collective-permute-start | bytes 417800 | tf_op jit(solution)/shard_map/ppermute | solution.py:379
  38.5 9.1 %collective-permute-start.12 = (f32[2,128,128]{2,1,0:T(8,128)S(1)}, f32[2,128,128]{2,1,0:T(8,128)S(1)}, u32[]{:S(2)}, u32[]{:S(2)}) collective-permute-start(f32[2,128,128]{2,1,0:T(8,128)S(1)} %add_add_fusion.refs_0_), channel_id=1, source_target_pairs={{0,24},{1,25},{2,26},{3,27},{4,28},{5,29},{6,30},{7,31},{8,16},{9,... | collective-permute-start | bytes 393224 | tf_op jit(solution)/shard_map/ppermute | solution.py:334
  40.7 10.0 %collective-permute-start.10 = (f32[2,128,128]{2,1,0:T(8,128)S(1)}, f32[2,128,128]{2,1,0:T(8,128)S(1)}, u32[]{:S(2)}, u32[]{:S(2)}) collective-permute-start(f32[2,128,128]{2,1,0:T(8,128)S(1)} %add_add_fusion.refs_0_), channel_id=1, source_target_pairs={{0,16},{1,17},{2,18},{3,19},{4,20},{5,21},{6,22},{7,23},{8,24},{9,... | collective-permute-start | bytes 393224 | tf_op jit(solution)/shard_map/ppermute | solution.py:334
  45.2 5.5 %collective-permute-start.8 = (f32[2,128,128]{2,1,0:T(8,128)S(1)}, f32[2,128,128]{2,1,0:T(8,128)S(1)}, u32[]{:S(2)}, u32[]{:S(2)}) collective-permute-start(f32[2,128,128]{2,1,0:T(8,128)S(1)} %add_add_fusion.refs_0_), channel_id=1, source_target_pairs={{0,8},{1,9},{2,10},{3,11},{4,12},{5,13},{6,14},{7,15},{8,0},{9,1},... | collective-permute-start | bytes 393224 | tf_op jit(solution)/shard_map/ppermute | solution.py:334
  45.2 6.0 %collective-permute-start.14 = (bf16[2,272,128]{2,1,0:T(8,128)(2,1)S(1)}, bf16[2,272,128]{2,1,0:T(8,128)(2,1)S(1)}, u32[]{:S(2)}, u32[]{:S(2)}) collective-permute-start(bf16[2,272,128]{2,1,0:T(8,128)(2,1)S(1)} %get-tuple-element.32), channel_id=1, source_target_pairs={{0,0},{4,1},{8,2},{12,3},{1,4},{5,5},{9,6},{13,7},{2,8},{6,9},{10,... | collective-permute-start | bytes 417800 | tf_op jit(solution)/shard_map/ppermute | solution.py:378
  46.1 10.8 %collective-permute-start.7 = (f32[2,128,128]{2,1,0:T(8,128)S(1)}, f32[2,128,128]{2,1,0:T(8,128)S(1)}, u32[]{:S(2)}, u32[]{:S(2)}) collective-permute-start(f32[2,128,128]{2,1,0:T(8,128)S(1)} %add_add_fusion.refs_0_), channel_id=1, source_target_pairs={{0,4},{1,5},{2,6},{3,7},{4,0},{5,1},{6,2},{7,3},{8,12},{9,13},{10,... | collective-permute-start | bytes 393224 | tf_op jit(solution)/shard_map/ppermute | solution.py:334
  47.7 10.9 %collective-permute-start.13 = (f32[2,128,128]{2,1,0:T(8,128)S(1)}, f32[2,128,128]{2,1,0:T(8,128)S(1)}, u32[]{:S(2)}, u32[]{:S(2)}) collective-permute-start(f32[2,128,128]{2,1,0:T(8,128)S(1)} %collective-permute-done.12.refs_6_), channel_id=1, source_target_pairs={{0,4},{1,5},{2,6},{3,7},{4,0},{5,1},{6,2},{7,3},{8,12},{9,13},{10,... | collective-permute-start | bytes 393224 | tf_op jit(solution)/shard_map/ppermute | solution.py:334
  50.7 7.8 %collective-permute-start.11 = (f32[2,128,128]{2,1,0:T(8,128)S(1)}, f32[2,128,128]{2,1,0:T(8,128)S(1)}, u32[]{:S(2)}, u32[]{:S(2)}) collective-permute-start(f32[2,128,128]{2,1,0:T(8,128)S(1)} %collective-permute-done.10.refs_4_), channel_id=1, source_target_pairs={{0,4},{1,5},{2,6},{3,7},{4,0},{5,1},{6,2},{7,3},{8,12},{9,13},{10,... | collective-permute-start | bytes 393224 | tf_op jit(solution)/shard_map/ppermute | solution.py:334
  50.7 11.4 %collective-permute-start.9 = (f32[2,128,128]{2,1,0:T(8,128)S(1)}, f32[2,128,128]{2,1,0:T(8,128)S(1)}, u32[]{:S(2)}, u32[]{:S(2)}) collective-permute-start(f32[2,128,128]{2,1,0:T(8,128)S(1)} %collective-permute-done.8.refs_2_), channel_id=1, source_target_pairs={{0,4},{1,5},{2,6},{3,7},{4,0},{5,1},{6,2},{7,3},{8,12},{9,13},{10,... | collective-permute-start | bytes 393224 | tf_op jit(solution)/shard_map/ppermute | solution.py:334
  51.2 24.9 %collective-permute-start.18 = (bf16[2,272,128]{2,1,0:T(8,128)(2,1)S(1)}, bf16[2,272,128]{2,1,0:T(8,128)(2,1)S(1)}, u32[]{:S(2)}, u32[]{:S(2)}) collective-permute-start(bf16[2,272,128]{2,1,0:T(8,128)(2,1)S(1)} %collective-permute-done.14.refs_3_), channel_id=1, source_target_pairs={{0,24},{1,25},{2,26},{3,27},{4,28},{5,29},{6,30},{7,31},{8,16},{9,... | collective-permute-start | bytes 417800 | tf_op jit(solution)/shard_map/ppermute | solution.py:334
  56.9 20.2 %collective-permute-start.17 = (bf16[2,272,128]{2,1,0:T(8,128)(2,1)S(1)}, bf16[2,272,128]{2,1,0:T(8,128)(2,1)S(1)}, u32[]{:S(2)}, u32[]{:S(2)}) collective-permute-start(bf16[2,272,128]{2,1,0:T(8,128)(2,1)S(1)} %collective-permute-done.14.refs_3_), channel_id=1, source_target_pairs={{0,16},{1,17},{2,18},{3,19},{4,20},{5,21},{6,22},{7,23},{8,24},{9,... | collective-permute-start | bytes 417800 | tf_op jit(solution)/shard_map/ppermute | solution.py:334
  58.6 18.6 %collective-permute-start.16 = (bf16[2,272,128]{2,1,0:T(8,128)(2,1)S(1)}, bf16[2,272,128]{2,1,0:T(8,128)(2,1)S(1)}, u32[]{:S(2)}, u32[]{:S(2)}) collective-permute-start(bf16[2,272,128]{2,1,0:T(8,128)(2,1)S(1)} %collective-permute-done.14.refs_3_), channel_id=1, source_target_pairs={{0,8},{1,9},{2,10},{3,11},{4,12},{5,13},{6,14},{7,15},{8,0},{9,1},... | collective-permute-start | bytes 417800 | tf_op jit(solution)/shard_map/ppermute | solution.py:334
  58.6 19.1 %collective-permute-start.25 = (bf16[2,272,128]{2,1,0:T(8,128)(2,1)S(1)}, bf16[2,272,128]{2,1,0:T(8,128)(2,1)S(1)}, u32[]{:S(2)}, u32[]{:S(2)}) collective-permute-start(bf16[2,272,128]{2,1,0:T(8,128)(2,1)S(1)} %collective-permute-done.15.refs_11_), channel_id=1, source_target_pairs={{0,3},{1,2},{2,1},{3,0},{4,7},{5,6},{6,5},{7,4},{8,11},{9,10},{10,... | collective-permute-start | bytes 417800 | tf_op jit(solution)/shard_map/ppermute | solution.py:334
  62.1 15.6 %collective-permute-start.24 = (bf16[2,272,128]{2,1,0:T(8,128)(2,1)S(1)}, bf16[2,272,128]{2,1,0:T(8,128)(2,1)S(1)}, u32[]{:S(2)}, u32[]{:S(2)}) collective-permute-start(bf16[2,272,128]{2,1,0:T(8,128)(2,1)S(1)} %collective-permute-done.15.refs_11_), channel_id=1, source_target_pairs={{0,2},{1,3},{2,0},{3,1},{4,6},{5,7},{6,4},{7,5},{8,10},{9,11},{10,... | collective-permute-start | bytes 417800 | tf_op jit(solution)/shard_map/ppermute | solution.py:334
  62.2 19.1 %copy-start = (f32[256,512]{1,0:T(8,128)S(1)}, f32[256,512]{1,0:T(8,128)}, u32[]{:S(2)}) copy-start(f32[256,512]{1,0:T(8,128)} %refs_15_.1) | copy-start | bytes 1572868
  76.1 5.1 %collective-permute-start.23 = (bf16[2,272,128]{2,1,0:T(8,128)(2,1)S(1)}, bf16[2,272,128]{2,1,0:T(8,128)(2,1)S(1)}, u32[]{:S(2)}, u32[]{:S(2)}) collective-permute-start(bf16[2,272,128]{2,1,0:T(8,128)(2,1)S(1)} %collective-permute-done.15.refs_11_), channel_id=1, source_target_pairs={{0,1},{1,0},{2,3},{3,2},{4,5},{5,4},{6,7},{7,6},{8,9},{9,8},{10,11... | collective-permute-start | bytes 417800 | tf_op jit(solution)/shard_map/ppermute | solution.py:334
  77.1 4.1 %collective-permute-start.19 = (bf16[2,272,128]{2,1,0:T(8,128)(2,1)S(1)}, bf16[2,272,128]{2,1,0:T(8,128)(2,1)S(1)}, u32[]{:S(2)}, u32[]{:S(2)}) collective-permute-start(bf16[2,272,128]{2,1,0:T(8,128)(2,1)S(1)} %collective-permute-done.14.refs_3_), channel_id=1, source_target_pairs={{0,4},{1,5},{2,6},{3,7},{4,0},{5,1},{6,2},{7,3},{8,12},{9,13},{10,... | collective-permute-start | bytes 417800 | tf_op jit(solution)/shard_map/ppermute | solution.py:334
  77.1 4.1 %collective-permute-start.20 = (bf16[2,272,128]{2,1,0:T(8,128)(2,1)S(1)}, bf16[2,272,128]{2,1,0:T(8,128)(2,1)S(1)}, u32[]{:S(2)}, u32[]{:S(2)}) collective-permute-start(bf16[2,272,128]{2,1,0:T(8,128)(2,1)S(1)} %collective-permute-done.16.refs_5_), channel_id=1, source_target_pairs={{0,4},{1,5},{2,6},{3,7},{4,0},{5,1},{6,2},{7,3},{8,12},{9,13},{10,... | collective-permute-start | bytes 417800 | tf_op jit(solution)/shard_map/ppermute | solution.py:334
  77.7 3.6 %collective-permute-start.21 = (bf16[2,272,128]{2,1,0:T(8,128)(2,1)S(1)}, bf16[2,272,128]{2,1,0:T(8,128)(2,1)S(1)}, u32[]{:S(2)}, u32[]{:S(2)}) collective-permute-start(bf16[2,272,128]{2,1,0:T(8,128)(2,1)S(1)} %collective-permute-done.17.refs_7_), channel_id=1, source_target_pairs={{0,4},{1,5},{2,6},{3,7},{4,0},{5,1},{6,2},{7,3},{8,12},{9,13},{10,... | collective-permute-start | bytes 417800 | tf_op jit(solution)/shard_map/ppermute | solution.py:334
  77.7 3.6 %collective-permute-start.22 = (bf16[2,272,128]{2,1,0:T(8,128)(2,1)S(1)}, bf16[2,272,128]{2,1,0:T(8,128)(2,1)S(1)}, u32[]{:S(2)}, u32[]{:S(2)}) collective-permute-start(bf16[2,272,128]{2,1,0:T(8,128)(2,1)S(1)} %collective-permute-done.18.refs_9_), channel_id=1, source_target_pairs={{0,4},{1,5},{2,6},{3,7},{4,0},{5,1},{6,2},{7,3},{8,12},{9,13},{10,... | collective-permute-start | bytes 417800 | tf_op jit(solution)/shard_map/ppermute | solution.py:334

commit v4 on v3

--- a/solution.py
+++ b/solution.py
@@ -13,7 +13,9 @@
 BF16 = jnp.bfloat16
 SUB = 8
 TAIL = 16
-EARLY = 2
+CUT = 3
+FLOPS_PER_MICRO = 10**9
+BYTES_PER_MICRO = 3 * 10**6
 VMEM_BYTES = 40 * 1024 * 1024
 
 ROWS_BY_ROWS = (((0,), (0,)), ((), ()))
@@ -202,8 +204,9 @@
     return levels
 
 
-def eliminate(level, diag, off, work):
-    inverses = inverse_factors([diag[k] for k, _, _ in level], work)
+def eliminate(level, diag, off, work=(), inverses=None):
+    if inverses is None:
+        inverses = inverse_factors([diag[k] for k, _, _ in level], work)
     lows = {}
     for (k, before, after), inv in zip(level, inverses):
         if before is not None:
@@ -219,15 +222,22 @@
     return {k: inv for (k, _, _), inv in zip(level, inverses)}, lows
 
 
-def early_layout():
+def layout():
     levels = levels_of(PBLK)
-    early, late = levels[:EARLY], levels[EARLY:]
-    invs = [k for level in early for k, _, _ in level]
+    invs = [k for level in levels[:CUT] for k, _, _ in level]
     lows = [
-        (k, n) for level in early for k, before, after in level for n in (before, after) if n is not None
+        (k, n) for level in levels[:CUT] for k, before, after in level for n in (before, after) if n is not None
     ]
-    left = sorted(k for level in late for k, _, _ in level)
+    left = sorted(k for level in levels[CUT:] for k, _, _ in level)
     return invs, lows, left, list(zip(left[1:], left[:-1]))
+
+
+def own_kernel(me, *refs):
+    *parts, out_ref = refs
+    diag = tree_sum([part[0] for part in parts])
+    out_ref[1] = tree_sum([part[1] for part in parts])
+    inverse = inverse_factors([diag])[0]
+    out_ref[0] = jnp.where(lax.rem(me, 2) == 0, inverse, diag)
 
 
 def factor_kernel(me, *refs):
@@ -237,9 +247,11 @@
         tri[lax.bitwise_xor(me, j)] = pieces[j][...]
     diag = {k: tri[k, 0] for k in range(PBLK)}
     off = {(k, k - 1): tri[k, 1] for k in range(1, PBLK)}
-    invs, lows, left, links = early_layout()
-    for level in levels_of(PBLK)[:EARLY]:
-        new_invs, new_lows = eliminate(level, diag, off, ())
+    invs, lows, left, links = layout()
+    levels = levels_of(PBLK)[:CUT]
+    given = [diag[k] for k, _, _ in levels[0]]
+    for level, inverses in zip(levels, [given] + [None] * (CUT - 1)):
+        new_invs, new_lows = eliminate(level, diag, off, inverses=inverses)
         for k, value in new_invs.items():
             inv_ref[invs.index(k)] = value
         for key, value in new_lows.items():
@@ -250,7 +262,8 @@
         left_ref[len(left) + i] = off[key]
 
 
-def panel_kernel(cols_me, rows_me, n_row, per, n_cols, inv_ref, low_ref, left_ref, *refs):
+def panel_kernel(cols_me, rows_me, n_row, per, n_cols, *refs):
+    (inv_ref, low_ref, left_ref), refs = refs[:3], refs[3:]
     terms, (trail_ref, out_ref, panel, solved) = refs[:-4], refs[-4:]
     slots, height, block = terms[0].shape
     height = height - TAIL
@@ -289,16 +302,16 @@
         return items
 
     panel[...] = jnp.zeros_like(panel)
-    invs, lows, left, links = early_layout()
+    levels = levels_of(PBLK)
+    work = [functools.partial(place, n, b) for n in range(len(terms)) for b in range(slots)]
+    invs, lows, left, links = layout()
     early_invs = {k: inv_ref.at[i] for i, k in enumerate(invs)}
     early_lows = {key: low_ref.at[i] for i, key in enumerate(lows)}
+    for level in levels[:CUT]:
+        work += solve_level(level, early_invs, early_lows)
     diag = {k: left_ref[i] for i, k in enumerate(left)}
     off = {key: left_ref[len(left) + i] for i, key in enumerate(links)}
-    levels = levels_of(PBLK)
-    work = [functools.partial(place, n, b) for n in range(len(terms)) for b in range(slots)]
-    for level in levels[:EARLY]:
-        work += solve_level(level, early_invs, early_lows)
-    for level in levels[EARLY:]:
+    for level in levels[CUT:]:
         new_invs, new_lows = eliminate(level, diag, off, work)
         work = solve_level(level, new_invs, new_lows)
     for item in work:
@@ -315,7 +328,7 @@
 PARAMS = pltpu.CompilerParams(vmem_limit_bytes=VMEM_BYTES)
 
 
-def call(kernel, out_shape, ins, scratch=(), scalars=0, hbm=()):
+def call(kernel, out_shape, ins, scratch=(), scalars=0, hbm=(), micros=1):
     return pl.pallas_call(
         kernel,
         out_shape=out_shape,
@@ -323,6 +336,9 @@
         out_specs=jax.tree.map(lambda _: VMEM, out_shape),
         scratch_shapes=scratch,
         compiler_params=PARAMS,
+        cost_estimate=pl.CostEstimate(
+            flops=micros * FLOPS_PER_MICRO, bytes_accessed=micros * BYTES_PER_MICRO, transcendentals=0
+        ),
     )(*ins)
 
 
@@ -374,39 +390,50 @@
     ]
     direct = n_col <= 4 and n_rec == low_rec
     got = flipped(send, n_col, count)
-    piece = after(piece, got)
     pcols = lax.ppermute(piece, AXES, to_cols)
-    prows = lax.ppermute(piece, AXES, to_rows)
     pieces = call(add_kernel, [shape((2, block, block), F32)] * half, [keep, got])
     total = sum([flipped(pieces[j], 2 * j * n_col, count) for j in range(1, half)], pieces[0])
+    total, pcols = lax.optimization_barrier((total, pcols))
     for bit in range(1, n_rec // low_rec):
         if bit & (bit - 1) == 0:
             total = total + flipped(total, bit * low_rec * n_row * n_col, count)
     if direct:
-        total = sum([flipped(total, m, count) for m in range(1, n_col)], total)
+        parts = [total] + [flipped(total, m, count) for m in range(1, n_col)]
     else:
-        total = lax.psum(total, "col")
-    evens = [total] + [flipped(total, 2 * j * n_col, count) for j in range(1, half)]
-    pcols, prows = after((pcols, prows), evens)
+        parts = [lax.psum(total, "col")]
+    if direct:
+        pcols = [pcols] + [flipped(pcols, 2 * j * n_col, count) for j in range(1, half)]
+    else:
+        pcols = list(lax.all_gather(pcols, ("rec", "row"), axis=0))
+    pcols, parts, piece = lax.optimization_barrier((pcols, parts, piece))
+    prows = lax.ppermute(piece, AXES, to_rows)
+    own = call(
+        lambda ids_ref, *refs: own_kernel(ids_ref[0], *refs),
+        shape((2, block, block), F32),
+        [ids, *parts],
+        scalars=1,
+        micros=4,
+    )
+    evens = [own] + [flipped(own, 2 * j * n_col, count) for j in range(1, half)]
+    prows = after(prows, evens)
     odds = [flipped(x, n_col, count) for x in evens]
     tri = [x for pair in zip(evens, odds) for x in pair]
     if direct:
-        pcols = [pcols] + [flipped(pcols, 2 * j * n_col, count) for j in range(1, half)]
         prows = [prows] + [flipped(prows, m, count) for m in range(1, n_col)]
         cols_me, rows_me = me, col
     else:
-        pcols = list(lax.all_gather(pcols, ("rec", "row"), axis=0))
         prows = list(lax.all_gather(prows, "col", axis=0))
         cols_me = rows_me = jnp.int32(0)
     wide = trailing_block.shape[0] + trailing_block.shape[1]
     key = jnp.stack([me, cols_me, rows_me]).astype(jnp.int32)
-    invs, lows, left, links = early_layout()
+    invs, lows, left, links = layout()
     early = call(
         lambda key_ref, *refs: factor_kernel(key_ref[0], *refs),
         [shape((n, block, block), F32) for n in (len(invs), len(lows), len(left) + len(links))],
         [key, *tri],
         [pltpu.VMEM((PBLK, 2, block, block), F32)],
         scalars=1,
+        micros=12,
     )
     if direct:
         pcols = after(pcols, early)

time: 93.2 us -> 91.6 us (0.983)
  waiting for transfers between devices: 23.2 us -> 17.3 us
  starting transfers between devices: 32.7 us -> 38.4 us
  Pallas kernels: 33.6 us -> 32.3 us
    ppermute x24, waiting for transfers between devices: 23.2 us -> 17.3 us  [flipped(): return lax.ppermute(x, AXES, [(i, i ^ mask) for i in range(count)])]
    ppermute x24, starting transfers between devices: 31.2 us -> 36.9 us  [flipped(): return lax.ppermute(x, AXES, [(i, i ^ mask) for i in range(count)])]
    pallas_call x4 -> x5, Pallas kernels: 33.6 us -> 32.3 us  [call(): pl.pallas_call(kernel, out_shape=out_shape, in_specs=[SMEM if i < scalars...]
  transfers between devices with their start and end apart: 26 -> 26, of which waited for: 8 -> 14; matrix products, arithmetic and copies ran while one was open for 0% -> 0% of each run, Pallas kernels for 15% -> 13%
where the time goes in v4:
time: 91.6 us; the launch traced here: 91.4 us
  starting transfers between devices  38.4 us (42%)
  Pallas kernels  32.3 us (35%)
  waiting for transfers between devices  17.3 us (19%)
  local copies, waits for them, and re-layouts  2.57 us (3%)
    ppermute x24, starting transfers between devices, flipped(): return lax.ppermute(x, AXES, [(i, i ^ mask) for i in range(count)])  36.9 us
    pallas_call x5, Pallas kernels, call(): pl.pallas_call(kernel, out_shape=out_shape, in_specs=[SMEM if i < scalars...  32.3 us
    ppermute x24, waiting for transfers between devices, flipped(): return lax.ppermute(x, AXES, [(i, i ^ mask) for i in range(count)])  17.3 us
    unnamed x10, local copies, waits for them, and re-layouts  2.57 us
  transfers between devices with their start and end apart: 26, of which 14 were waited for; matrix products, arithmetic and copies ran while one was open for 0% of the time, Pallas kernels for 13%

profile of v4, /device:TPU:0, one launch (start us, length us, event | category | flops | bytes accessed | tf_op | source)
XLA Modules:
  0.0 91.4 jit_solution(15368917884320165839)
XLA Ops:
  0.7 0.0 copy-start.3
  0.7 0.0 copy-start.4
  0.7 0.7 copy-done.3
  1.3 1.0 %copy-done.1 = bf16[2,256,384]{2,1,0:T(8,128)(2,1)S(1)} copy-done((bf16[2,256,384]{2,1,0:T(8,128)(2,1)S(1)}, bf16[2,256,384]{2,1,0:T(8,128)(2,1)}, u32[]{:S(2)}) %copy-start.1) | copy-done | bytes 393240
  2.3 0.9 copy-done.2
  3.2 7.9 %shard_map.64 = (f32[4,2,128,128]{3,2,1,0:T(8,128)S(1)}, f32[4,2,128,128]{3,2,1,0:T(8,128)S(1)}, bf16[2,272,128]{2,1,0:T(8,128)(2,1)S(1)}) custom-call(s32[1]{0:T(128)} %bitcast.ids_ref, s32[2]{0:T(128)S(1)} %copy-done.4, s32[1]{0:T(128)S(6)} %copy.7.refs_1_, bf16[2,256,128]{2,1,0:T(8,128)(2,1)S(1)} %copy-done.2, bf16[2,256,384]{2,1,0:T(8,128)(2,1)S(1)} %copy-done.1, ...), custom_call_target="tpu_custom_call" | custom-call | flops 1000000000 | bytes 3000000 | tf_op jit(solution)/shard_map/pallas_call | solution.py:332
  11.1 0.5 collective-permute-start
  11.7 1.5 %collective-permute-done.b_ref = f32[4,2,128,128]{3,2,1,0:T(8,128)S(1)} collective-permute-done((f32[4,2,128,128]{3,2,1,0:T(8,128)S(1)}, f32[4,2,128,128]{3,2,1,0:T(8,128)S(1)}, u32[]{:S(2)}, u32[]{:S(2)}) %collective-permute-start) | collective-permute-done | bytes 524320 | tf_op jit(solution)/shard_map/ppermute | solution.py:350
  13.2 0.1 shard_map.65
  13.3 3.0 %collective-permute-start.1 = (f32[2,128,128]{2,1,0:T(8,128)S(1)}, f32[2,128,128]{2,1,0:T(8,128)S(1)}, u32[]{:S(2)}, u32[]{:S(2)}) collective-permute-start(f32[2,128,128]{2,1,0:T(8,128)S(1)} %get-tuple-element.34), channel_id=1, source_target_pairs={{0,8},{1,9},{2,10},{3,11},{4,12},{5,13},{6,14},{7,15},{8,0},{9,1},... | collective-permute-start | bytes 393224 | tf_op jit(solution)/shard_map/ppermute | solution.py:350
  16.2 1.5 %collective-permute-start.2 = (f32[2,128,128]{2,1,0:T(8,128)S(1)}, f32[2,128,128]{2,1,0:T(8,128)S(1)}, u32[]{:S(2)}, u32[]{:S(2)}) collective-permute-start(f32[2,128,128]{2,1,0:T(8,128)S(1)} %get-tuple-element.35), channel_id=1, source_target_pairs={{0,16},{1,17},{2,18},{3,19},{4,20},{5,21},{6,22},{7,23},{8,24},{9,... | collective-permute-start | bytes 393224 | tf_op jit(solution)/shard_map/ppermute | solution.py:350
  17.7 0.1 collective-permute-start.3
  17.8 0.7 collective-permute-start.4
  18.4 1.6 %collective-permute-done.1 = f32[2,128,128]{2,1,0:T(8,128)S(1)} collective-permute-done((f32[2,128,128]{2,1,0:T(8,128)S(1)}, f32[2,128,128]{2,1,0:T(8,128)S(1)}, u32[]{:S(2)}, u32[]{:S(2)}) %collective-permute-start.1) | collective-permute-done | bytes 131104 | tf_op jit(solution)/shard_map/ppermute | solution.py:350
  20.0 2.6 %collective-permute-done.2 = f32[2,128,128]{2,1,0:T(8,128)S(1)} collective-permute-done((f32[2,128,128]{2,1,0:T(8,128)S(1)}, f32[2,128,128]{2,1,0:T(8,128)S(1)}, u32[]{:S(2)}, u32[]{:S(2)}) %collective-permute-start.2) | collective-permute-done | bytes 131104 | tf_op jit(solution)/shard_map/ppermute | solution.py:350
  22.6 1.5 %collective-permute-done.3 = f32[2,128,128]{2,1,0:T(8,128)S(1)} collective-permute-done((f32[2,128,128]{2,1,0:T(8,128)S(1)}, f32[2,128,128]{2,1,0:T(8,128)S(1)}, u32[]{:S(2)}, u32[]{:S(2)}) %collective-permute-start.3) | collective-permute-done | bytes 131104 | tf_op jit(solution)/shard_map/ppermute | solution.py:350
  24.1 0.0 collective-permute-done.4.refs_3_
  24.1 7.9 %collective-permute-start.10 = (f32[2,128,128]{2,1,0:T(8,128)S(1)}, f32[2,128,128]{2,1,0:T(8,128)S(1)}, u32[]{:S(2)}, u32[]{:S(2)}) collective-permute-start(f32[2,128,128]{2,1,0:T(8,128)S(1)} %add_add_fusion.refs_0_), channel_id=1, source_target_pairs={{0,3},{1,2},{2,1},{3,0},{4,7},{5,6},{6,5},{7,4},{8,11},{9,10},{10,... | collective-permute-start | bytes 393224 | tf_op jit(solution)/shard_map/ppermute | solution.py:350
  32.0 1.2 %collective-permute-start.7 = (bf16[2,272,128]{2,1,0:T(8,128)(2,1)S(1)}, bf16[2,272,128]{2,1,0:T(8,128)(2,1)S(1)}, u32[]{:S(2)}, u32[]{:S(2)}) collective-permute-start(bf16[2,272,128]{2,1,0:T(8,128)(2,1)S(1)} %collective-permute-done.4.refs_3_), channel_id=1, source_target_pairs={{0,24},{1,25},{2,26},{3,27},{4,28},{5,29},{6,30},{7,31},{8,16},{9,... | collective-permute-start | bytes 417800 | tf_op jit(solution)/shard_map/ppermute | solution.py:350
  33.2 0.5 collective-permute-start.6
  33.7 1.8 %collective-permute-start.5 = (bf16[2,272,128]{2,1,0:T(8,128)(2,1)S(1)}, bf16[2,272,128]{2,1,0:T(8,128)(2,1)S(1)}, u32[]{:S(2)}, u32[]{:S(2)}) collective-permute-start(bf16[2,272,128]{2,1,0:T(8,128)(2,1)S(1)} %collective-permute-done.4.refs_3_), channel_id=1, source_target_pairs={{0,8},{1,9},{2,10},{3,11},{4,12},{5,13},{6,14},{7,15},{8,0},{9,1},... | collective-permute-start | bytes 417800 | tf_op jit(solution)/shard_map/ppermute | solution.py:350
  35.5 0.2 collective-permute-start.9
  35.7 0.7 collective-permute-done.10.refs_3_
  36.4 4.8 %collective-permute-start.8 = (f32[2,128,128]{2,1,0:T(8,128)S(1)}, f32[2,128,128]{2,1,0:T(8,128)S(1)}, u32[]{:S(2)}, u32[]{:S(2)}) collective-permute-start(f32[2,128,128]{2,1,0:T(8,128)S(1)} %add_add_fusion.refs_0_), channel_id=1, source_target_pairs={{0,1},{1,0},{2,3},{3,2},{4,5},{5,4},{6,7},{7,6},{8,9},{9,8},{10,11... | collective-permute-start | bytes 393224 | tf_op jit(solution)/shard_map/ppermute | solution.py:350
  41.3 2.3 %collective-permute-done.9.refs_2_ = f32[2,128,128]{2,1,0:T(8,128)S(1)} collective-permute-done((f32[2,128,128]{2,1,0:T(8,128)S(1)}, f32[2,128,128]{2,1,0:T(8,128)S(1)}, u32[]{:S(2)}, u32[]{:S(2)}) %collective-permute-start.9) | collective-permute-done | bytes 131104 | tf_op jit(solution)/shard_map/ppermute | solution.py:350
  43.6 2.7 %collective-permute-done.8.refs_1_ = f32[2,128,128]{2,1,0:T(8,128)S(1)} collective-permute-done((f32[2,128,128]{2,1,0:T(8,128)S(1)}, f32[2,128,128]{2,1,0:T(8,128)S(1)}, u32[]{:S(2)}, u32[]{:S(2)}) %collective-permute-start.8) | collective-permute-done | bytes 131104 | tf_op jit(solution)/shard_map/ppermute | solution.py:350
  46.3 0.0 collective-permute-done.7.refs_9_
  46.3 0.0 collective-permute-done.6.refs_7_
  46.3 0.0 collective-permute-done.5.refs_5_
  46.4 3.9 %shard_map.66.refs_0_ = f32[2,128,128]{2,1,0:T(8,128)S(1)} custom-call(s32[1]{0:T(128)} %bitcast.ids_ref, f32[2,128,128]{2,1,0:T(8,128)S(1)} %add_add_fusion.refs_0_, f32[2,128,128]{2,1,0:T(8,128)S(1)} %collective-permute-done.8.refs_1_, f32[2,128,128]{2,1,0:T(8,128)S(1)} %collective-permute-done.9.refs_2_, f32[2,128,128]{2,1,0:T(8,128)S(1)} %collective-permute-done.10.refs_3_), custom_call_target="tpu_custom_call" | custom-call | flops 4000000000 | bytes 12000000 | tf_op jit(solution)/shard_map/pallas_call | solution.py:332
  50.2 0.7 collective-permute-start.16
  50.9 0.9 %collective-permute-start.14 = (f32[2,128,128]{2,1,0:T(8,128)S(1)}, f32[2,128,128]{2,1,0:T(8,128)S(1)}, u32[]{:S(2)}, u32[]{:S(2)}) collective-permute-start(f32[2,128,128]{2,1,0:T(8,128)S(1)} %shard_map.66.refs_0_), channel_id=1, source_target_pairs={{0,16},{1,17},{2,18},{3,19},{4,20},{5,21},{6,22},{7,23},{8,24},{9,... | collective-permute-start | bytes 393224 | tf_op jit(solution)/shard_map/ppermute | solution.py:350
  51.8 1.9 %collective-permute-start.12 = (f32[2,128,128]{2,1,0:T(8,128)S(1)}, f32[2,128,128]{2,1,0:T(8,128)S(1)}, u32[]{:S(2)}, u32[]{:S(2)}) collective-permute-start(f32[2,128,128]{2,1,0:T(8,128)S(1)} %shard_map.66.refs_0_), channel_id=1, source_target_pairs={{0,8},{1,9},{2,10},{3,11},{4,12},{5,13},{6,14},{7,15},{8,0},{9,1},... | collective-permute-start | bytes 393224 | tf_op jit(solution)/shard_map/ppermute | solution.py:350
  53.8 0.8 collective-permute-start.22
  54.6 1.5 %collective-permute-start.11 = (f32[2,128,128]{2,1,0:T(8,128)S(1)}, f32[2,128,128]{2,1,0:T(8,128)S(1)}, u32[]{:S(2)}, u32[]{:S(2)}) collective-permute-start(f32[2,128,128]{2,1,0:T(8,128)S(1)} %shard_map.66.refs_0_), channel_id=1, source_target_pairs={{0,4},{1,5},{2,6},{3,7},{4,0},{5,1},{6,2},{7,3},{8,12},{9,13},{10,... | collective-permute-start | bytes 393224 | tf_op jit(solution)/shard_map/ppermute | solution.py:350
  56.1 1.4 %collective-permute-done.16.refs_6_ = f32[2,128,128]{2,1,0:T(8,128)S(1)} collective-permute-done((f32[2,128,128]{2,1,0:T(8,128)S(1)}, f32[2,128,128]{2,1,0:T(8,128)S(1)}, u32[]{:S(2)}, u32[]{:S(2)}) %collective-permute-start.16) | collective-permute-done | bytes 131104 | tf_op jit(solution)/shard_map/ppermute | solution.py:350
  57.5 0.0 collective-permute-start.17
  57.5 0.8 collective-permute-done.14.refs_4_
  58.3 0.0 collective-permute-start.15
  58.3 1.2 %collective-permute-done.12.refs_2_ = f32[2,128,128]{2,1,0:T(8,128)S(1)} collective-permute-done((f32[2,128,128]{2,1,0:T(8,128)S(1)}, f32[2,128,128]{2,1,0:T(8,128)S(1)}, u32[]{:S(2)}, u32[]{:S(2)}) %collective-permute-start.12) | collective-permute-done | bytes 131104 | tf_op jit(solution)/shard_map/ppermute | solution.py:350
  59.5 0.0 collective-permute-start.13
  59.5 0.1 pad_add_fusion.key_ref
  59.5 0.0 collective-permute-done.22.refs_11_
  59.6 8.7 %collective-permute-start.25 = (bf16[2,272,128]{2,1,0:T(8,128)(2,1)S(1)}, bf16[2,272,128]{2,1,0:T(8,128)(2,1)S(1)}, u32[]{:S(2)}, u32[]{:S(2)}) collective-permute-start(bf16[2,272,128]{2,1,0:T(8,128)(2,1)S(1)} %collective-permute-done.22.refs_11_), channel_id=1, source_target_pairs={{0,3},{1,2},{2,1},{3,0},{4,7},{5,6},{6,5},{7,4},{8,11},{9,10},{10,... | collective-permute-start | bytes 417800 | tf_op jit(solution)/shard_map/ppermute | solution.py:350
  68.2 0.0 collective-permute-done.11.refs_1_
  68.2 0.0 collective-permute-start.24
  68.2 0.0 collective-permute-done.17.refs_7_
  68.2 0.6 collective-permute-start.23
  68.8 0.0 collective-permute-done.15.refs_5_
  68.8 0.0 collective-permute-done.13.refs_3_
  68.8 12.2 %shard_map.67 = (f32[7,128,128]{2,1,0:T(8,128)S(1)}, f32[11,128,128]{2,1,0:T(8,128)S(1)}, f32[1,128,128]{2,1,0:T(8,128)S(1)}) custom-call(s32[3]{0:T(128)S(1)} %pad_add_fusion.key_ref, f32[2,128,128]{2,1,0:T(8,128)S(1)} %shard_map.66.refs_0_, f32[2,128,128]{2,1,0:T(8,128)S(1)} %collective-permute-done.11.refs_1_, ...), custom_call_target="tpu_custom_call" | custom-call | flops 12000000000 | bytes 36000000 | tf_op jit(solution)/shard_map/pallas_call | solution.py:332
  81.0 0.1 collective-permute-start.18
  81.1 0.5 collective-permute-start.19
  81.6 0.0 collective-permute-done.25.refs_14_
  81.6 0.1 collective-permute-start.20
  81.7 0.0 collective-permute-done.24.refs_13_
  81.7 0.4 collective-permute-start.21
  82.1 0.0 collective-permute-done.23.refs_12_
  82.1 0.3 collective-permute-done.18.refs_4_
  82.5 0.2 collective-permute-done.19.refs_6_
  82.7 0.3 collective-permute-done.20.refs_8_
  83.0 0.2 collective-permute-done.21.refs_10_
  83.2 0.0 copy-done
  83.2 8.2 %shard_map.68 = f32[256,512]{1,0:T(8,128)} custom-call(s32[3]{0:T(128)S(1)} %pad_add_fusion.key_ref, f32[7,128,128]{2,1,0:T(8,128)S(1)} %get-tuple-element.44.refs_0_, f32[11,128,128]{2,1,0:T(8,128)S(1)} %get-tuple-element.45.refs_1_, f32[1,128,128]{2,1,0:T(8,128)S(1)} %get-tuple-element.46.refs_2_, bf16[2,272,128]{2,1,0:T(8,128)(2,1)S(1)} %collective-permute-done.4.refs_3_, ...), custom_call_target="tpu_custom_call" | custom-call | flops 1000000000 | bytes 3000000 | tf_op jit(solution)/shard_map/pallas_call | solution.py:332
  (5 shorter events, 0.0 us)
Async XLA Ops:
  0.7 0.7 copy-start.3
  0.7 0.7 copy-start.4
  1.3 1.0 %copy-start.1 = (bf16[2,256,384]{2,1,0:T(8,128)(2,1)S(1)}, bf16[2,256,384]{2,1,0:T(8,128)(2,1)}, u32[]{:S(2)}) copy-start(bf16[2,256,384]{2,1,0:T(8,128)(2,1)} %refs_3_.1) | copy-start | bytes 1179652
  2.3 0.9 copy-start.2
  11.1 2.1 %collective-permute-start = (f32[4,2,128,128]{3,2,1,0:T(8,128)S(1)}, f32[4,2,128,128]{3,2,1,0:T(8,128)S(1)}, u32[]{:S(2)}, u32[]{:S(2)}) collective-permute-start(f32[4,2,128,128]{3,2,1,0:T(8,128)S(1)} %get-tuple-element.32), channel_id=1, source_target_pairs={{0,4},{1,5},{2,6},{3,7},{4,0},{5,1},{6,2},{7,3},{8,12},{9,13},{10,... | collective-permute-start | bytes 1572872 | tf_op jit(solution)/shard_map/ppermute | solution.py:350
  13.3 6.8 %collective-permute-start.1 = (f32[2,128,128]{2,1,0:T(8,128)S(1)}, f32[2,128,128]{2,1,0:T(8,128)S(1)}, u32[]{:S(2)}, u32[]{:S(2)}) collective-permute-start(f32[2,128,128]{2,1,0:T(8,128)S(1)} %get-tuple-element.34), channel_id=1, source_target_pairs={{0,8},{1,9},{2,10},{3,11},{4,12},{5,13},{6,14},{7,15},{8,0},{9,1},... | collective-permute-start | bytes 393224 | tf_op jit(solution)/shard_map/ppermute | solution.py:350
  16.2 6.4 %collective-permute-start.2 = (f32[2,128,128]{2,1,0:T(8,128)S(1)}, f32[2,128,128]{2,1,0:T(8,128)S(1)}, u32[]{:S(2)}, u32[]{:S(2)}) collective-permute-start(f32[2,128,128]{2,1,0:T(8,128)S(1)} %get-tuple-element.35), channel_id=1, source_target_pairs={{0,16},{1,17},{2,18},{3,19},{4,20},{5,21},{6,22},{7,23},{8,24},{9,... | collective-permute-start | bytes 393224 | tf_op jit(solution)/shard_map/ppermute | solution.py:350
  17.7 6.4 %collective-permute-start.3 = (f32[2,128,128]{2,1,0:T(8,128)S(1)}, f32[2,128,128]{2,1,0:T(8,128)S(1)}, u32[]{:S(2)}, u32[]{:S(2)}) collective-permute-start(f32[2,128,128]{2,1,0:T(8,128)S(1)} %get-tuple-element.36), channel_id=1, source_target_pairs={{0,24},{1,25},{2,26},{3,27},{4,28},{5,29},{6,30},{7,31},{8,16},{9,... | collective-permute-start | bytes 393224 | tf_op jit(solution)/shard_map/ppermute | solution.py:350
  17.8 6.4 %collective-permute-start.4 = (bf16[2,272,128]{2,1,0:T(8,128)(2,1)S(1)}, bf16[2,272,128]{2,1,0:T(8,128)(2,1)S(1)}, u32[]{:S(2)}, u32[]{:S(2)}) collective-permute-start(bf16[2,272,128]{2,1,0:T(8,128)(2,1)S(1)} %get-tuple-element.55), channel_id=1, source_target_pairs={{0,0},{4,1},{8,2},{12,3},{1,4},{5,5},{9,6},{13,7},{2,8},{6,9},{10,... | collective-permute-start | bytes 417800 | tf_op jit(solution)/shard_map/ppermute | solution.py:393
  24.1 12.3 %collective-permute-start.10 = (f32[2,128,128]{2,1,0:T(8,128)S(1)}, f32[2,128,128]{2,1,0:T(8,128)S(1)}, u32[]{:S(2)}, u32[]{:S(2)}) collective-permute-start(f32[2,128,128]{2,1,0:T(8,128)S(1)} %add_add_fusion.refs_0_), channel_id=1, source_target_pairs={{0,3},{1,2},{2,1},{3,0},{4,7},{5,6},{6,5},{7,4},{8,11},{9,10},{10,... | collective-permute-start | bytes 393224 | tf_op jit(solution)/shard_map/ppermute | solution.py:350
  32.0 14.3 %collective-permute-start.7 = (bf16[2,272,128]{2,1,0:T(8,128)(2,1)S(1)}, bf16[2,272,128]{2,1,0:T(8,128)(2,1)S(1)}, u32[]{:S(2)}, u32[]{:S(2)}) collective-permute-start(bf16[2,272,128]{2,1,0:T(8,128)(2,1)S(1)} %collective-permute-done.4.refs_3_), channel_id=1, source_target_pairs={{0,24},{1,25},{2,26},{3,27},{4,28},{5,29},{6,30},{7,31},{8,16},{9,... | collective-permute-start | bytes 417800 | tf_op jit(solution)/shard_map/ppermute | solution.py:350
  33.2 13.2 %collective-permute-start.6 = (bf16[2,272,128]{2,1,0:T(8,128)(2,1)S(1)}, bf16[2,272,128]{2,1,0:T(8,128)(2,1)S(1)}, u32[]{:S(2)}, u32[]{:S(2)}) collective-permute-start(bf16[2,272,128]{2,1,0:T(8,128)(2,1)S(1)} %collective-permute-done.4.refs_3_), channel_id=1, source_target_pairs={{0,16},{1,17},{2,18},{3,19},{4,20},{5,21},{6,22},{7,23},{8,24},{9,... | collective-permute-start | bytes 417800 | tf_op jit(solution)/shard_map/ppermute | solution.py:350
  33.7 12.6 %collective-permute-start.5 = (bf16[2,272,128]{2,1,0:T(8,128)(2,1)S(1)}, bf16[2,272,128]{2,1,0:T(8,128)(2,1)S(1)}, u32[]{:S(2)}, u32[]{:S(2)}) collective-permute-start(bf16[2,272,128]{2,1,0:T(8,128)(2,1)S(1)} %collective-permute-done.4.refs_3_), channel_id=1, source_target_pairs={{0,8},{1,9},{2,10},{3,11},{4,12},{5,13},{6,14},{7,15},{8,0},{9,1},... | collective-permute-start | bytes 417800 | tf_op jit(solution)/shard_map/ppermute | solution.py:350
  35.5 8.1 %collective-permute-start.9 = (f32[2,128,128]{2,1,0:T(8,128)S(1)}, f32[2,128,128]{2,1,0:T(8,128)S(1)}, u32[]{:S(2)}, u32[]{:S(2)}) collective-permute-start(f32[2,128,128]{2,1,0:T(8,128)S(1)} %add_add_fusion.refs_0_), channel_id=1, source_target_pairs={{0,2},{1,3},{2,0},{3,1},{4,6},{5,7},{6,4},{7,5},{8,10},{9,11},{10,... | collective-permute-start | bytes 393224 | tf_op jit(solution)/shard_map/ppermute | solution.py:350
  36.4 9.9 %collective-permute-start.8 = (f32[2,128,128]{2,1,0:T(8,128)S(1)}, f32[2,128,128]{2,1,0:T(8,128)S(1)}, u32[]{:S(2)}, u32[]{:S(2)}) collective-permute-start(f32[2,128,128]{2,1,0:T(8,128)S(1)} %add_add_fusion.refs_0_), channel_id=1, source_target_pairs={{0,1},{1,0},{2,3},{3,2},{4,5},{5,4},{6,7},{7,6},{8,9},{9,8},{10,11... | collective-permute-start | bytes 393224 | tf_op jit(solution)/shard_map/ppermute | solution.py:350
  50.2 7.3 %collective-permute-start.16 = (f32[2,128,128]{2,1,0:T(8,128)S(1)}, f32[2,128,128]{2,1,0:T(8,128)S(1)}, u32[]{:S(2)}, u32[]{:S(2)}) collective-permute-start(f32[2,128,128]{2,1,0:T(8,128)S(1)} %shard_map.66.refs_0_), channel_id=1, source_target_pairs={{0,24},{1,25},{2,26},{3,27},{4,28},{5,29},{6,30},{7,31},{8,16},{9,... | collective-permute-start | bytes 393224 | tf_op jit(solution)/shard_map/ppermute | solution.py:350
  50.9 7.4 %collective-permute-start.14 = (f32[2,128,128]{2,1,0:T(8,128)S(1)}, f32[2,128,128]{2,1,0:T(8,128)S(1)}, u32[]{:S(2)}, u32[]{:S(2)}) collective-permute-start(f32[2,128,128]{2,1,0:T(8,128)S(1)} %shard_map.66.refs_0_), channel_id=1, source_target_pairs={{0,16},{1,17},{2,18},{3,19},{4,20},{5,21},{6,22},{7,23},{8,24},{9,... | collective-permute-start | bytes 393224 | tf_op jit(solution)/shard_map/ppermute | solution.py:350
  51.8 7.6 %collective-permute-start.12 = (f32[2,128,128]{2,1,0:T(8,128)S(1)}, f32[2,128,128]{2,1,0:T(8,128)S(1)}, u32[]{:S(2)}, u32[]{:S(2)}) collective-permute-start(f32[2,128,128]{2,1,0:T(8,128)S(1)} %shard_map.66.refs_0_), channel_id=1, source_target_pairs={{0,8},{1,9},{2,10},{3,11},{4,12},{5,13},{6,14},{7,15},{8,0},{9,1},... | collective-permute-start | bytes 393224 | tf_op jit(solution)/shard_map/ppermute | solution.py:350
  53.8 5.8 %collective-permute-start.22 = (bf16[2,272,128]{2,1,0:T(8,128)(2,1)S(1)}, bf16[2,272,128]{2,1,0:T(8,128)(2,1)S(1)}, u32[]{:S(2)}, u32[]{:S(2)}) collective-permute-start(bf16[2,272,128]{2,1,0:T(8,128)(2,1)S(1)} %get-tuple-element.55), channel_id=1, source_target_pairs={{0,0},{1,1},{16,2},{17,3},{18,4},{19,5},{2,6},{3,7},{4,8},{5,9},{2... | collective-permute-start | bytes 417800 | tf_op jit(solution)/shard_map/ppermute | solution.py:409
  54.6 13.6 %collective-permute-start.11 = (f32[2,128,128]{2,1,0:T(8,128)S(1)}, f32[2,128,128]{2,1,0:T(8,128)S(1)}, u32[]{:S(2)}, u32[]{:S(2)}) collective-permute-start(f32[2,128,128]{2,1,0:T(8,128)S(1)} %shard_map.66.refs_0_), channel_id=1, source_target_pairs={{0,4},{1,5},{2,6},{3,7},{4,0},{5,1},{6,2},{7,3},{8,12},{9,13},{10,... | collective-permute-start | bytes 393224 | tf_op jit(solution)/shard_map/ppermute | solution.py:350
  57.5 10.7 %collective-permute-start.17 = (f32[2,128,128]{2,1,0:T(8,128)S(1)}, f32[2,128,128]{2,1,0:T(8,128)S(1)}, u32[]{:S(2)}, u32[]{:S(2)}) collective-permute-start(f32[2,128,128]{2,1,0:T(8,128)S(1)} %collective-permute-done.16.refs_6_), channel_id=1, source_target_pairs={{0,4},{1,5},{2,6},{3,7},{4,0},{5,1},{6,2},{7,3},{8,12},{9,13},{10,... | collective-permute-start | bytes 393224 | tf_op jit(solution)/shard_map/ppermute | solution.py:350
  58.3 10.5 %collective-permute-start.15 = (f32[2,128,128]{2,1,0:T(8,128)S(1)}, f32[2,128,128]{2,1,0:T(8,128)S(1)}, u32[]{:S(2)}, u32[]{:S(2)}) collective-permute-start(f32[2,128,128]{2,1,0:T(8,128)S(1)} %collective-permute-done.14.refs_4_), channel_id=1, source_target_pairs={{0,4},{1,5},{2,6},{3,7},{4,0},{5,1},{6,2},{7,3},{8,12},{9,13},{10,... | collective-permute-start | bytes 393224 | tf_op jit(solution)/shard_map/ppermute | solution.py:350
  59.5 9.4 %collective-permute-start.13 = (f32[2,128,128]{2,1,0:T(8,128)S(1)}, f32[2,128,128]{2,1,0:T(8,128)S(1)}, u32[]{:S(2)}, u32[]{:S(2)}) collective-permute-start(f32[2,128,128]{2,1,0:T(8,128)S(1)} %collective-permute-done.12.refs_2_), channel_id=1, source_target_pairs={{0,4},{1,5},{2,6},{3,7},{4,0},{5,1},{6,2},{7,3},{8,12},{9,13},{10,... | collective-permute-start | bytes 393224 | tf_op jit(solution)/shard_map/ppermute | solution.py:350
  59.5 23.6 %copy-start = (f32[256,512]{1,0:T(8,128)S(1)}, f32[256,512]{1,0:T(8,128)}, u32[]{:S(2)}) copy-start(f32[256,512]{1,0:T(8,128)} %refs_15_.1) | copy-start | bytes 1572868
  59.6 22.1 %collective-permute-start.25 = (bf16[2,272,128]{2,1,0:T(8,128)(2,1)S(1)}, bf16[2,272,128]{2,1,0:T(8,128)(2,1)S(1)}, u32[]{:S(2)}, u32[]{:S(2)}) collective-permute-start(bf16[2,272,128]{2,1,0:T(8,128)(2,1)S(1)} %collective-permute-done.22.refs_11_), channel_id=1, source_target_pairs={{0,3},{1,2},{2,1},{3,0},{4,7},{5,6},{6,5},{7,4},{8,11},{9,10},{10,... | collective-permute-start | bytes 417800 | tf_op jit(solution)/shard_map/ppermute | solution.py:350
  68.2 13.5 %collective-permute-start.24 = (bf16[2,272,128]{2,1,0:T(8,128)(2,1)S(1)}, bf16[2,272,128]{2,1,0:T(8,128)(2,1)S(1)}, u32[]{:S(2)}, u32[]{:S(2)}) collective-permute-start(bf16[2,272,128]{2,1,0:T(8,128)(2,1)S(1)} %collective-permute-done.22.refs_11_), channel_id=1, source_target_pairs={{0,2},{1,3},{2,0},{3,1},{4,6},{5,7},{6,4},{7,5},{8,10},{9,11},{10,... | collective-permute-start | bytes 417800 | tf_op jit(solution)/shard_map/ppermute | solution.py:350
  68.2 13.9 %collective-permute-start.23 = (bf16[2,272,128]{2,1,0:T(8,128)(2,1)S(1)}, bf16[2,272,128]{2,1,0:T(8,128)(2,1)S(1)}, u32[]{:S(2)}, u32[]{:S(2)}) collective-permute-start(bf16[2,272,128]{2,1,0:T(8,128)(2,1)S(1)} %collective-permute-done.22.refs_11_), channel_id=1, source_target_pairs={{0,1},{1,0},{2,3},{3,2},{4,5},{5,4},{6,7},{7,6},{8,9},{9,8},{10,11... | collective-permute-start | bytes 417800 | tf_op jit(solution)/shard_map/ppermute | solution.py:350
  81.0 1.4 %collective-permute-start.18 = (bf16[2,272,128]{2,1,0:T(8,128)(2,1)S(1)}, bf16[2,272,128]{2,1,0:T(8,128)(2,1)S(1)}, u32[]{:S(2)}, u32[]{:S(2)}) collective-permute-start(bf16[2,272,128]{2,1,0:T(8,128)(2,1)S(1)} %collective-permute-done.4.refs_3_), channel_id=1, source_target_pairs={{0,4},{1,5},{2,6},{3,7},{4,0},{5,1},{6,2},{7,3},{8,12},{9,13},{10,... | collective-permute-start | bytes 417800 | tf_op jit(solution)/shard_map/ppermute | solution.py:350
  81.1 1.5 %collective-permute-start.19 = (bf16[2,272,128]{2,1,0:T(8,128)(2,1)S(1)}, bf16[2,272,128]{2,1,0:T(8,128)(2,1)S(1)}, u32[]{:S(2)}, u32[]{:S(2)}) collective-permute-start(bf16[2,272,128]{2,1,0:T(8,128)(2,1)S(1)} %collective-permute-done.5.refs_5_), channel_id=1, source_target_pairs={{0,4},{1,5},{2,6},{3,7},{4,0},{5,1},{6,2},{7,3},{8,12},{9,13},{10,... | collective-permute-start | bytes 417800 | tf_op jit(solution)/shard_map/ppermute | solution.py:350
  81.6 1.4 %collective-permute-start.20 = (bf16[2,272,128]{2,1,0:T(8,128)(2,1)S(1)}, bf16[2,272,128]{2,1,0:T(8,128)(2,1)S(1)}, u32[]{:S(2)}, u32[]{:S(2)}) collective-permute-start(bf16[2,272,128]{2,1,0:T(8,128)(2,1)S(1)} %collective-permute-done.6.refs_7_), channel_id=1, source_target_pairs={{0,4},{1,5},{2,6},{3,7},{4,0},{5,1},{6,2},{7,3},{8,12},{9,13},{10,... | collective-permute-start | bytes 417800 | tf_op jit(solution)/shard_map/ppermute | solution.py:350
  81.7 1.5 %collective-permute-start.21 = (bf16[2,272,128]{2,1,0:T(8,128)(2,1)S(1)}, bf16[2,272,128]{2,1,0:T(8,128)(2,1)S(1)}, u32[]{:S(2)}, u32[]{:S(2)}) collective-permute-start(bf16[2,272,128]{2,1,0:T(8,128)(2,1)S(1)} %collective-permute-done.7.refs_9_), channel_id=1, source_target_pairs={{0,4},{1,5},{2,6},{3,7},{4,0},{5,1},{6,2},{7,3},{8,12},{9,13},{10,... | collective-permute-start | bytes 417800 | tf_op jit(solution)/shard_map/ppermute | solution.py:350
